TPU v7x, 128 devices: a whole 4x4x4 slice. The times are simulated.
128 devices in a mesh: front: 16 (over z_hi, y, core), row: 4 (over x), col: 2 (over z_lo).
Axes of the slice: x: 4, y: 4, z: 4 (z_hi: 2, z_lo: 2; z = z_hi * 2 + z_lo), core: 2. Of those that a mesh axis runs over, the one named last changes fastest.
Arguments:
- own_rows: float32 [16, 1536, 4096], P('front', 'row', 'col'), may hold values from -1.5 to 1.5
- child_rows: float32 [32768, 4096], P(('front', 'row'), 'col'), may hold values from -3 to 3
- child_dest: int32 [32768, 1], P(('front', 'row')), may hold values from 0 to 15; in each aligned block of 512 rows (0 to 511, 512 to 1023, ...) at most 64 rows name the same one
- child_stair: int32 [32768], P(('front', 'row')), may hold values from 0 to 7
Outputs:
- r_factor: float32 [16, 1024, 4096], P('front', 'row', 'col')
Inputs may be any that keep to these rules, and one draw needn't show every extreme that they name: `child_dest`: among the 512 rows of one device at most 64 name one parent, and in every draw some device has exactly 64 rows for some parent.
All inputs are finite; a program needn't handle non-finite values.
Results may differ from a plain program's by a relative error of at most 0.0003.
Values sent between devices are 32-bit elements; how exact they have to be, the bound alone decides.
No kernel may reach another device: no remote copies, remote signals or barrier semaphores. Data moves between devices by JAX's collectives and lax.ppermute only.
A program may use at most 128 MiB of HBM per device.

v0:
```python
import jax
import jax.numpy as jnp
from jax import lax
from jax.sharding import PartitionSpec as P

PANEL_COLUMNS = 512
PANEL_COUNT = 2
STAIR_BLK = 128


def broadcast(shard, axis, root):
    return lax.dynamic_index_in_dim(lax.all_gather(shard, axis), root, 0, keepdims=False)


def padded_to(lines, peers):
    spare = -len(lines) % peers
    return jnp.pad(lines, [(0, spare)] + [(0, 0)] * (lines.ndim - 1))


def sum_by_parts(shard, axis):
    lines = shard.reshape(-1, *shard.shape[1:][-1:])
    padded = padded_to(lines, lax.axis_size(axis))
    own = lax.psum_scatter(padded, axis, scatter_dimension=0, tiled=True)
    whole = lax.all_gather(own, axis, axis=0, tiled=True)
    return whole[: len(lines)].reshape(shard.shape)


def panel_factor(sums_block, panel_cols):
    lower_cholesky_factor = jnp.linalg.cholesky(sums_block[1])
    factor_rows = jax.scipy.linalg.solve_triangular(
        lower_cholesky_factor, sums_block[0], lower=True
    )
    basis = jax.scipy.linalg.solve_triangular(lower_cholesky_factor, panel_cols.T, lower=True).T
    return (factor_rows, basis)


def body(own_rows, child_rows, child_dest, child_stair):
    n_front = lax.axis_size("front")
    row_count = lax.axis_size("row")
    source_rows = child_rows.shape[0]
    half_cols = child_rows.shape[1]
    capacity = max(2, 2 * source_rows // n_front)
    col_index = lax.axis_index("col")
    global_cols = col_index * half_cols + lax.broadcasted_iota(
        jnp.int32, (source_rows, half_cols), 1
    )
    masked_rows = jnp.where(global_cols >= (child_stair * STAIR_BLK)[:, None], child_rows, 0.0)
    targets = child_dest[:, 0]
    onehot = (targets[:, None] == jnp.arange(n_front, dtype=jnp.int32)[None, :]).astype(jnp.int32)
    slot = jnp.sum((jnp.cumsum(onehot, axis=0) - onehot) * onehot, axis=1)
    eliminated_panel = PANEL_COUNT * PANEL_COLUMNS
    quarter_block = eliminated_panel // row_count
    row_start = lax.axis_index("row") * quarter_block
    position = targets * capacity + slot
    send_block = (
        jnp.zeros((n_front * capacity, half_cols), jnp.float32).at[position].set(masked_rows)
    )
    received = lax.all_to_all(send_block, "front", split_axis=0, concat_axis=0, tiled=True)
    front_block = jnp.concatenate([own_rows[0], received], 0)
    local_cols = col_index * half_cols + lax.broadcasted_iota(
        jnp.int32, (PANEL_COLUMNS, half_cols), 1
    )
    blocks = []
    for step in range(PANEL_COUNT):
        start_col = step * PANEL_COLUMNS
        panel_cols = broadcast(front_block[:, start_col : start_col + PANEL_COLUMNS], "col", 0)
        products = jnp.dot(
            panel_cols.T,
            front_block,
            precision=lax.Precision.HIGHEST,
            preferred_element_type=jnp.float32,
        )
        gramian_block = jnp.dot(
            panel_cols.T,
            panel_cols,
            precision=lax.Precision.HIGHEST,
            preferred_element_type=jnp.float32,
        )
        sums_block = (sum_by_parts(products, "row"), sum_by_parts(gramian_block, "row"))
        factor_rows, basis = panel_factor(sums_block, panel_cols)
        front_block = front_block - jnp.dot(
            basis, factor_rows, precision=lax.Precision.HIGHEST, preferred_element_type=jnp.float32
        )
        blocks.append(jnp.where(local_cols >= start_col, factor_rows, 0.0))
    factor_all = jnp.concatenate(blocks, 0)
    mine = lax.dynamic_slice_in_dim(factor_all, row_start, quarter_block, 0)
    return mine[None]


def solution(mesh):
    placed = (
        P("front", "row", "col"),
        P(("front", "row"), "col"),
        P(("front", "row"), None),
        P(("front", "row")),
    )
    return jax.shard_map(
        body, mesh=mesh, in_specs=placed, out_specs=P("front", "row", "col"), check_vma=False
    )
```

profile of v0, /device:TPU:0, one launch (start us, length us, event | category | flops | bytes accessed | tf_op | source)
XLA Modules:
  0.0 861.9 jit_solution(2290344186289988039)
XLA Ops:
  10.8 8.8 %scatter_custom_fusion = f32[1024,2048]{1,0:T(8,128)} fusion(s32[512]{0:T(512)S(1)} %bitcast.154, f32[512,2048]{1,0:T(8,128)} %param.8, f32[]{:T(128)} %constant.145.clone.1, s32[2048]{0:T(1024)S(1)} %iota_add_fusion, s32[512]{0:T(512)S(1)} %broadcast_multiply_fusion), kind=kCustom, calls=%fused_computation.14 | custom fusion | flops 2097152 | bytes 12594176 | tf_op jit(solution)/shard_map/scatter | solution.py:56
  19.6 104.9 %all_to_all.12 = f32[16,64,2048]{2,1,0:T(8,128)S(1)} all-to-all(f32[16,64,2048]{2,1,0:T(8,128)} %bitcast.147), channel_id=1, replica_groups=mesh['front'=16,'row'=4,'col'=2] {'front'}, dimensions={0} | all-to-all | bytes 16777216 | tf_op jit(solution)/shard_map/all_to_all | solution.py:58
  129.7 74.0 %all-gather.17.cloned.1.call-done = f32[2816,512]{1,0:T(8,128)} async-done(((f32[1408,512]{1,0:T(8,128)}), f32[2816,512]{1,0:T(8,128)}) %all-gather.17.cloned.1.call-update) | async-done | bytes 5767184 | tf_op jit(solution)/shard_map/all_gather | solution.py:12
  203.7 8.9 %fusion.31 = f32[512,512]{0,1:T(8,128)} fusion(f32[2816,512]{1,0:T(8,128)} %all-gather.17.cloned.1.call-done), kind=kOutput, calls=%fused_computation.43 | convolution fusion | flops 4429185024 | bytes 3932160 | tf_op jit(solution)/shard_map/dot_general | solution.py:73
  212.7 24.6 %reduce-scatter.5.cloned.1.call-done = f32[128,512]{0,1:T(8,128)} async-done(((f32[512,512]{0,1:T(8,128)}), f32[128,512]{0,1:T(8,128)}) %reduce-scatter.5.cloned.1.call-update) | async-done | bytes 262160 | tf_op jit(solution)/shard_map/reduce_scatter | solution.py:23
  237.6 24.4 %fusion = f32[512,2048]{1,0:T(8,128)} fusion(f32[384,2048]{1,0:T(8,128)S(1)} %bitcast.149, f32[1024,2048]{1,0:T(8,128)} %bitcast.143, f32[2816,512]{1,0:T(8,128)} %all-gather.17.cloned.1.call-done), kind=kOutput, calls=%fused_computation.8 | convolution fusion | flops 17719623680 | bytes 18612224 | tf_op jit(solution)/shard_map/dot_general | solution.py:67
  267.2 47.7 %reduce-scatter.7.cloned.1.call-done = f32[128,2048]{1,0:T(8,128)} async-done(((f32[512,2048]{1,0:T(8,128)}), f32[128,2048]{1,0:T(8,128)}) %reduce-scatter.7.cloned.1.call-update) | async-done | bytes 1048592 | tf_op jit(solution)/shard_map/reduce_scatter | solution.py:23
  318.2 11.7 %cholesky.286 = f32[128,128]{1,0:T(8,128)S(1)} custom-call(f32[128,128]{1,0:T(8,128)S(1)} %cholesky.426), custom_call_target="Cholesky" | custom-call | tf_op jit(solution)/shard_map/jit(cholesky)/cholesky | solution.py:29
  329.9 9.8 %custom-call.32 = f32[1,128,128]{1,2,0:T(8,128)S(1)} custom-call(f32[1,128,128]{2,1,0:T(8,128)S(1)} %get-tuple-element.70), custom_call_target="InvertDiagBlocksLowerTriangular" | custom-call | tf_op jit(solution)/shard_map/jit(cholesky)/cholesky | solution.py:29
  344.0 11.7 %cholesky.305 = f32[128,128]{1,0:T(8,128)S(1)} custom-call(f32[128,128]{1,0:T(8,128)S(1)} %cholesky.430), custom_call_target="Cholesky" | custom-call | tf_op jit(solution)/shard_map/jit(cholesky)/cholesky | solution.py:29
  356.4 10.0 %custom-call.33 = f32[1,128,128]{1,2,0:T(8,128)S(1)} custom-call(f32[1,128,128]{2,1,0:T(8,128)S(1)} %get-tuple-element.67), custom_call_target="InvertDiagBlocksLowerTriangular" | custom-call | tf_op jit(solution)/shard_map/jit(cholesky)/cholesky | solution.py:29
  368.7 11.7 %cholesky.326 = f32[128,128]{1,0:T(8,128)S(1)} custom-call(f32[128,128]{1,0:T(8,128)S(1)} %cholesky.435), custom_call_target="Cholesky" | custom-call | tf_op jit(solution)/shard_map/jit(cholesky)/cholesky | solution.py:29
  381.1 9.8 %custom-call.34 = f32[1,128,128]{1,2,0:T(8,128)S(1)} custom-call(f32[1,128,128]{2,1,0:T(8,128)S(1)} %get-tuple-element.64), custom_call_target="InvertDiagBlocksLowerTriangular" | custom-call | tf_op jit(solution)/shard_map/jit(cholesky)/cholesky | solution.py:29
  393.1 11.7 %cholesky.343 = f32[128,128]{1,0:T(8,128)S(1)} custom-call(f32[128,128]{1,0:T(8,128)S(1)} %convolution_subtract_fusion.12), custom_call_target="Cholesky" | custom-call | tf_op jit(solution)/shard_map/jit(cholesky)/cholesky | solution.py:29
  412.5 11.7 %while.5 = (s32[]{:T(128)}, f32[512,512]{1,0:T(8,128)}, s32[4,2]{0,1:T(2,128)S(1)}, f32[4,128,128]{2,1,0:T(8,128)S(1)}, s32[]{:T(128)}) while((s32[]{:T(128)}, f32[512,512]{1,0:T(8,128)}, s32[4,2]{0,1:T(2,128)S(1)}, f32[4,128,128]{2,1,0:T(8,128)S(1)}, s32[]{:T(128)}) %tuple.55), condition=%wide.while_cond, body=%wide.while_body.sunk | while | flops 2 | bytes 131181 | solution.py:30
  424.2 39.5 %custom-call.35 = f32[4,128,128]{1,2,0:T(8,128)S(1)} custom-call(f32[4,128,128]{2,1,0:T(8,128)S(1)} %get-tuple-element.29), custom_call_target="InvertDiagBlocksLowerTriangular" | custom-call | tf_op jit(solution)/shard_map/jit(_solve_triangular)/triangular_solve | solution.py:30
  472.1 4.9 convolution_subtract_fusion
  492.7 21.2 %fusion.1 = f32[1408,2048]{1,0:T(8,128)} fusion(f32[1024,2048]{1,0:T(8,128)S(1)} %bitcast.146, f32[384,2048]{1,0:T(8,128)S(1)} %bitcast.150, f32[128,1408]{1,0:T(8,128)S(1)} %copy-done.14, f32[128,1408]{1,0:T(8,128)S(1)} %copy-done.12, f32[128,1408]{1,0:T(8,128)S(1)} %copy-done.5, f32[128,1408]{1,0:T(8,128)S(1)} %copy-done.3, f32[128,2048]{1,0:T(8,128)S(1)} %fusion.104, ...), kind=kOutput, calls=%fused_computation.9 | convolution fusion | flops 17727815680 | bytes 30146560 | tf_op jit(solution)/shard_map/dot_general | solution.py:81
  518.1 76.5 %all-gather.19.cloned.1.call-done = f32[2816,512]{1,0:T(8,128)} async-done(((f32[1408,512]{1,0:T(8,128)}), f32[2816,512]{1,0:T(8,128)}) %all-gather.19.cloned.1.call-update) | async-done | bytes 5767184 | tf_op jit(solution)/shard_map/all_gather | solution.py:12
  594.6 9.0 %fusion.26 = f32[512,512]{0,1:T(8,128)} fusion(f32[2816,512]{1,0:T(8,128)} %all-gather.19.cloned.1.call-done), kind=kOutput, calls=%fused_computation.38 | convolution fusion | flops 4429185024 | bytes 3932160 | tf_op jit(solution)/shard_map/dot_general | solution.py:73
  603.6 24.9 %fusion.28 = f32[512,2048]{1,0:T(8,128)} fusion(f32[1408,2048]{1,0:T(8,128)} %fusion.1, f32[2816,512]{1,0:T(8,128)} %all-gather.19.cloned.1.call-done), kind=kOutput, calls=%fused_computation.40 | convolution fusion | flops 17716740096 | bytes 18612224 | tf_op jit(solution)/shard_map/dot_general | solution.py:67
  629.5 47.8 %reduce-scatter.11.cloned.1.call-done = f32[128,2048]{1,0:T(8,128)} async-done(((f32[512,2048]{1,0:T(8,128)}), f32[128,2048]{1,0:T(8,128)}) %reduce-scatter.11.cloned.1.call-update) | async-done | bytes 1048592 | tf_op jit(solution)/shard_map/reduce_scatter | solution.py:23
  681.0 23.6 %all-gather.13.cloned.1.call-done = f32[512,512]{0,1:T(8,128)} async-done(((f32[128,512]{0,1:T(8,128)}), f32[512,512]{0,1:T(8,128)}) %all-gather.13.cloned.1.call-update) | async-done | bytes 1048592 | tf_op jit(solution)/shard_map/all_gather | solution.py:24
  707.6 11.7 %cholesky.358 = f32[128,128]{1,0:T(8,128)S(1)} custom-call(f32[128,128]{1,0:T(8,128)S(1)} %cholesky.439), custom_call_target="Cholesky" | custom-call | tf_op jit(solution)/shard_map/jit(cholesky)/cholesky | solution.py:29
  719.5 9.8 %custom-call.36 = f32[1,128,128]{1,2,0:T(8,128)S(1)} custom-call(f32[1,128,128]{2,1,0:T(8,128)S(1)} %get-tuple-element.60), custom_call_target="InvertDiagBlocksLowerTriangular" | custom-call | tf_op jit(solution)/shard_map/jit(cholesky)/cholesky | solution.py:29
  730.0 11.7 %cholesky.377 = f32[128,128]{1,0:T(8,128)S(1)} custom-call(f32[128,128]{1,0:T(8,128)S(1)} %cholesky.443), custom_call_target="Cholesky" | custom-call | tf_op jit(solution)/shard_map/jit(cholesky)/cholesky | solution.py:29
  741.7 10.0 %custom-call.37 = f32[1,128,128]{1,2,0:T(8,128)S(1)} custom-call(f32[1,128,128]{2,1,0:T(8,128)S(1)} %get-tuple-element.57), custom_call_target="InvertDiagBlocksLowerTriangular" | custom-call | tf_op jit(solution)/shard_map/jit(cholesky)/cholesky | solution.py:29
  752.4 11.7 %cholesky.398 = f32[128,128]{1,0:T(8,128)S(1)} custom-call(f32[128,128]{1,0:T(8,128)S(1)} %cholesky.448), custom_call_target="Cholesky" | custom-call | tf_op jit(solution)/shard_map/jit(cholesky)/cholesky | solution.py:29
  764.1 9.8 %custom-call.38 = f32[1,128,128]{1,2,0:T(8,128)S(1)} custom-call(f32[1,128,128]{2,1,0:T(8,128)S(1)} %get-tuple-element.54), custom_call_target="InvertDiagBlocksLowerTriangular" | custom-call | tf_op jit(solution)/shard_map/jit(cholesky)/cholesky | solution.py:29
  774.5 11.9 %cholesky.415 = f32[128,128]{1,0:T(8,128)S(1)} custom-call(f32[128,128]{1,0:T(8,128)S(1)} %convolution_subtract_fusion.11), custom_call_target="Cholesky" | custom-call | tf_op jit(solution)/shard_map/jit(cholesky)/cholesky | solution.py:29
  791.9 8.1 while.6
  800.0 39.3 %custom-call.39 = f32[4,128,128]{1,2,0:T(8,128)S(1)} custom-call(f32[4,128,128]{2,1,0:T(8,128)S(1)} %get-tuple-element.30), custom_call_target="InvertDiagBlocksLowerTriangular" | custom-call | tf_op jit(solution)/shard_map/jit(_solve_triangular)/triangular_solve | solution.py:30
  (164 shorter events, 108.8 us)
Async XLA Ops:
  6.5 197.2 %all-gather.17.cloned.1.call-start = ((), (), s32[]{:S(2)}) async-start(), calls=%async_computation.13 | async-start | bytes 8650752 | tf_op jit(solution)/shard_map/all_gather | solution.py:12
  19.6 108.1 %copy-start.9 = (f32[1,384,2048]{2,1,0:T(8,128)S(1)}, f32[1,384,2048]{2,1,0:T(8,128)}, u32[]{:S(2)}) copy-start(f32[1,384,2048]{2,1,0:T(8,128)} %param.7) | copy-start | bytes 9437188
  124.5 3.2 copy-start
  129.7 107.6 %reduce-scatter.5.cloned.1.call-start = ((), (), s32[]{:S(2)}) async-start(), calls=%async_computation.5 | async-start | bytes 1310720 | tf_op jit(solution)/shard_map/reduce_scatter | solution.py:23
  212.7 52.0 %all-gather.9.cloned.1.call-start = ((), (), s32[]{:S(2)}) async-start(), calls=%async_computation.6 | async-start | bytes 1310720 | tf_op jit(solution)/shard_map/all_gather | solution.py:24
  237.3 77.5 %reduce-scatter.7.cloned.1.call-start = ((), (), s32[]{:S(2)}) async-start(), calls=%async_computation.7 | async-start | bytes 5242880 | tf_op jit(solution)/shard_map/reduce_scatter | solution.py:23
  262.0 216.7 %all-gather.11.cloned.1.call-start = ((), (), s32[]{:S(2)}) async-start(), calls=%async_computation.8 | async-start | bytes 5242880 | tf_op jit(solution)/shard_map/all_gather | solution.py:24
  314.9 279.7 %all-gather.19.cloned.1.call-start = ((), (), s32[]{:S(2)}) async-start(), calls=%async_computation.14 | async-start | bytes 8650752 | tf_op jit(solution)/shard_map/all_gather | solution.py:12
  317.1 1.1 copy-start.13
  464.6 12.4 %copy-start.2 = (f32[128,1408]{1,0:T(8,128)}, f32[128,1408]{1,0:T(8,128)S(1)}, u32[]{:S(2)}) copy-start(f32[128,1408]{1,0:T(8,128)S(1)} %fusion.65) | copy-start | bytes 2162692
  467.7 9.3 %copy-start.4 = (f32[128,1408]{1,0:T(8,128)}, f32[128,1408]{1,0:T(8,128)S(1)}, u32[]{:S(2)}) copy-start(f32[128,1408]{1,0:T(8,128)S(1)} %fusion.99) | copy-start | bytes 2162692
  472.1 4.9 copy-start.11
  478.7 6.2 copy-start.8
  483.9 8.8 %slice-start = ((s8[8388608]{0:T(1024)(128)(4,1)}), s8[4194304]{0:T(1024)(128)(4,1)S(1)}, s32[]{:S(2)}) async-start(s8[8388608]{0:T(1024)(128)(4,1)} %bitcast.144), calls=%async_computation.15 | async-start | bytes 8388608
  484.9 7.7 copy-start.14
  487.3 5.4 slice-start.1
  488.4 4.3 copy-start.3
  488.4 4.3 copy-start.5
  488.4 4.3 copy-start.10
  488.4 4.3 copy-start.12
  492.7 21.2 %copy-start.6 = (f32[128,2048]{1,0:T(8,128)}, f32[128,2048]{1,0:T(8,128)S(1)}, u32[]{:S(2)}) copy-start(f32[128,2048]{1,0:T(8,128)S(1)} %fusion.104) | copy-start | bytes 3145732
  517.6 111.0 %reduce-scatter.9.cloned.1.call-start = ((), (), s32[]{:S(2)}) async-start(), calls=%async_computation.9 | async-start | bytes 1310720 | tf_op jit(solution)/shard_map/reduce_scatter | solution.py:23
  603.6 73.7 %reduce-scatter.11.cloned.1.call-start = ((), (), s32[]{:S(2)}) async-start(), calls=%async_computation.11 | async-start | bytes 5242880 | tf_op jit(solution)/shard_map/reduce_scatter | solution.py:23
  628.5 76.0 %all-gather.13.cloned.1.call-start = ((), (), s32[]{:S(2)}) async-start(), calls=%async_computation.10 | async-start | bytes 1310720 | tf_op jit(solution)/shard_map/all_gather | solution.py:24
  629.3 210.1 %all-gather.15.cloned.1.call-start = ((), (), s32[]{:S(2)}) async-start(), calls=%async_computation.12 | async-start | bytes 5242880 | tf_op jit(solution)/shard_map/all_gather | solution.py:24
  839.3 5.7 copy-start.7
  850.5 2.2 copy-start.1
Sparse Core Ops, SparseCore 0:
  129.8 73.9 all-gather.16
  212.8 24.4 reduce-scatter.4
  239.1 25.5 all-gather.8
  267.0 47.7 reduce-scatter.6
  316.4 48.0 all-gather.10
  517.7 76.7 all-gather.18
  603.7 24.4 reduce-scatter.8
  630.7 46.5 reduce-scatter.10
  679.0 25.5 all-gather.12
  706.1 49.2 all-gather.14
where the time goes:
time: 871 us; the launch traced here: 862 us
  waiting for transfers between devices  296 us (34%)
  other arithmetic  265 us (30%)
  matrix products  138 us (16%)
  blocking collectives  105 us (12%)
  local copies, waits for them, and re-layouts  36.9 us (4%)
  between operations  19.7 us (2%)
    another operation x29, other arithmetic, panel_factor(): lower_cholesky_factor = jnp.linalg.cholesky(sums_block[1])  160 us
    all_gather x2, waiting for transfers between devices, broadcast(): lax.all_gather(shard, axis)  151 us
    reduce_scatter x4, waiting for transfers between devices, sum_by_parts(): own = lax.psum_scatter(padded, axis, scatter_dimension=0, tiled=True)  120 us
    all_to_all x1, blocking collectives, body(): lax.all_to_all(send_block, 'front', split_axis=0, concat_axis=0, tiled=True)  105 us
    another operation x5, other arithmetic, panel_factor(): jax.scipy.linalg.solve_triangular(lower_cholesky_factor, sums_block[0], l...  81.3 us
    dot_general x2, matrix products, body(): jnp.dot(panel_cols.T, front_block, precision=lax.Precision.HIGHEST, prefe...  49.3 us
    another operation x14, matrix products, panel_factor(): jax.scipy.linalg.solve_triangular(lower_cholesky_factor, sums_block[0], l...  24.8 us
    all_gather x4, waiting for transfers between devices, sum_by_parts(): whole = lax.all_gather(own, axis, axis=0, tiled=True)  24.1 us
  transfers between devices with their start and end apart: 10, of which 7 were waited for; matrix products, arithmetic and copies ran while one was open for 40% of the time, Pallas kernels for 0%

commit v1 on v0

v1 whole, which is shorter than its diff:
```python
import jax
import jax.numpy as jnp
from jax import lax
from jax.experimental import pallas as pl
from jax.experimental.pallas import tpu as pltpu
from jax.sharding import PartitionSpec as P

ELIMINATED = 1024
STAIR_BLK = 128
BLK = 128
STEPS = ELIMINATED // BLK
LINES = 8


def lower_inverse(diag_block):
    lane = lax.broadcasted_iota(jnp.int32, (LINES, BLK), 1)
    sublane = lax.broadcasted_iota(jnp.int32, (LINES, BLK), 0)
    count = BLK // LINES
    strips = [diag_block[LINES * i : LINES * (i + 1), :] for i in range(count)]
    for b in range(count):
        first = LINES * b
        within = (lane >= first) & (lane < first + LINES)
        strip = strips[b]
        column = [
            jnp.broadcast_to(strip[:, first + t : first + t + 1], (LINES, BLK))
            for t in range(LINES)
        ]
        entry = [
            [jnp.broadcast_to(column[t][i : i + 1, :], (LINES, BLK)) for t in range(i + 1)]
            for i in range(LINES)
        ]
        scale = []
        for t in range(LINES):
            scale.append(lax.rsqrt(entry[t][t]))
            for i in range(t + 1, LINES):
                entry[i][t] = entry[i][t] * scale[t]
            for u in range(t + 1, LINES):
                for i in range(u, LINES):
                    entry[i][u] = entry[i][u] - entry[i][t] * entry[u][t]
        solved = []
        augmented = jnp.where(within, jnp.where(lane == sublane + first, 1.0, 0.0), strip)
        for t in range(LINES):
            line = jnp.broadcast_to(augmented[t : t + 1, :], (LINES, BLK))
            for s in range(t):
                line = line - entry[t][s] * solved[s]
            solved.append(line * scale[t])
        merged = solved[0]
        for t in range(1, LINES):
            merged = jnp.where(sublane == t, solved[t], merged)
        strips[b] = merged
        for i in range(b + 1, count):
            below = strips[i]
            rest = jnp.where(within, 0.0, below)
            factors = []
            for t in range(LINES):
                value = jnp.broadcast_to(below[:, first + t : first + t + 1], (LINES, BLK))
                for s in range(t):
                    value = value - entry[t][s] * factors[s]
                value = value * scale[t]
                factors.append(value)
                rest = rest - value * solved[t]
            strips[i] = rest
    row = lax.broadcasted_iota(jnp.int32, (BLK, BLK), 0)
    col = lax.broadcasted_iota(jnp.int32, (BLK, BLK), 1)
    return jnp.where(row >= col, jnp.concatenate(strips, axis=0), 0.0)


def exact_dot(a, b, dims):
    return lax.dot_general(
        a, b, (dims, ((), ())), precision=lax.Precision.HIGHEST, preferred_element_type=jnp.float32
    )


def factor_kernel(gram_ref, work_ref, diag_ref):
    work_ref[...] = gram_ref[...]
    row = lax.broadcasted_iota(jnp.int32, (BLK, BLK), 0)
    col = lax.broadcasted_iota(jnp.int32, (BLK, BLK), 1)

    def step(k, _):
        here = pl.ds(pl.multiple_of(k * BLK, BLK), BLK)
        block = work_ref[here, here]
        inverse = lower_inverse(block)
        diag_ref[here, :] = jnp.where(row <= col, exact_dot(inverse, block, ((1,), (0,))), 0.0)
        work_ref[here, :] = exact_dot(inverse, work_ref[here, :], ((1,), (0,)))
        work_ref[here, here] = inverse

        def update(i, _):
            there = pl.ds(pl.multiple_of(i * BLK, BLK), BLK)
            work_ref[there, here] = jnp.zeros((BLK, BLK), jnp.float32)
            work_ref[there, :] -= exact_dot(work_ref[here, there], work_ref[here, :], ((0,), (0,)))
            return 0

        lax.fori_loop(k + 1, STEPS, update, 0)
        return 0

    lax.fori_loop(0, STEPS, step, 0)


def factor(gram):
    return pl.pallas_call(
        factor_kernel,
        out_shape=(
            jax.ShapeDtypeStruct((ELIMINATED, ELIMINATED), jnp.float32),
            jax.ShapeDtypeStruct((ELIMINATED, BLK), jnp.float32),
        ),
        in_specs=[pl.BlockSpec(memory_space=pltpu.VMEM)],
        out_specs=(pl.BlockSpec(memory_space=pltpu.VMEM), pl.BlockSpec(memory_space=pltpu.VMEM)),
        compiler_params=pltpu.CompilerParams(vmem_limit_bytes=48 * 1024 * 1024),
        cost_estimate=pl.CostEstimate(flops=10**10, bytes_accessed=9 * 2**20, transcendentals=1024),
    )(gram)


def cross(a, b):
    return lax.dot_general(
        a,
        b,
        (((0,), (0,)), ((), ())),
        precision=lax.Precision.HIGH,
        preferred_element_type=jnp.float32,
    )


def body(own_rows, child_rows, child_dest, child_stair):
    n_front = lax.axis_size("front")
    row_count = lax.axis_size("row")
    source_rows, half_cols = child_rows.shape
    capacity = max(2, 2 * source_rows // n_front)
    col_index = lax.axis_index("col")
    row_index = lax.axis_index("row")
    quarter = ELIMINATED // row_count
    global_cols = col_index * half_cols + lax.broadcasted_iota(
        jnp.int32, (source_rows, half_cols), 1
    )
    masked_rows = jnp.where(global_cols >= (child_stair * STAIR_BLK)[:, None], child_rows, 0.0)
    targets = child_dest[:, 0]
    order = jnp.arange(source_rows, dtype=jnp.int32)
    earlier = (targets[:, None] == targets[None, :]) & (order[None, :] < order[:, None])
    slot = jnp.sum(earlier.astype(jnp.int32), axis=1)
    position = targets * capacity + slot
    send = jnp.zeros((n_front * capacity, half_cols), jnp.float32).at[position].set(masked_rows)

    own = own_rows[0]
    own_a, own_b = own[:, :ELIMINATED], own[:, ELIMINATED:]
    passed = lax.ppermute(own_a, "col", [(0, 1)])
    own_panel = jnp.where(col_index == 0, own_a, passed)

    doubled = jnp.broadcast_to(
        send[:, :ELIMINATED].reshape(n_front, 1, capacity, ELIMINATED),
        (n_front, 2, capacity, ELIMINATED),
    ).reshape(2 * n_front * capacity, ELIMINATED)
    arrived = lax.all_to_all(doubled, ("front", "col"), split_axis=0, concat_axis=0, tiled=True)
    arrived = arrived.reshape(n_front, 2, capacity, ELIMINATED)
    child_panel = arrived[:, 0].reshape(n_front * capacity, ELIMINATED)
    child_a = arrived[:, 1].reshape(n_front * capacity, ELIMINATED)
    child_b = lax.all_to_all(send[:, ELIMINATED:], "front", split_axis=0, concat_axis=0, tiled=True)

    gram = lax.psum(cross(own_panel, own_panel) + cross(child_panel, child_panel), "row")
    work, diag = factor(gram)
    block_row = lax.broadcasted_iota(jnp.int32, (ELIMINATED, ELIMINATED), 0) // BLK
    block_col = lax.broadcasted_iota(jnp.int32, (ELIMINATED, ELIMINATED), 1) // BLK
    inverse = jnp.where(block_row >= block_col, work, 0.0)
    leading = jnp.where(
        block_row < block_col, work, jnp.where(block_row == block_col, jnp.tile(diag, (1, STEPS)), 0.0)
    )
    leading = lax.dynamic_slice_in_dim(leading, row_index * quarter, quarter, 0)

    def finish(own_part, child_part):
        sums = lax.psum_scatter(
            cross(own_part, own_panel) + cross(child_part, child_panel),
            "row",
            scatter_dimension=0,
            tiled=True,
        )
        rows = exact_dot(inverse, sums, ((1,), (1,)))
        return lax.all_to_all(rows, "row", split_axis=0, concat_axis=1, tiled=True)

    first = jnp.where(col_index == 0, leading, finish(own_a, child_a))
    second = finish(own_b, child_b)
    return jnp.concatenate([first, second], 1)[None]


def solution(mesh):
    placed = (
        P("front", "row", "col"),
        P(("front", "row"), "col"),
        P(("front", "row"), None),
        P(("front", "row")),
    )
    return jax.shard_map(
        body, mesh=mesh, in_specs=placed, out_specs=P("front", "row", "col"), check_vma=False
    )
```

time: 871 us -> 465 us (0.53)
  other arithmetic: 265 us -> 19.3 us
  blocking collectives: 105 us -> 0 us
  matrix products: 138 us -> 59.7 us
  Pallas kernels: 0 us -> 60.9 us
  waiting for transfers between devices: 296 us -> 252 us
  starting transfers between devices: 1.56 us -> 30.5 us
  local copies, waits for them, and re-layouts: 36.9 us -> 23.4 us
    another operation x36 -> x0, other arithmetic: 242 us -> none  [the longest x29 160 us: panel_factor(): lower_cholesky_factor = jnp.linalg.cholesky(sums_block[1])]
    all_gather x6 -> x0, waiting for transfers between devices: 175 us -> none  [the longest x2 151 us: broadcast(): lax.all_gather(shard, axis)]
    all_to_all x0 -> x4, waiting for transfers between devices: none -> 122 us  [the longest x1 106 us: body(): lax.all_to_all(doubled, ('front', 'col'), split_axis=0, concat_axis=0, ti...]
    all_to_all x1 -> x0, blocking collectives: 105 us -> none  [body(): lax.all_to_all(send_block, 'front', split_axis=0, concat_axis=0, tiled=True)]
    reduce_scatter x4 -> x2, waiting for transfers between devices: 120 us -> 36 us  [finish(): lax.psum_scatter(cross(own_part, own_panel) + cross(child_part, child_pan...]
    psum x0 -> x1, waiting for transfers between devices: none -> 63 us  [body(): lax.psum(cross(own_panel, own_panel) + cross(child_panel, child_panel), '...]
    pallas_call x0 -> x1, Pallas kernels: none -> 60.9 us  [factor(): pl.pallas_call(factor_kernel, out_shape=(jax.ShapeDtypeStruct((ELIMINATED...]
    another operation x33 -> x0, matrix products: 49.4 us -> none  [the longest x14 24.8 us: panel_factor(): jax.scipy.linalg.solve_triangular(lower_cholesky_factor, sums_block[0], l...]
  transfers between devices with their start and end apart: 10 -> 8, of which waited for: 7 -> 6; matrix products, arithmetic and copies ran while one was open for 40% -> 16% of each run, Pallas kernels for 0% -> 13%
where the time goes in v1:
time: 465 us; the launch traced here: 460 us
  waiting for transfers between devices  252 us (54%)
  Pallas kernels  60.9 us (13%)
  matrix products  59.7 us (13%)
  starting transfers between devices  30.5 us (7%)
  local copies, waits for them, and re-layouts  23.4 us (5%)
  other arithmetic  19.3 us (4%)
  between operations  13.5 us (3%)
    all_to_all x1, waiting for transfers between devices, body(): lax.all_to_all(doubled, ('front', 'col'), split_axis=0, concat_axis=0, ti...  106 us
    psum x1, waiting for transfers between devices, body(): lax.psum(cross(own_panel, own_panel) + cross(child_panel, child_panel), '...  63 us
    pallas_call x1, Pallas kernels, factor(): pl.pallas_call(factor_kernel, out_shape=(jax.ShapeDtypeStruct((ELIMINATED...  60.9 us
    dot_general x6, matrix products, cross(): lax.dot_general(a, b, (((0,), (0,)), ((), ())), precision=lax.Precision.H...  45.6 us
    reduce_scatter x2, waiting for transfers between devices, finish(): lax.psum_scatter(cross(own_part, own_panel) + cross(child_part, child_pan...  36 us
    ppermute x1, waiting for transfers between devices, body(): passed = lax.ppermute(own_a, 'col', [(0, 1)])  31.6 us
    dot_general x2, matrix products, exact_dot(): lax.dot_general(a, b, (dims, ((), ())), precision=lax.Precision.HIGHEST,...  14.1 us
  transfers between devices with their start and end apart: 8, of which 6 were waited for; matrix products, arithmetic and copies ran while one was open for 16% of the time, Pallas kernels for 13%

profile of v1, /device:TPU:0, one launch (start us, length us, event | category | flops | bytes accessed | tf_op | source)
XLA Modules:
  0.0 459.6 jit_solution(12396896421773568209)
XLA Ops:
  6.5 1.0 convert_reduce_fusion
  8.9 8.8 %scatter_custom_fusion = f32[1024,2048]{1,0:T(8,128)} fusion(s32[512]{0:T(512)S(1)} %bitcast.66, f32[512,2048]{1,0:T(8,128)} %param.5, f32[]{:T(128)} %constant.48.clone.1, s32[2048]{0:T(1024)S(1)} %iota_add_fusion, s32[512]{0:T(512)S(1)} %broadcast_multiply_fusion), kind=kCustom, calls=%fused_computation.10 | custom fusion | flops 2097152 | bytes 12594176 | tf_op jit(solution)/shard_map/scatter | solution.py:140
  17.7 6.7 %fusion.26 = (f32[1024,1024]{1,0:T(8,128)S(1)}, f32[1024,1024]{1,0:T(8,128)}) fusion(f32[1024,2048]{1,0:T(8,128)} %scatter_custom_fusion), kind=kLoop, calls=%fused_computation.48 | loop fusion | bytes 16777216 | tf_op jit(solution)/shard_map/slice | solution.py:148
  24.4 4.3 broadcast_in_dim.29
  28.7 8.8 %all-to-all-start = ((f32[32,64,1024]{2,1,0:T(8,128)}), f32[32,64,1024]{2,1,0:T(8,128)}, u32[]{:S(2)}, u32[]{:S(2)}) async-start(f32[32,64,1024]{2,1,0:T(8,128)} %bitcast.49), calls=%async_computation | async-start | bytes 16777216 | tf_op jit(solution)/shard_map/all_to_all | solution.py:151
  37.6 1.2 slice.24
  38.8 4.8 %collective-permute-start = (f32[384,1024]{1,0:T(8,128)}, f32[384,1024]{1,0:T(8,128)}, u32[]{:S(2)}, u32[]{:S(2)}) collective-permute-start(f32[384,1024]{1,0:T(8,128)} %slice.24), channel_id=1, source_target_pairs={{0,1},{2,3},{4,5},{6,7},{8,9},{10,11},{12,13},{14,15},{16,17},{18,... | collective-permute-start | bytes 4718600 | tf_op jit(solution)/shard_map/ppermute | solution.py:144
  43.6 105.7 %all-to-all-done = f32[32,64,1024]{2,1,0:T(8,128)} async-done(((f32[32,64,1024]{2,1,0:T(8,128)}), f32[32,64,1024]{2,1,0:T(8,128)}, u32[]{:S(2)}, u32[]{:S(2)}) %all-to-all-start) | async-done | bytes 8388640 | tf_op jit(solution)/shard_map/all_to_all | solution.py:151
  149.3 8.8 %all-to-all-start.2 = ((f32[16,64,1024]{2,1,0:T(8,128)}), f32[16,64,1024]{2,1,0:T(8,128)}, u32[]{:S(2)}, u32[]{:S(2)}) async-start(f32[16,64,1024]{2,1,0:T(8,128)} %bitcast.56), calls=%async_computation.3 | async-start | bytes 8388608 | tf_op jit(solution)/shard_map/all_to_all | solution.py:155
  158.7 10.1 %fusion.2 = f32[1024,1024,1]{1,0,2:T(8,128)S(1)} fusion(f32[16,2,64,1024]{3,2,1,0:T(8,128)} %bitcast.6), kind=kOutput, calls=%fused_computation.5 | convolution fusion | flops 6442450944 | bytes 8388608 | tf_op jit(solution)/shard_map/dot_general | solution.py:114
  168.9 31.6 %collective-permute-done = f32[384,1024]{1,0:T(8,128)} collective-permute-done((f32[384,1024]{1,0:T(8,128)}, f32[384,1024]{1,0:T(8,128)}, u32[]{:S(2)}, u32[]{:S(2)}) %collective-permute-start) | collective-permute-done | bytes 1572896 | tf_op jit(solution)/shard_map/ppermute | solution.py:144
  200.5 5.4 %bitcast_add_fusion.2 = f32[1024,1024]{1,0:T(8,128)} fusion(f32[1024,1024,1]{1,0,2:T(8,128)S(1)} %fusion.2, f32[384,1024]{1,0:T(8,128)} %collective-permute-done, pred[]{:T(512)S(6)} %eq.22, f32[384,2048]{1,0:T(8,128)S(1)} %bitcast.51), kind=kOutput, calls=%fused_computation.9 | convolution fusion | flops 2417360896 | bytes 11534337 | tf_op jit(solution)/shard_map/dot_general | solution.py:114
  206.2 4.7 %slice.26 = f32[16,1,64,1024]{3,2,1,0:T(8,128)} slice(f32[16,2,64,1024]{3,2,1,0:T(8,128)} %bitcast.6), slice={[0:16], [0:1], [0:64], [0:1024]} | slice | bytes 8388608 | tf_op jit(solution)/shard_map/slice | solution.py:153
  210.9 8.7 %all-to-all-done.2 = f32[16,64,1024]{2,1,0:T(8,128)} async-done(((f32[16,64,1024]{2,1,0:T(8,128)}), f32[16,64,1024]{2,1,0:T(8,128)}, u32[]{:S(2)}, u32[]{:S(2)}) %all-to-all-start.2) | async-done | bytes 4194336 | tf_op jit(solution)/shard_map/all_to_all | solution.py:155
  219.6 9.8 %fusion.27 = f32[1024,1024]{0,1:T(8,128)S(1)} fusion(f32[1024,1024]{1,0:T(8,128)} %bitcast.16, f32[1024,1024]{1,0:T(8,128)} %bitcast.58), kind=kOutput, calls=%fused_computation.49 | convolution fusion | flops 6442450944 | bytes 12582912 | tf_op jit(solution)/shard_map/dot_general | solution.py:114
  229.5 5.1 %bitcast_add_fusion = f32[1024,1024]{0,1:T(8,128)} fusion(f32[1024,1024]{0,1:T(8,128)S(1)} %fusion.27, f32[384,2048]{1,0:T(8,128)S(1)} %bitcast.52, f32[384,1024]{1,0:T(8,128)} %collective-permute-done, pred[]{:T(512)S(6)} %eq.22), kind=kOutput, calls=%fused_computation.7 | convolution fusion | flops 2417360896 | bytes 13107201 | tf_op jit(solution)/shard_map/dot_general | solution.py:114
  234.9 9.9 %fusion = f32[1024,1024,1]{0,1,2:T(8,128)S(1)} fusion(f32[16,2,64,1024]{3,2,1,0:T(8,128)} %bitcast.6), kind=kOutput, calls=%fused_computation.3 | convolution fusion | flops 6442450944 | bytes 12582912 | tf_op jit(solution)/shard_map/dot_general | solution.py:114
  244.8 5.1 %bitcast_add_fusion.1 = f32[1024,1024]{0,1:T(8,128)} fusion(f32[1024,1024,1]{0,1,2:T(8,128)S(1)} %fusion, f32[384,1024]{1,0:T(8,128)} %collective-permute-done, pred[]{:T(512)S(6)} %eq.22, f32[384,2048]{1,0:T(8,128)S(1)} %bitcast.53), kind=kOutput, calls=%fused_computation.8 | convolution fusion | flops 2417360896 | bytes 13107201 | tf_op jit(solution)/shard_map/dot_general | solution.py:114
  250.0 63.0 %all-reduce.2.cloned.1.call-done.gram_ref = f32[1024,1024]{1,0:T(8,128)} async-done(((f32[1024,1024]{1,0:T(8,128)}), f32[1024,1024]{1,0:T(8,128)}) %all-reduce.2.cloned.1.call-update) | async-done | bytes 4194320 | tf_op jit(solution)/shard_map/psum | solution.py:157
  313.0 60.9 %shard_map.46 = (f32[1024,1024]{1,0:T(8,128)S(1)}, f32[1024,128]{1,0:T(8,128)S(1)}) custom-call(f32[1024,1024]{1,0:T(8,128)} %all-reduce.2.cloned.1.call-done.gram_ref), custom_call_target="tpu_custom_call" | custom-call | flops 10000000000 | bytes 9437184 | tf_op jit(solution)/shard_map/pallas_call | solution.py:100
  373.9 1.9 copy-done
  375.9 7.0 %fusion.12 = f32[1024,256]{1,0:T(8,128)} fusion(f32[256,1024]{0,1:T(8,128)} %reduce-scatter.5.cloned.1.call-done, f32[1024,1024]{1,0:T(8,128)} %copy-done, s32[1024]{0:T(1024)S(1)} %get-tuple-element.13, s32[1024]{0:T(1024)S(1)} %get-tuple-element.14, pred[1024]{0:T(1024)(128)(4,1)S(1)} %fusion.18), kind=kOutput, calls=%fused_computation.22 | convolution fusion | flops 3225419776 | bytes 6300672 | tf_op jit(solution)/shard_map/dot_general | solution.py:69
  382.9 3.5 all-to-all-start.3
  386.4 36.0 %reduce-scatter.3.cloned.1.call-done = f32[256,1024]{0,1:T(8,128)} async-done(((f32[1024,1024]{0,1:T(8,128)}), f32[256,1024]{0,1:T(8,128)}) %reduce-scatter.3.cloned.1.call-update) | async-done | bytes 1048592 | tf_op jit(solution)/shard_map/reduce_scatter | solution.py:168
  422.4 7.1 %fusion.13 = f32[1024,256]{1,0:T(8,128)} fusion(f32[256,1024]{0,1:T(8,128)} %reduce-scatter.3.cloned.1.call-done, f32[1024,1024]{1,0:T(8,128)} %copy-done, s32[1024]{0:T(1024)S(1)} %get-tuple-element.13, s32[1024]{0:T(1024)S(1)} %get-tuple-element.14, pred[1024]{0:T(1024)(128)(4,1)S(1)} %fusion.18), kind=kOutput, calls=%fused_computation.23 | convolution fusion | flops 3225419776 | bytes 6300672 | tf_op jit(solution)/shard_map/dot_general | solution.py:69
  429.5 3.5 all-to-all-start.1
  433.0 3.8 broadcast_select_fusion.1
  437.1 3.0 copy.31
  440.1 1.1 copy.28
  441.2 7.2 %all-to-all-done.1 = f32[4,256,256]{2,1,0:T(8,128)S(1)} async-done(((f32[4,256,256]{2,1,0:T(8,128)}), f32[4,256,256]{2,1,0:T(8,128)S(1)}, u32[]{:S(2)}, u32[]{:S(2)}) %all-to-all-start.1) | async-done | bytes 1048608 | tf_op jit(solution)/shard_map/all_to_all | solution.py:175
  448.6 2.8 fusion.14
  451.4 1.5 maximum_bitcast_fusion
  (20 shorter events, 2.9 us)
Async XLA Ops:
  28.7 8.8 %copy-start.1 = (f32[1,384,2048]{2,1,0:T(8,128)S(1)}, f32[1,384,2048]{2,1,0:T(8,128)}, u32[]{:S(2)}) copy-start(f32[1,384,2048]{2,1,0:T(8,128)} %param.4) | copy-start | bytes 9437188
  28.7 120.6 %all-to-all-start = ((f32[32,64,1024]{2,1,0:T(8,128)}), f32[32,64,1024]{2,1,0:T(8,128)}, u32[]{:S(2)}, u32[]{:S(2)}) async-start(f32[32,64,1024]{2,1,0:T(8,128)} %bitcast.49), calls=%async_computation | async-start | bytes 16777216 | tf_op jit(solution)/shard_map/all_to_all | solution.py:151
  38.8 161.7 %collective-permute-start = (f32[384,1024]{1,0:T(8,128)}, f32[384,1024]{1,0:T(8,128)}, u32[]{:S(2)}, u32[]{:S(2)}) collective-permute-start(f32[384,1024]{1,0:T(8,128)} %slice.24), channel_id=1, source_target_pairs={{0,1},{2,3},{4,5},{6,7},{8,9},{10,11},{12,13},{14,15},{16,17},{18,... | collective-permute-start | bytes 4718600 | tf_op jit(solution)/shard_map/ppermute | solution.py:144
  149.3 70.3 %all-to-all-start.2 = ((f32[16,64,1024]{2,1,0:T(8,128)}), f32[16,64,1024]{2,1,0:T(8,128)}, u32[]{:S(2)}, u32[]{:S(2)}) async-start(f32[16,64,1024]{2,1,0:T(8,128)} %bitcast.56), calls=%async_computation.3 | async-start | bytes 8388608 | tf_op jit(solution)/shard_map/all_to_all | solution.py:155
  158.1 154.9 %all-reduce.2.cloned.1.call-start = ((), (), s32[]{:S(2)}) async-start(), calls=%async_computation.6 | async-start | bytes 8388608 | tf_op jit(solution)/shard_map/psum | solution.py:157
  205.9 169.9 %reduce-scatter.5.cloned.1.call-start = ((), (), s32[]{:S(2)}) async-start(), calls=%async_computation.8 | async-start | bytes 5242880 | tf_op jit(solution)/shard_map/reduce_scatter | solution.py:168
  234.6 187.8 %reduce-scatter.3.cloned.1.call-start = ((), (), s32[]{:S(2)}) async-start(), calls=%async_computation.7 | async-start | bytes 5242880 | tf_op jit(solution)/shard_map/reduce_scatter | solution.py:168
  373.9 2.0 copy-start
  382.9 46.6 %all-to-all-start.3 = ((f32[4,256,256]{2,1,0:T(8,128)}), f32[4,256,256]{2,1,0:T(8,128)S(1)}, u32[]{:S(2)}, u32[]{:S(2)}) async-start(f32[4,256,256]{2,1,0:T(8,128)} %bitcast.18), calls=%async_computation.5 | async-start | bytes 2097152 | tf_op jit(solution)/shard_map/all_to_all | solution.py:175
  429.5 18.9 %all-to-all-start.1 = ((f32[4,256,256]{2,1,0:T(8,128)}), f32[4,256,256]{2,1,0:T(8,128)S(1)}, u32[]{:S(2)}, u32[]{:S(2)}) async-start(f32[4,256,256]{2,1,0:T(8,128)} %bitcast.63), calls=%async_computation.2 | async-start | bytes 2097152 | tf_op jit(solution)/shard_map/all_to_all | solution.py:175
  448.4 2.9 copy-start.2
Sparse Core Ops, SparseCore 0:
  206.1 106.9 all-reduce.1
  315.5 46.6 reduce-scatter.4
  364.6 57.7 reduce-scatter.2

commit v2 on v1

--- a/solution.py
+++ b/solution.py
@@ -10,6 +10,8 @@
 BLK = 128
 STEPS = ELIMINATED // BLK
 LINES = 8
+VMEM_BYTES = 60 * 2**20
+LIGHT = pl.CostEstimate(flops=1, bytes_accessed=1, transcendentals=0)
 
 
 def lower_inverse(diag_block):
@@ -71,8 +73,164 @@
     )
 
 
-def factor_kernel(gram_ref, work_ref, diag_ref):
-    work_ref[...] = gram_ref[...]
+PAIRS = ((0, 3), (1, 2))
+WIDE = 256
+PACKED = ELIMINATED + WIDE
+
+
+def offsets():
+    found = []
+    for pair, (long, short) in enumerate(PAIRS):
+        found.append((long, pair, 0))
+        found.append((short, pair, ELIMINATED - WIDE * long))
+    return found
+
+
+def halves(x):
+    high = x.astype(jnp.bfloat16)
+    return high, (x - high.astype(jnp.float32)).astype(jnp.bfloat16)
+
+
+def place_kernel(first_ref, dest_ref, stair_ref, rows_ref, out_ref, select_ref):
+    fronts, copies, capacity, width = out_ref.shape
+    slots, sources = select_ref.shape
+    chunk = pl.program_id(0)
+
+    @pl.when(chunk == 0)
+    def _():
+        dest = dest_ref[...]
+        named = lax.broadcasted_iota(jnp.int32, (fronts, sources), 0) == dest
+        source = lax.broadcasted_iota(jnp.int32, (sources, sources), 0)
+        later = lax.broadcasted_iota(jnp.int32, (sources, sources), 1)
+        before = jnp.dot(
+            named.astype(jnp.float32).astype(jnp.bfloat16),
+            (source < later).astype(jnp.float32).astype(jnp.bfloat16),
+            preferred_element_type=jnp.float32,
+        )
+        slot = jnp.sum(jnp.where(named, before, 0.0), axis=0, keepdims=True).astype(jnp.int32)
+        position = dest * capacity + slot
+        line = lax.broadcasted_iota(jnp.int32, (slots, sources), 0)
+        select_ref[...] = (line == position).astype(jnp.float32).astype(jnp.bfloat16)
+
+    cols = (
+        first_ref[0, 0] + chunk * width + lax.broadcasted_iota(jnp.int32, (sources, width), 1)
+    )
+    high, low = halves(jnp.where(cols >= stair_ref[...] * STAIR_BLK, rows_ref[...], 0.0))
+    select = select_ref[...]
+    placed = jnp.dot(select, high, preferred_element_type=jnp.float32) + jnp.dot(
+        select, low, preferred_element_type=jnp.float32
+    )
+    placed = placed.reshape(fronts, capacity, width)
+    for copy in range(copies):
+        out_ref[:, copy] = placed
+
+
+def place(first_col, dest, stair, rows, start, copies, n_front, capacity):
+    sources = rows.shape[0]
+    skipped = start // WIDE
+    return pl.pallas_call(
+        place_kernel,
+        grid=(ELIMINATED // WIDE,),
+        out_shape=jax.ShapeDtypeStruct((n_front, copies, capacity, ELIMINATED), jnp.float32),
+        in_specs=[
+            pl.BlockSpec(memory_space=pltpu.SMEM),
+            pl.BlockSpec((1, sources), lambda j: (0, 0)),
+            pl.BlockSpec((sources, 1), lambda j: (0, 0)),
+            pl.BlockSpec((sources, WIDE), lambda j: (0, skipped + j)),
+        ],
+        out_specs=pl.BlockSpec((n_front, copies, capacity, WIDE), lambda j: (0, 0, 0, j)),
+        scratch_shapes=[pltpu.VMEM((n_front * capacity, sources), jnp.bfloat16)],
+        compiler_params=pltpu.CompilerParams(vmem_limit_bytes=VMEM_BYTES),
+        cost_estimate=LIGHT,
+    )((first_col + start).reshape(1, 1), dest, stair, rows)
+
+
+def gram_kernel(turn_ref, own_ref, child_ref, *rest):
+    outs, (high_ref, low_ref, packed_ref) = rest[:-3], rest[-3:]
+    own_count = own_ref.shape[0]
+    child = child_ref[:, 0].reshape(-1, ELIMINATED)
+    high_ref[:own_count], low_ref[:own_count] = halves(own_ref[...])
+    high_ref[own_count:], low_ref[own_count:] = halves(child)
+    dims = (((0,), (0,)), ((), ()))
+    for block, pair, offset in offsets():
+        start = WIDE * block
+        left_high, left_low = high_ref[:, start : start + WIDE], low_ref[:, start : start + WIDE]
+        right_high, right_low = high_ref[:, start:], low_ref[:, start:]
+        total = lax.dot_general(left_high, right_high, dims, preferred_element_type=jnp.float32)
+        total += lax.dot_general(left_high, right_low, dims, preferred_element_type=jnp.float32)
+        total += lax.dot_general(left_low, right_high, dims, preferred_element_type=jnp.float32)
+        for half in range(2):
+            packed_ref[2 * pair + half, :, offset : offset + ELIMINATED - start] = total[
+                BLK * half : BLK * (half + 1)
+            ]
+    count = len(outs)
+    for s in range(count):
+        outs[s][...] = packed_ref[lax.rem(turn_ref[0, 0] + s, count)]
+
+
+def packed_gram(turn, own_panel, arrived):
+    fronts, _, capacity, _ = arrived.shape
+    rows = own_panel.shape[0] + fronts * capacity
+    vmem = pl.BlockSpec(memory_space=pltpu.VMEM)
+    return pl.pallas_call(
+        gram_kernel,
+        grid=(1,),
+        out_shape=[jax.ShapeDtypeStruct((BLK, PACKED), jnp.float32)] * 4
+        + [jax.ShapeDtypeStruct((rows, ELIMINATED), jnp.bfloat16)] * 2,
+        in_specs=[
+            pl.BlockSpec(memory_space=pltpu.SMEM),
+            vmem,
+            pl.BlockSpec((fronts, 1, capacity, ELIMINATED), lambda j: (0, 0, 0, 0)),
+        ],
+        out_specs=[vmem] * 6,
+        scratch_shapes=[pltpu.VMEM((4, BLK, PACKED), jnp.float32)],
+        compiler_params=pltpu.CompilerParams(vmem_limit_bytes=VMEM_BYTES),
+        cost_estimate=LIGHT,
+    )(turn, own_panel, arrived)
+
+
+def cross_kernel(high_ref, low_ref, own_ref, child_ref, out_ref):
+    child = child_ref[:, 0].reshape(-1, WIDE)
+    high, low = halves(jnp.concatenate([own_ref[...], child], axis=0))
+    dims = (((0,), (0,)), ((), ()))
+    total = lax.dot_general(high, high_ref[...], dims, preferred_element_type=jnp.float32)
+    total += lax.dot_general(high, low_ref[...], dims, preferred_element_type=jnp.float32)
+    total += lax.dot_general(low, high_ref[...], dims, preferred_element_type=jnp.float32)
+    out_ref[...] = total
+
+
+def cross(high, low, own, start, child, part):
+    fronts, _, capacity, _ = child.shape
+    skipped = start // WIDE
+    vmem = pl.BlockSpec(memory_space=pltpu.VMEM)
+    return pl.pallas_call(
+        cross_kernel,
+        grid=(ELIMINATED // WIDE,),
+        out_shape=jax.ShapeDtypeStruct((ELIMINATED, ELIMINATED), jnp.float32),
+        in_specs=[
+            vmem,
+            vmem,
+            pl.BlockSpec((own.shape[0], WIDE), lambda j: (0, skipped + j)),
+            pl.BlockSpec((fronts, 1, capacity, WIDE), lambda j: (0, part, 0, j)),
+        ],
+        out_specs=pl.BlockSpec((WIDE, ELIMINATED), lambda j: (j, 0)),
+        compiler_params=pltpu.CompilerParams(vmem_limit_bytes=VMEM_BYTES),
+        cost_estimate=LIGHT,
+    )(high, low, own, child)
+
+
+def factor_kernel(turn_ref, *rest):
+    pieces, (work_ref, leading_ref, diag_ref, packed_ref) = rest[:-4], rest[-4:]
+    count = len(pieces)
+    for s in range(count):
+        packed_ref[lax.rem(turn_ref[0, 0] + count - s, count)] = pieces[s][...]
+    work_ref[...] = jnp.zeros_like(work_ref)
+    for block, pair, offset in offsets():
+        start = WIDE * block
+        for half in range(2):
+            work_ref[start + BLK * half : start + BLK * (half + 1), start:] = packed_ref[
+                2 * pair + half, :, offset : offset + ELIMINATED - start
+            ]
     row = lax.broadcasted_iota(jnp.int32, (BLK, BLK), 0)
     col = lax.broadcasted_iota(jnp.int32, (BLK, BLK), 1)
 
@@ -94,30 +252,62 @@
         return 0
 
     lax.fori_loop(0, STEPS, step, 0)
-
-
-def factor(gram):
+    taken = leading_ref.shape[0] // BLK
+    place_of = lax.broadcasted_iota(jnp.int32, (BLK, ELIMINATED), 1) // BLK
+    for b in range(taken):
+        block = turn_ref[0, 0] * taken + b
+        here = pl.ds(pl.multiple_of(block * BLK, BLK), BLK)
+        diag = jnp.concatenate([diag_ref[here, :]] * STEPS, axis=1)
+        leading_ref[BLK * b : BLK * (b + 1), :] = jnp.where(
+            place_of > block, work_ref[here, :], jnp.where(place_of == block, diag, 0.0)
+        )
+    for k in range(STEPS - 1):
+        work_ref[BLK * k : BLK * (k + 1), BLK * (k + 1) :] = jnp.zeros(
+            (BLK, ELIMINATED - BLK * (k + 1)), jnp.float32
+        )
+
+
+def factor(turn, pieces):
+    vmem = pl.BlockSpec(memory_space=pltpu.VMEM)
     return pl.pallas_call(
         factor_kernel,
         out_shape=(
             jax.ShapeDtypeStruct((ELIMINATED, ELIMINATED), jnp.float32),
-            jax.ShapeDtypeStruct((ELIMINATED, BLK), jnp.float32),
+            jax.ShapeDtypeStruct((ELIMINATED // len(pieces), ELIMINATED), jnp.float32),
         ),
-        in_specs=[pl.BlockSpec(memory_space=pltpu.VMEM)],
-        out_specs=(pl.BlockSpec(memory_space=pltpu.VMEM), pl.BlockSpec(memory_space=pltpu.VMEM)),
-        compiler_params=pltpu.CompilerParams(vmem_limit_bytes=48 * 1024 * 1024),
-        cost_estimate=pl.CostEstimate(flops=10**10, bytes_accessed=9 * 2**20, transcendentals=1024),
-    )(gram)
-
-
-def cross(a, b):
-    return lax.dot_general(
-        a,
-        b,
-        (((0,), (0,)), ((), ())),
-        precision=lax.Precision.HIGH,
-        preferred_element_type=jnp.float32,
-    )
+        in_specs=[pl.BlockSpec(memory_space=pltpu.SMEM)] + [vmem] * len(pieces),
+        out_specs=(vmem, vmem),
+        scratch_shapes=[
+            pltpu.VMEM((ELIMINATED, BLK), jnp.float32),
+            pltpu.VMEM((len(pieces), BLK, PACKED), jnp.float32),
+        ],
+        compiler_params=pltpu.CompilerParams(vmem_limit_bytes=VMEM_BYTES),
+        cost_estimate=LIGHT,
+    )(turn, *pieces)
+
+
+def join_kernel(col_ref, leading_ref, first_ref, second_ref, out_ref):
+    parts, _, width = first_ref.shape
+    for j in range(parts):
+        cols = slice(width * j, width * (j + 1))
+        out_ref[0, :, cols] = jnp.where(col_ref[0, 0] == 0, leading_ref[:, cols], first_ref[j])
+        out_ref[0, :, ELIMINATED + width * j : ELIMINATED + width * (j + 1)] = second_ref[j]
+
+
+def join(col, leading, first, second):
+    vmem = pl.BlockSpec(memory_space=pltpu.VMEM)
+    rows = leading.shape[0]
+    return pl.pallas_call(
+        join_kernel,
+        out_shape=jax.ShapeDtypeStruct((1, rows, 2 * ELIMINATED), jnp.float32),
+        in_specs=[pl.BlockSpec(memory_space=pltpu.SMEM)] + [vmem] * 3,
+        out_specs=vmem,
+        compiler_params=pltpu.CompilerParams(vmem_limit_bytes=VMEM_BYTES),
+    )(col, leading, first, second)
+
+
+def shifted(x, shift, count):
+    return lax.ppermute(x, "row", [(i, (i + shift) % count) for i in range(count)])
 
 
 def body(own_rows, child_rows, child_dest, child_stair):
@@ -128,55 +318,58 @@
     col_index = lax.axis_index("col")
     row_index = lax.axis_index("row")
     quarter = ELIMINATED // row_count
-    global_cols = col_index * half_cols + lax.broadcasted_iota(
-        jnp.int32, (source_rows, half_cols), 1
-    )
-    masked_rows = jnp.where(global_cols >= (child_stair * STAIR_BLK)[:, None], child_rows, 0.0)
-    targets = child_dest[:, 0]
-    order = jnp.arange(source_rows, dtype=jnp.int32)
-    earlier = (targets[:, None] == targets[None, :]) & (order[None, :] < order[:, None])
-    slot = jnp.sum(earlier.astype(jnp.int32), axis=1)
-    position = targets * capacity + slot
-    send = jnp.zeros((n_front * capacity, half_cols), jnp.float32).at[position].set(masked_rows)
-
     own = own_rows[0]
-    own_a, own_b = own[:, :ELIMINATED], own[:, ELIMINATED:]
+    own_a = own[:, :ELIMINATED]
     passed = lax.ppermute(own_a, "col", [(0, 1)])
+
+    first_col = col_index * half_cols
+    dest, stair = child_dest.reshape(1, source_rows), child_stair.reshape(source_rows, 1)
+    doubled = place(first_col, dest, stair, child_rows, 0, 2, n_front, capacity)
+    single = place(first_col, dest, stair, child_rows, ELIMINATED, 1, n_front, capacity)
+    doubled, single, passed = lax.optimization_barrier((doubled, single, passed))
+    arrived = lax.all_to_all(
+        doubled.reshape(2 * n_front * capacity, ELIMINATED),
+        ("front", "col"),
+        split_axis=0,
+        concat_axis=0,
+        tiled=True,
+    ).reshape(n_front, 2, capacity, ELIMINATED)
+    child_b = lax.all_to_all(
+        single.reshape(n_front * capacity, ELIMINATED), "front", split_axis=0, concat_axis=0, tiled=True
+    ).reshape(n_front, 1, capacity, ELIMINATED)
     own_panel = jnp.where(col_index == 0, own_a, passed)
 
-    doubled = jnp.broadcast_to(
-        send[:, :ELIMINATED].reshape(n_front, 1, capacity, ELIMINATED),
-        (n_front, 2, capacity, ELIMINATED),
-    ).reshape(2 * n_front * capacity, ELIMINATED)
-    arrived = lax.all_to_all(doubled, ("front", "col"), split_axis=0, concat_axis=0, tiled=True)
-    arrived = arrived.reshape(n_front, 2, capacity, ELIMINATED)
-    child_panel = arrived[:, 0].reshape(n_front * capacity, ELIMINATED)
-    child_a = arrived[:, 1].reshape(n_front * capacity, ELIMINATED)
-    child_b = lax.all_to_all(send[:, ELIMINATED:], "front", split_axis=0, concat_axis=0, tiled=True)
-
-    gram = lax.psum(cross(own_panel, own_panel) + cross(child_panel, child_panel), "row")
-    work, diag = factor(gram)
-    block_row = lax.broadcasted_iota(jnp.int32, (ELIMINATED, ELIMINATED), 0) // BLK
-    block_col = lax.broadcasted_iota(jnp.int32, (ELIMINATED, ELIMINATED), 1) // BLK
-    inverse = jnp.where(block_row >= block_col, work, 0.0)
-    leading = jnp.where(
-        block_row < block_col, work, jnp.where(block_row == block_col, jnp.tile(diag, (1, STEPS)), 0.0)
-    )
-    leading = lax.dynamic_slice_in_dim(leading, row_index * quarter, quarter, 0)
-
-    def finish(own_part, child_part):
-        sums = lax.psum_scatter(
-            cross(own_part, own_panel) + cross(child_part, child_panel),
-            "row",
-            scatter_dimension=0,
-            tiled=True,
-        )
-        rows = exact_dot(inverse, sums, ((1,), (1,)))
-        return lax.all_to_all(rows, "row", split_axis=0, concat_axis=1, tiled=True)
-
-    first = jnp.where(col_index == 0, leading, finish(own_a, child_a))
-    second = finish(own_b, child_b)
-    return jnp.concatenate([first, second], 1)[None]
+    turn = row_index.reshape(1, 1)
+    *shares, high, low = packed_gram(turn, own_panel, arrived)
+    products_a = cross(high, low, own, 0, arrived, 1)
+    shares, products_a = lax.optimization_barrier((shares, products_a))
+    sent = [shifted(shares[shift], shift, row_count) for shift in range(1, row_count)]
+    piece = shares[0]
+    for other in sent:
+        piece = piece + other
+    pieces = [piece] + [shifted(piece, shift, row_count) for shift in range(1, row_count)]
+
+    def summed(products):
+        return lax.psum_scatter(products, "row", scatter_dimension=0, tiled=True)
+
+    def solved(sums):
+        rows = lax.dot_general(
+            inverse,
+            sums,
+            (((1,), (1,)), ((), ())),
+            precision=lax.Precision.HIGH,
+            preferred_element_type=jnp.float32,
+        )
+        return lax.all_to_all(
+            rows.reshape(row_count, quarter, quarter), "row", split_axis=0, concat_axis=0, tiled=True
+        )
+
+    sums_a = summed(products_a)
+    products_b = cross(high, low, own, ELIMINATED, child_b, 0)
+    pieces, products_b = lax.optimization_barrier((pieces, products_b))
+    sums_b = summed(products_b)
+    inverse, leading = factor(turn, pieces)
+    return join(col_index.reshape(1, 1), leading, solved(sums_a), solved(sums_b))
 
 
 def solution(mesh):

time: 465 us -> 415 us (0.89)
  Pallas kernels: 60.9 us -> 121 us
  matrix products: 59.7 us -> 9.61 us
  waiting for transfers between devices: 252 us -> 209 us
  local copies, waits for them, and re-layouts: 23.4 us -> 5.05 us
  other arithmetic: 19.3 us -> 1.56 us
  blocking collectives: 0 us -> 17.6 us
  starting transfers between devices: 30.5 us -> 36.6 us
    ppermute x0 -> x6, waiting for transfers between devices: none -> 69.6 us  [shifted(): lax.ppermute(x, 'row', [(i, (i + shift) % count) for i in range(count)])]
    psum x1 -> x0, waiting for transfers between devices: 63 us -> none  [body(): lax.psum(cross(own_panel, own_panel) + cross(child_panel, child_panel), '...]
    pallas_call x0 -> x6, Pallas kernels: none -> 58.6 us  [the longest x2 29.5 us: cross(): pl.pallas_call(cross_kernel, grid=(ELIMINATED // WIDE,), out_shape=jax.Sh...]
    dot_general x8 -> x2, matrix products: 59.7 us -> 9.61 us  [solved(): lax.dot_general(inverse, sums, (((1,), (1,)), ((), ())), precision=lax.Pr...]
    reduce_scatter x2, waiting for transfers between devices: 36 us -> 0.01 us  [summed(): return lax.psum_scatter(products, 'row', scatter_dimension=0, tiled=True)]
    all_to_all x0 -> x1, blocking collectives: none -> 17.6 us  [solved(): lax.all_to_all(rows.reshape(row_count, quarter, quarter), 'row', split_ax...]
    ppermute x1, waiting for transfers between devices: 31.6 us -> 17.9 us  [body(): passed = lax.ppermute(own_a, 'col', [(0, 1)])]
    slice x3 -> x1, local copies, waits for them, and re-layouts: 12.7 us -> 1.51 us  [body(): own_a = own[:, :ELIMINATED]]
  transfers between devices with their start and end apart: 8 -> 12, of which waited for: 6 -> 8; matrix products, arithmetic and copies ran while one was open for 16% -> 3% of each run, Pallas kernels for 13% -> 22%
where the time goes in v2:
time: 415 us; the launch traced here: 414 us
  waiting for transfers between devices  209 us (50%)
  Pallas kernels  121 us (29%)
  starting transfers between devices  36.6 us (9%)
  blocking collectives  17.6 us (4%)
  between operations  13.6 us (3%)
  matrix products  9.61 us (2%)
  local copies, waits for them, and re-layouts  5.05 us (1%)
    all_to_all x1, waiting for transfers between devices, body(): lax.all_to_all(doubled.reshape(2 * n_front * capacity, ELIMINATED), ('fro...  110 us
    ppermute x6, waiting for transfers between devices, shifted(): lax.ppermute(x, 'row', [(i, (i + shift) % count) for i in range(count)])  69.6 us
    pallas_call x1, Pallas kernels, factor(): pl.pallas_call(factor_kernel, out_shape=(jax.ShapeDtypeStruct((ELIMINATED...  62.9 us
    pallas_call x2, Pallas kernels, cross(): pl.pallas_call(cross_kernel, grid=(ELIMINATED // WIDE,), out_shape=jax.Sh...  29.5 us
    ppermute x1, waiting for transfers between devices, body(): passed = lax.ppermute(own_a, 'col', [(0, 1)])  17.9 us
    all_to_all x1, blocking collectives, solved(): lax.all_to_all(rows.reshape(row_count, quarter, quarter), 'row', split_ax...  17.6 us
    pallas_call x2, Pallas kernels, place(): pl.pallas_call(place_kernel, grid=(ELIMINATED // WIDE,), out_shape=jax.Sh...  14 us
    pallas_call x1, Pallas kernels, packed_gram(): pl.pallas_call(gram_kernel, grid=(1,), out_shape=[jax.ShapeDtypeStruct((B...  11.7 us
  transfers between devices with their start and end apart: 12, of which 8 were waited for; matrix products, arithmetic and copies ran while one was open for 3% of the time, Pallas kernels for 22%

profile of v2, /device:TPU:0, one launch (start us, length us, event | category | flops | bytes accessed | tf_op | source)
XLA Modules:
  0.0 414.3 jit_solution(8457008678101965511)
XLA Ops:
  6.5 1.5 slice.4
  8.0 4.0 collective-permute-start
  12.1 1.5 copy.5.stair_ref
  13.6 6.6 %shard_map.47 = f32[16,1,64,1024]{3,2,1,0:T(8,128)} custom-call(s32[1,1]{1,0:T(1,128)} %bitcast.6.first_ref, s32[1,512]{1,0:T(1,128)} %bitcast.24, s32[512,1]{1,0:T(8,128)} %copy.5.stair_ref, f32[512,2048]{1,0:T(8,128)} %rows_ref.3), custom_call_target="tpu_custom_call" | custom-call | flops 1 | bytes 1 | tf_op jit(solution)/shard_map/pallas_call | solution.py:131
  20.3 7.4 %shard_map.46 = f32[16,2,64,1024]{3,2,1,0:T(8,128)} custom-call(s32[1,1]{1,0:T(1,128)} %bitcast.3.first_ref, s32[1,512]{1,0:T(1,128)} %bitcast.25, s32[512,1]{1,0:T(8,128)} %copy.5.stair_ref, f32[512,2048]{1,0:T(8,128)} %rows_ref.3), custom_call_target="tpu_custom_call" | custom-call | flops 1 | bytes 1 | tf_op jit(solution)/shard_map/pallas_call | solution.py:131
  27.6 17.9 %collective-permute-done = f32[384,1024]{1,0:T(8,128)S(1)} collective-permute-done((f32[384,1024]{1,0:T(8,128)S(1)}, f32[384,1024]{1,0:T(8,128)S(1)}, u32[]{:S(2)}, u32[]{:S(2)}) %collective-permute-start) | collective-permute-done | bytes 1572896 | tf_op jit(solution)/shard_map/ppermute | solution.py:323
  45.6 1.1 copy-done.3
  46.7 9.3 %all-to-all-start = ((f32[32,64,1024]{2,1,0:T(8,128)}), f32[32,64,1024]{2,1,0:T(8,128)}, u32[]{:S(2)}, u32[]{:S(2)}) async-start(f32[32,64,1024]{2,1,0:T(8,128)} %bitcast.17), calls=%async_computation | async-start | bytes 16777216 | tf_op jit(solution)/shard_map/all_to_all | solution.py:330
  56.1 1.4 broadcast_select_fusion.own_ref
  57.5 110.2 %all-to-all-done = f32[32,64,1024]{2,1,0:T(8,128)} async-done(((f32[32,64,1024]{2,1,0:T(8,128)}), f32[32,64,1024]{2,1,0:T(8,128)}, u32[]{:S(2)}, u32[]{:S(2)}) %all-to-all-start) | async-done | bytes 8388640 | tf_op jit(solution)/shard_map/all_to_all | solution.py:330
  167.7 11.7 %shard_map.48 = (f32[128,1280]{1,0:T(8,128)}, f32[128,1280]{1,0:T(8,128)}, f32[128,1280]{1,0:T(8,128)}, f32[128,1280]{1,0:T(8,128)}, bf16[1408,1024]{1,0:T(8,128)(2,1)}, /*index=5*/bf16[1408,1024]{1,0:T(8,128)(2,1)}) custom-call(s32[1,1]{1,0:T(1,128)} %bitcast.1.turn_ref, f32[384,1024]{1,0:T(8,128)} %broadcast_select_fusion.own_ref, ...), custom_call_target="tpu_custom_call" | custom-call | flops 1 | bytes 1 | tf_op jit(solution)/shard_map/pallas_call | solution.py:175
  179.4 14.8 %shard_map.49 = f32[1024,1024]{1,0:T(8,128)} custom-call(bf16[1408,1024]{1,0:T(8,128)(2,1)} %get-tuple-element.32.high_ref, bf16[1408,1024]{1,0:T(8,128)(2,1)} %get-tuple-element.33.low_ref, f32[384,2048]{1,0:T(8,128)} %bitcast.19, f32[16,2,64,1024]{3,2,1,0:T(8,128)} %bitcast.8.child_ref), custom_call_target="tpu_custom_call" | custom-call | flops 1 | bytes 1 | tf_op jit(solution)/shard_map/pallas_call | solution.py:206
  194.2 8.9 %all-to-all-start.1 = ((f32[16,64,1024]{2,1,0:T(8,128)}), f32[16,64,1024]{2,1,0:T(8,128)}, u32[]{:S(2)}, u32[]{:S(2)}) async-start(f32[16,64,1024]{2,1,0:T(8,128)} %bitcast.22), calls=%async_computation.1 | async-start | bytes 8388608 | tf_op jit(solution)/shard_map/all_to_all | solution.py:337
  203.2 1.7 collective-permute-start.1
  204.9 2.8 collective-permute-start.2
  207.7 1.4 collective-permute-start.3
  209.1 25.5 %collective-permute-done.1 = f32[128,1280]{1,0:T(8,128)S(1)} collective-permute-done((f32[128,1280]{1,0:T(8,128)S(1)}, f32[128,1280]{1,0:T(8,128)S(1)}, u32[]{:S(2)}, u32[]{:S(2)}) %collective-permute-start.1) | collective-permute-done | bytes 655392 | tf_op jit(solution)/shard_map/ppermute | solution.py:310
  234.6 29.8 %collective-permute-done.2 = f32[128,1280]{1,0:T(8,128)S(1)} collective-permute-done((f32[128,1280]{1,0:T(8,128)S(1)}, f32[128,1280]{1,0:T(8,128)S(1)}, u32[]{:S(2)}, u32[]{:S(2)}) %collective-permute-start.2) | collective-permute-done | bytes 655392 | tf_op jit(solution)/shard_map/ppermute | solution.py:310
  264.6 1.4 collective-permute-start.6
  266.0 2.0 collective-permute-start.5
  268.0 1.3 collective-permute-start.4
  269.3 14.7 %shard_map.50 = f32[1024,1024]{1,0:T(8,128)} custom-call(bf16[1408,1024]{1,0:T(8,128)(2,1)} %get-tuple-element.32.high_ref, bf16[1408,1024]{1,0:T(8,128)(2,1)} %get-tuple-element.33.low_ref, f32[384,2048]{1,0:T(8,128)} %bitcast.20, f32[16,1,64,1024]{3,2,1,0:T(8,128)} %bitcast.10.child_ref), custom_call_target="tpu_custom_call" | custom-call | flops 1 | bytes 1 | tf_op jit(solution)/shard_map/pallas_call | solution.py:206
  284.4 0.9 collective-permute-done.5.rest_2_
  285.2 13.2 %collective-permute-done.4.rest_1_ = f32[128,1280]{1,0:T(8,128)S(1)} collective-permute-done((f32[128,1280]{1,0:T(8,128)S(1)}, f32[128,1280]{1,0:T(8,128)S(1)}, u32[]{:S(2)}, u32[]{:S(2)}) %collective-permute-start.4) | collective-permute-done | bytes 655392 | tf_op jit(solution)/shard_map/ppermute | solution.py:310
  298.4 0.8 copy-done.7
  299.3 62.9 %shard_map.51 = (f32[1024,1024]{1,0:T(8,128)}, f32[256,1024]{1,0:T(8,128)}) custom-call(s32[1,1]{1,0:T(1,128)} %bitcast.1.turn_ref, f32[128,1280]{1,0:T(8,128)} %copy-done.2, f32[128,1280]{1,0:T(8,128)} %copy-done.7, f32[128,1280]{1,0:T(8,128)} %copy-done.6, f32[128,1280]{1,0:T(8,128)} %copy-done.5), custom_call_target="tpu_custom_call" | custom-call | flops 1 | bytes 1 | tf_op jit(solution)/shard_map/pallas_call | solution.py:272
  362.1 5.3 %fusion = f32[1024,256]{1,0:T(8,128)} fusion(f32[1024,1024]{1,0:T(8,128)} %get-tuple-element.44, f32[256,1024]{1,0:T(8,128)} %reduce-scatter.3.cloned.1.call-done), kind=kOutput, calls=%fused_computation.2 | convolution fusion | flops 1610612736 | bytes 6291456 | tf_op jit(solution)/shard_map/dot_general | solution.py:356
  367.4 3.6 all-to-all-start.2
  371.1 4.3 %fusion.1 = f32[1024,256]{1,0:T(8,128)S(1)} fusion(f32[1024,1024]{1,0:T(8,128)} %get-tuple-element.44, f32[256,1024]{1,0:T(8,128)} %reduce-scatter.5.cloned.1.call-done), kind=kOutput, calls=%fused_computation.3 | convolution fusion | flops 1610612736 | bytes 6291456 | tf_op jit(solution)/shard_map/dot_general | solution.py:356
  375.4 11.0 %all-to-all-done.2.first_ref = f32[4,256,256]{2,1,0:T(8,128)S(1)} async-done(((f32[4,256,256]{2,1,0:T(8,128)}), f32[4,256,256]{2,1,0:T(8,128)S(1)}, u32[]{:S(2)}, u32[]{:S(2)}) %all-to-all-start.2) | async-done | bytes 1048608 | tf_op jit(solution)/shard_map/all_to_all | solution.py:363
  386.4 17.6 %all_to_all.28.second_ref = f32[4,256,256]{2,1,0:T(8,128)} all-to-all(f32[4,256,256]{2,1,0:T(8,128)S(1)} %bitcast.23), channel_id=1, replica_groups=mesh['front'=16,'row'=4,'col'=2] {'row'}, dimensions={0} | all-to-all | bytes 2097152 | tf_op jit(solution)/shard_map/all_to_all | solution.py:363
  404.0 3.4 shard_map.52
  (30 shorter events, 0.6 us)
Async XLA Ops:
  8.0 37.5 %collective-permute-start = (f32[384,1024]{1,0:T(8,128)S(1)}, f32[384,1024]{1,0:T(8,128)S(1)}, u32[]{:S(2)}, u32[]{:S(2)}) collective-permute-start(f32[384,1024]{1,0:T(8,128)S(1)} %slice.4), channel_id=1, source_target_pairs={{0,1},{2,3},{4,5},{6,7},{8,9},{10,11},{12,13},{14,15},{16,17},{18,... | collective-permute-start | bytes 4718600 | tf_op jit(solution)/shard_map/ppermute | solution.py:323
  45.6 1.1 copy-start.3
  46.7 9.4 %copy-start = (f32[1,384,2048]{2,1,0:T(8,128)S(1)}, f32[1,384,2048]{2,1,0:T(8,128)}, u32[]{:S(2)}) copy-start(f32[1,384,2048]{2,1,0:T(8,128)} %param.4) | copy-start | bytes 9437188
  46.7 120.9 %all-to-all-start = ((f32[32,64,1024]{2,1,0:T(8,128)}), f32[32,64,1024]{2,1,0:T(8,128)}, u32[]{:S(2)}, u32[]{:S(2)}) async-start(f32[32,64,1024]{2,1,0:T(8,128)} %bitcast.17), calls=%async_computation | async-start | bytes 16777216 | tf_op jit(solution)/shard_map/all_to_all | solution.py:330
  56.0 306.1 %reduce-scatter.3.cloned.1.call-start = ((), (), s32[]{:S(2)}) async-start(), calls=%async_computation.6 | async-start | bytes 5242880 | tf_op jit(solution)/shard_map/reduce_scatter | solution.py:353
  194.2 9.0 %copy-start.10 = (f32[128,1280]{1,0:T(8,128)S(1)}, f32[128,1280]{1,0:T(8,128)}, u32[]{:S(2)}) copy-start(f32[128,1280]{1,0:T(8,128)} %get-tuple-element.35) | copy-start | bytes 1966084
  194.2 10.7 %copy-start.9 = (f32[128,1280]{1,0:T(8,128)S(1)}, f32[128,1280]{1,0:T(8,128)}, u32[]{:S(2)}) copy-start(f32[128,1280]{1,0:T(8,128)} %get-tuple-element.36) | copy-start | bytes 1966084
  194.2 13.5 %copy-start.8 = (f32[128,1280]{1,0:T(8,128)S(1)}, f32[128,1280]{1,0:T(8,128)}, u32[]{:S(2)}) copy-start(f32[128,1280]{1,0:T(8,128)} %get-tuple-element.37) | copy-start | bytes 1966084
  194.2 70.2 %copy-start.4 = (f32[128,1280]{1,0:T(8,128)S(1)}, f32[128,1280]{1,0:T(8,128)}, u32[]{:S(2)}) copy-start(f32[128,1280]{1,0:T(8,128)} %get-tuple-element.34) | copy-start | bytes 1966084
  194.2 75.1 %all-to-all-start.1 = ((f32[16,64,1024]{2,1,0:T(8,128)}), f32[16,64,1024]{2,1,0:T(8,128)}, u32[]{:S(2)}, u32[]{:S(2)}) async-start(f32[16,64,1024]{2,1,0:T(8,128)} %bitcast.22), calls=%async_computation.1 | async-start | bytes 8388608 | tf_op jit(solution)/shard_map/all_to_all | solution.py:337
  203.1 168.0 %reduce-scatter.5.cloned.1.call-start = ((), (), s32[]{:S(2)}) async-start(), calls=%async_computation.7 | async-start | bytes 5242880 | tf_op jit(solution)/shard_map/reduce_scatter | solution.py:353
  203.2 31.4 %collective-permute-start.1 = (f32[128,1280]{1,0:T(8,128)S(1)}, f32[128,1280]{1,0:T(8,128)S(1)}, u32[]{:S(2)}, u32[]{:S(2)}) collective-permute-start(f32[128,1280]{1,0:T(8,128)S(1)} %copy-done.10), channel_id=1, source_target_pairs={{0,2},{2,4},{4,6},{6,0},{1,3},{3,5},{5,7},{7,1},{8,10},{10,12},{12... | collective-permute-start | bytes 1966088 | tf_op jit(solution)/shard_map/ppermute | solution.py:310
  204.9 59.5 %collective-permute-start.2 = (f32[128,1280]{1,0:T(8,128)S(1)}, f32[128,1280]{1,0:T(8,128)S(1)}, u32[]{:S(2)}, u32[]{:S(2)}) collective-permute-start(f32[128,1280]{1,0:T(8,128)S(1)} %copy-done.9), channel_id=1, source_target_pairs={{0,4},{2,6},{4,0},{6,2},{1,5},{3,7},{5,1},{7,3},{8,12},{10,14},{12... | collective-permute-start | bytes 1966088 | tf_op jit(solution)/shard_map/ppermute | solution.py:310
  207.7 56.8 %collective-permute-start.3 = (f32[128,1280]{1,0:T(8,128)S(1)}, f32[128,1280]{1,0:T(8,128)S(1)}, u32[]{:S(2)}, u32[]{:S(2)}) collective-permute-start(f32[128,1280]{1,0:T(8,128)S(1)} %copy-done.8), channel_id=1, source_target_pairs={{0,6},{2,0},{4,2},{6,4},{1,7},{3,1},{5,3},{7,5},{8,14},{10,8},{12,... | collective-permute-start | bytes 1966088 | tf_op jit(solution)/shard_map/ppermute | solution.py:310
  264.6 19.5 %copy-start.2 = (f32[128,1280]{1,0:T(8,128)}, f32[128,1280]{1,0:T(8,128)S(1)}, u32[]{:S(2)}) copy-start(f32[128,1280]{1,0:T(8,128)S(1)} %add_add_fusion.rest_0_) | copy-start | bytes 1966084
  264.6 19.8 %collective-permute-start.6 = (f32[128,1280]{1,0:T(8,128)S(1)}, f32[128,1280]{1,0:T(8,128)S(1)}, u32[]{:S(2)}, u32[]{:S(2)}) collective-permute-start(f32[128,1280]{1,0:T(8,128)S(1)} %add_add_fusion.rest_0_), channel_id=1, source_target_pairs={{0,6},{2,0},{4,2},{6,4},{1,7},{3,1},{5,3},{7,5},{8,14},{10,8},{12,... | collective-permute-start | bytes 1966088 | tf_op jit(solution)/shard_map/ppermute | solution.py:310
  266.0 19.2 %collective-permute-start.5 = (f32[128,1280]{1,0:T(8,128)S(1)}, f32[128,1280]{1,0:T(8,128)S(1)}, u32[]{:S(2)}, u32[]{:S(2)}) collective-permute-start(f32[128,1280]{1,0:T(8,128)S(1)} %add_add_fusion.rest_0_), channel_id=1, source_target_pairs={{0,4},{2,6},{4,0},{6,2},{1,5},{3,7},{5,1},{7,3},{8,12},{10,14},{12... | collective-permute-start | bytes 1966088 | tf_op jit(solution)/shard_map/ppermute | solution.py:310
  268.0 30.4 %collective-permute-start.4 = (f32[128,1280]{1,0:T(8,128)S(1)}, f32[128,1280]{1,0:T(8,128)S(1)}, u32[]{:S(2)}, u32[]{:S(2)}) collective-permute-start(f32[128,1280]{1,0:T(8,128)S(1)} %add_add_fusion.rest_0_), channel_id=1, source_target_pairs={{0,2},{2,4},{4,6},{6,0},{1,3},{3,5},{5,7},{7,1},{8,10},{10,12},{12... | collective-permute-start | bytes 1966088 | tf_op jit(solution)/shard_map/ppermute | solution.py:310
  284.3 14.1 %copy-start.5 = (f32[128,1280]{1,0:T(8,128)}, f32[128,1280]{1,0:T(8,128)S(1)}, u32[]{:S(2)}) copy-start(f32[128,1280]{1,0:T(8,128)S(1)} %collective-permute-done.6.rest_3_) | copy-start | bytes 1966084
  285.2 13.2 %copy-start.6 = (f32[128,1280]{1,0:T(8,128)}, f32[128,1280]{1,0:T(8,128)S(1)}, u32[]{:S(2)}) copy-start(f32[128,1280]{1,0:T(8,128)S(1)} %collective-permute-done.5.rest_2_) | copy-start | bytes 1966084
  298.4 0.9 copy-start.7
  367.4 19.0 %all-to-all-start.2 = ((f32[4,256,256]{2,1,0:T(8,128)}), f32[4,256,256]{2,1,0:T(8,128)S(1)}, u32[]{:S(2)}, u32[]{:S(2)}) async-start(f32[4,256,256]{2,1,0:T(8,128)} %bitcast.11), calls=%async_computation.3 | async-start | bytes 2097152 | tf_op jit(solution)/shard_map/all_to_all | solution.py:363
  386.4 17.6 %copy-start.1 = (f32[4,256,256]{2,1,0:T(8,128)}, f32[4,256,256]{2,1,0:T(8,128)S(1)}, u32[]{:S(2)}) copy-start(f32[4,256,256]{2,1,0:T(8,128)S(1)} %all-to-all-done.2.first_ref) | copy-start | bytes 3145732
Sparse Core Ops, SparseCore 0:
  194.3 79.5 reduce-scatter.2
  298.5 47.2 reduce-scatter.4

commit v3 on v2

--- a/solution.py
+++ b/solution.py
@@ -14,7 +14,7 @@
 LIGHT = pl.CostEstimate(flops=1, bytes_accessed=1, transcendentals=0)
 
 
-def lower_inverse(diag_block):
+def lower_inverse(diag_block, beside):
     lane = lax.broadcasted_iota(jnp.int32, (LINES, BLK), 1)
     sublane = lax.broadcasted_iota(jnp.int32, (LINES, BLK), 0)
     count = BLK // LINES
@@ -50,6 +50,7 @@
         for t in range(1, LINES):
             merged = jnp.where(sublane == t, solved[t], merged)
         strips[b] = merged
+        beside(b, count)
         for i in range(b + 1, count):
             below = strips[i]
             rest = jnp.where(within, 0.0, below)
@@ -67,12 +68,6 @@
     return jnp.where(row >= col, jnp.concatenate(strips, axis=0), 0.0)
 
 
-def exact_dot(a, b, dims):
-    return lax.dot_general(
-        a, b, (dims, ((), ())), precision=lax.Precision.HIGHEST, preferred_element_type=jnp.float32
-    )
-
-
 PAIRS = ((0, 3), (1, 2))
 WIDE = 256
 PACKED = ELIMINATED + WIDE
@@ -145,8 +140,8 @@
     )((first_col + start).reshape(1, 1), dest, stair, rows)
 
 
-def gram_kernel(turn_ref, own_ref, child_ref, *rest):
-    outs, (high_ref, low_ref, packed_ref) = rest[:-3], rest[-3:]
+def gram_kernel(turn_ref, own_ref, child_ref, *outs):
+    high_ref, low_ref, packed_ref = outs[5:]
     own_count = own_ref.shape[0]
     child = child_ref[:, 0].reshape(-1, ELIMINATED)
     high_ref[:own_count], low_ref[:own_count] = halves(own_ref[...])
@@ -163,9 +158,15 @@
             packed_ref[2 * pair + half, :, offset : offset + ELIMINATED - start] = total[
                 BLK * half : BLK * (half + 1)
             ]
-    count = len(outs)
-    for s in range(count):
-        outs[s][...] = packed_ref[lax.rem(turn_ref[0, 0] + s, count)]
+    mine_ref, right_ref, left_ref, right_rest_ref, left_rest_ref, *_ = outs
+    turn = turn_ref[0, 0]
+    here, right, over, left = [lax.rem(turn + s, 4) for s in range(4)]
+    middle = BLK // 2
+    mine_ref[...] = packed_ref[here]
+    right_ref[:middle], right_ref[middle:] = packed_ref[over, :middle], packed_ref[right, middle:]
+    left_ref[:middle], left_ref[middle:] = packed_ref[over, middle:], packed_ref[left, :middle]
+    right_rest_ref[...] = packed_ref[right, :middle]
+    left_rest_ref[...] = packed_ref[left, middle:]
 
 
 def packed_gram(turn, own_panel, arrived):
@@ -175,14 +176,15 @@
     return pl.pallas_call(
         gram_kernel,
         grid=(1,),
-        out_shape=[jax.ShapeDtypeStruct((BLK, PACKED), jnp.float32)] * 4
+        out_shape=[jax.ShapeDtypeStruct((BLK, PACKED), jnp.float32)] * 3
+        + [jax.ShapeDtypeStruct((BLK // 2, PACKED), jnp.float32)] * 2
         + [jax.ShapeDtypeStruct((rows, ELIMINATED), jnp.bfloat16)] * 2,
         in_specs=[
             pl.BlockSpec(memory_space=pltpu.SMEM),
             vmem,
             pl.BlockSpec((fronts, 1, capacity, ELIMINATED), lambda j: (0, 0, 0, 0)),
         ],
-        out_specs=[vmem] * 6,
+        out_specs=[vmem] * 7,
         scratch_shapes=[pltpu.VMEM((4, BLK, PACKED), jnp.float32)],
         compiler_params=pltpu.CompilerParams(vmem_limit_bytes=VMEM_BYTES),
         cost_estimate=LIGHT,
@@ -219,12 +221,31 @@
     )(high, low, own, child)
 
 
-def factor_kernel(turn_ref, *rest):
-    pieces, (work_ref, leading_ref, diag_ref, packed_ref) = rest[:-4], rest[-4:]
-    count = len(pieces)
-    for s in range(count):
-        packed_ref[lax.rem(turn_ref[0, 0] + count - s, count)] = pieces[s][...]
+def sharp_dot(a, b, dims):
+    (high, low), (other_high, other_low) = a, b
+    dims = (dims, ((), ()))
+    total = lax.dot_general(high, other_high, dims, preferred_element_type=jnp.float32)
+    total += lax.dot_general(high, other_low, dims, preferred_element_type=jnp.float32)
+    return total + lax.dot_general(low, other_high, dims, preferred_element_type=jnp.float32)
+
+
+PLAIN = ((1,), (0,))
+
+
+def factor_kernel(
+    turn_ref, piece_ref, before_ref, after_ref, across_ref, across_rest_ref,
+    high_ref, low_ref, leading_ref, work_ref, diag_ref, packed_ref, panel_high_ref, panel_low_ref,
+):
+    turn = turn_ref[0, 0]
+    middle = BLK // 2
+    packed_ref[turn] = piece_ref[...]
+    packed_ref[lax.rem(turn + 1, 4)] = after_ref[...]
+    packed_ref[lax.rem(turn + 3, 4)] = before_ref[...]
+    packed_ref[lax.rem(turn + 2, 4), :middle] = across_ref[...]
+    packed_ref[lax.rem(turn + 2, 4), middle:] = across_rest_ref[...]
     work_ref[...] = jnp.zeros_like(work_ref)
+    panel_high_ref[...] = jnp.zeros_like(panel_high_ref)
+    panel_low_ref[...] = jnp.zeros_like(panel_low_ref)
     for block, pair, offset in offsets():
         start = WIDE * block
         for half in range(2):
@@ -233,77 +254,133 @@
             ]
     row = lax.broadcasted_iota(jnp.int32, (BLK, BLK), 0)
     col = lax.broadcasted_iota(jnp.int32, (BLK, BLK), 1)
+    place_of = lax.broadcasted_iota(jnp.int32, (BLK, ELIMINATED), 1) // BLK
+    chunk_of = lax.broadcasted_iota(jnp.int32, (BLK, WIDE), 1) // BLK
+    deferred = [(i, c) for i in range(2, STEPS) for c in range(ELIMINATED // WIDE)]
 
     def step(k, _):
         here = pl.ds(pl.multiple_of(k * BLK, BLK), BLK)
         block = work_ref[here, here]
-        inverse = lower_inverse(block)
-        diag_ref[here, :] = jnp.where(row <= col, exact_dot(inverse, block, ((1,), (0,))), 0.0)
-        work_ref[here, :] = exact_dot(inverse, work_ref[here, :], ((1,), (0,)))
+        turned = {}
+
+        def update(i, c):
+            below = i > k
+            rows, cols = slice(BLK * i, BLK * (i + 1)), slice(WIDE * c, WIDE * (c + 1))
+            if i not in turned:
+                kept = jnp.where(below, 1.0, 0.0)
+                turned[i] = [
+                    (ref[:, rows].astype(jnp.float32) * kept).T.astype(jnp.bfloat16)
+                    for ref in (panel_high_ref, panel_low_ref)
+                ]
+            panel = (panel_high_ref[:, cols], panel_low_ref[:, cols])
+            cleared = jnp.where(below, k - 1 - c * (WIDE // BLK), -1)
+            old = jnp.where(chunk_of == cleared, 0.0, work_ref[rows, cols])
+            work_ref[rows, cols] = old - sharp_dot(turned[i], panel, PLAIN)
+
+        def beside(b, count):
+            for i, c in deferred[len(deferred) * b // count : len(deferred) * (b + 1) // count]:
+                update(i, c)
+
+        inverse = lower_inverse(block, beside)
+        rows = sharp_dot(halves(inverse), halves(work_ref[here, :]), PLAIN)
+        work_ref[here, :] = rows
+        diag_ref[here, :] = jnp.where(row <= col, work_ref[here, here], 0.0)
         work_ref[here, here] = inverse
-
-        def update(i, _):
-            there = pl.ds(pl.multiple_of(i * BLK, BLK), BLK)
-            work_ref[there, here] = jnp.zeros((BLK, BLK), jnp.float32)
-            work_ref[there, :] -= exact_dot(work_ref[here, there], work_ref[here, :], ((0,), (0,)))
-            return 0
-
-        lax.fori_loop(k + 1, STEPS, update, 0)
+        panel_high_ref[...], panel_low_ref[...] = halves(work_ref[here, :])
+
+        @pl.when(k < STEPS - 1)
+        def _():
+            there = pl.ds(pl.multiple_of((k + 1) * BLK, BLK), BLK)
+            left = [ref[:, there].astype(jnp.float32).T.astype(jnp.bfloat16) for ref in (panel_high_ref, panel_low_ref)]
+            old = jnp.where(place_of == k, 0.0, work_ref[there, :])
+            work_ref[there, :] = old - sharp_dot(left, (panel_high_ref[...], panel_low_ref[...]), PLAIN)
+
         return 0
 
     lax.fori_loop(0, STEPS, step, 0)
     taken = leading_ref.shape[0] // BLK
-    place_of = lax.broadcasted_iota(jnp.int32, (BLK, ELIMINATED), 1) // BLK
     for b in range(taken):
-        block = turn_ref[0, 0] * taken + b
+        block = turn * taken + b
         here = pl.ds(pl.multiple_of(block * BLK, BLK), BLK)
         diag = jnp.concatenate([diag_ref[here, :]] * STEPS, axis=1)
         leading_ref[BLK * b : BLK * (b + 1), :] = jnp.where(
             place_of > block, work_ref[here, :], jnp.where(place_of == block, diag, 0.0)
         )
-    for k in range(STEPS - 1):
-        work_ref[BLK * k : BLK * (k + 1), BLK * (k + 1) :] = jnp.zeros(
-            (BLK, ELIMINATED - BLK * (k + 1)), jnp.float32
-        )
-
-
-def factor(turn, pieces):
+    for k in range(STEPS):
+        rows = slice(BLK * k, BLK * (k + 1))
+        high_ref[rows, :], low_ref[rows, :] = halves(jnp.where(place_of <= k, work_ref[rows, :], 0.0))
+
+
+def factor(turn, piece, before, after, across, across_rest):
     vmem = pl.BlockSpec(memory_space=pltpu.VMEM)
     return pl.pallas_call(
         factor_kernel,
         out_shape=(
-            jax.ShapeDtypeStruct((ELIMINATED, ELIMINATED), jnp.float32),
-            jax.ShapeDtypeStruct((ELIMINATED // len(pieces), ELIMINATED), jnp.float32),
+            jax.ShapeDtypeStruct((ELIMINATED, ELIMINATED), jnp.bfloat16),
+            jax.ShapeDtypeStruct((ELIMINATED, ELIMINATED), jnp.bfloat16),
+            jax.ShapeDtypeStruct((ELIMINATED // 4, ELIMINATED), jnp.float32),
         ),
-        in_specs=[pl.BlockSpec(memory_space=pltpu.SMEM)] + [vmem] * len(pieces),
-        out_specs=(vmem, vmem),
+        in_specs=[pl.BlockSpec(memory_space=pltpu.SMEM)] + [vmem] * 5,
+        out_specs=(vmem, vmem, vmem),
         scratch_shapes=[
+            pltpu.VMEM((ELIMINATED, ELIMINATED), jnp.float32),
             pltpu.VMEM((ELIMINATED, BLK), jnp.float32),
-            pltpu.VMEM((len(pieces), BLK, PACKED), jnp.float32),
+            pltpu.VMEM((4, BLK, PACKED), jnp.float32),
+            pltpu.VMEM((BLK, ELIMINATED), jnp.bfloat16),
+            pltpu.VMEM((BLK, ELIMINATED), jnp.bfloat16),
         ],
         compiler_params=pltpu.CompilerParams(vmem_limit_bytes=VMEM_BYTES),
         cost_estimate=LIGHT,
-    )(turn, *pieces)
-
-
-def join_kernel(col_ref, leading_ref, first_ref, second_ref, out_ref):
-    parts, _, width = first_ref.shape
+    )(turn, piece, before, after, across, across_rest)
+
+
+def solve_kernel(high_ref, low_ref, first_ref, second_ref, out_ref):
+    parts, quarter, _ = out_ref.shape
+    for j, sums_ref in enumerate((first_ref, second_ref)):
+        sums = halves(sums_ref[...])
+        for i in range(parts):
+            rows, depth = slice(quarter * i, quarter * (i + 1)), quarter * (i + 1)
+            out_ref[i, :, quarter * j : quarter * (j + 1)] = sharp_dot(
+                (high_ref[rows, :depth], low_ref[rows, :depth]),
+                tuple(x[:, :depth] for x in sums),
+                ((1,), (1,)),
+            )
+
+
+def solve(high, low, first, second):
+    vmem = pl.BlockSpec(memory_space=pltpu.VMEM)
+    quarter = first.shape[0]
+    return pl.pallas_call(
+        solve_kernel,
+        out_shape=jax.ShapeDtypeStruct((ELIMINATED // quarter, quarter, 2 * quarter), jnp.float32),
+        in_specs=[vmem] * 4,
+        out_specs=vmem,
+        compiler_params=pltpu.CompilerParams(vmem_limit_bytes=VMEM_BYTES),
+        cost_estimate=LIGHT,
+    )(high, low, first, second)
+
+
+def join_kernel(col_ref, leading_ref, rows_ref, out_ref):
+    parts, _, both = rows_ref.shape
+    width = both // 2
     for j in range(parts):
         cols = slice(width * j, width * (j + 1))
-        out_ref[0, :, cols] = jnp.where(col_ref[0, 0] == 0, leading_ref[:, cols], first_ref[j])
-        out_ref[0, :, ELIMINATED + width * j : ELIMINATED + width * (j + 1)] = second_ref[j]
-
-
-def join(col, leading, first, second):
+        out_ref[0, :, cols] = jnp.where(
+            col_ref[0, 0] == 0, leading_ref[:, cols], rows_ref[j, :, :width]
+        )
+        out_ref[0, :, ELIMINATED + width * j : ELIMINATED + width * (j + 1)] = rows_ref[j, :, width:]
+
+
+def join(col, leading, rows):
     vmem = pl.BlockSpec(memory_space=pltpu.VMEM)
-    rows = leading.shape[0]
     return pl.pallas_call(
         join_kernel,
-        out_shape=jax.ShapeDtypeStruct((1, rows, 2 * ELIMINATED), jnp.float32),
-        in_specs=[pl.BlockSpec(memory_space=pltpu.SMEM)] + [vmem] * 3,
+        out_shape=jax.ShapeDtypeStruct((1, leading.shape[0], 2 * ELIMINATED), jnp.float32),
+        in_specs=[pl.BlockSpec(memory_space=pltpu.SMEM)] + [vmem] * 2,
         out_specs=vmem,
         compiler_params=pltpu.CompilerParams(vmem_limit_bytes=VMEM_BYTES),
-    )(col, leading, first, second)
+        cost_estimate=LIGHT,
+    )(col, leading, rows)
 
 
 def shifted(x, shift, count):
@@ -340,36 +417,29 @@
     own_panel = jnp.where(col_index == 0, own_a, passed)
 
     turn = row_index.reshape(1, 1)
-    *shares, high, low = packed_gram(turn, own_panel, arrived)
+    mine, right, left, right_rest, left_rest, high, low = packed_gram(turn, own_panel, arrived)
     products_a = cross(high, low, own, 0, arrived, 1)
-    shares, products_a = lax.optimization_barrier((shares, products_a))
-    sent = [shifted(shares[shift], shift, row_count) for shift in range(1, row_count)]
-    piece = shares[0]
-    for other in sent:
-        piece = piece + other
-    pieces = [piece] + [shifted(piece, shift, row_count) for shift in range(1, row_count)]
+    mine, right, left, products_a = lax.optimization_barrier((mine, right, left, products_a))
+    middle = BLK // 2
+    from_left, from_right = shifted(right, 1, row_count), shifted(left, -1, row_count)
+    rest_left = shifted(right_rest + from_left[:middle], 1, row_count)
+    rest_right = shifted(left_rest + from_right[:middle], -1, row_count)
+    piece = mine + jnp.concatenate(
+        [rest_left + from_right[middle:], from_left[middle:] + rest_right], axis=0
+    )
+    before, after = shifted(piece, 1, row_count), shifted(piece, -1, row_count)
+    across, across_rest = shifted(before[:middle], 1, row_count), shifted(after[middle:], -1, row_count)
+    pieces = (piece, before, after, across, across_rest)
 
     def summed(products):
         return lax.psum_scatter(products, "row", scatter_dimension=0, tiled=True)
 
-    def solved(sums):
-        rows = lax.dot_general(
-            inverse,
-            sums,
-            (((1,), (1,)), ((), ())),
-            precision=lax.Precision.HIGH,
-            preferred_element_type=jnp.float32,
-        )
-        return lax.all_to_all(
-            rows.reshape(row_count, quarter, quarter), "row", split_axis=0, concat_axis=0, tiled=True
-        )
-
-    sums_a = summed(products_a)
     products_b = cross(high, low, own, ELIMINATED, child_b, 0)
     pieces, products_b = lax.optimization_barrier((pieces, products_b))
-    sums_b = summed(products_b)
-    inverse, leading = factor(turn, pieces)
-    return join(col_index.reshape(1, 1), leading, solved(sums_a), solved(sums_b))
+    inverse_high, inverse_low, leading = factor(turn, *pieces)
+    rows = solve(inverse_high, inverse_low, summed(products_a), summed(products_b))
+    rows = lax.all_to_all(rows, "row", split_axis=0, concat_axis=0, tiled=True)
+    return join(col_index.reshape(1, 1), leading, rows)
 
 
 def solution(mesh):

time: 415 us -> 390 us (0.940)
  waiting for transfers between devices: 209 us -> 189 us
  blocking collectives: 17.6 us -> 30.1 us
  matrix products: 9.61 us -> 0 us
  Pallas kernels: 121 us -> 113 us
    pallas_call x1, Pallas kernels: 62.9 us -> 49.2 us  [factor(): pl.pallas_call(factor_kernel, out_shape=(jax.ShapeDtypeStruct((ELIMINATED...]
    all_to_all x1, blocking collectives: 17.6 us -> 30.1 us  [body(): rows = lax.all_to_all(rows, 'row', split_axis=0, concat_axis=0, tiled=True)]
    all_to_all x1 -> x0, waiting for transfers between devices: 11 us -> none  [solved(): lax.all_to_all(rows.reshape(row_count, quarter, quarter), 'row', split_ax...]
    dot_general x2 -> x0, matrix products: 9.61 us -> none  [solved(): lax.dot_general(inverse, sums, (((1,), (1,)), ((), ())), precision=lax.Pr...]
    ppermute x6 -> x8, waiting for transfers between devices: 69.6 us -> 60.2 us  [shifted(): lax.ppermute(x, 'row', [(i, (i + shift) % count) for i in range(count)])]
    pallas_call x1 -> x2, Pallas kernels: 3.39 us -> 9.84 us  [the longest x1 6.39 us: solve(): pl.pallas_call(solve_kernel, out_shape=jax.ShapeDtypeStruct((ELIMINATED /...]
    ppermute x6 -> x8, starting transfers between devices: 10.7 us -> 14.3 us  [shifted(): lax.ppermute(x, 'row', [(i, (i + shift) % count) for i in range(count)])]
  transfers between devices with their start and end apart: 12 -> 13, of which waited for: 8 -> 6; matrix products, arithmetic and copies ran while one was open for 3% -> 1% of each run, Pallas kernels for 22% -> 20%
where the time goes in v3:
time: 390 us
  waiting for transfers between devices  189 us (48%)
  Pallas kernels  113 us (29%)
  starting transfers between devices  36.6 us (9%)
  blocking collectives  30.1 us (8%)
  between operations  13.6 us (3%)
  local copies, waits for them, and re-layouts  5.5 us (1%)
    all_to_all x1, waiting for transfers between devices, body(): lax.all_to_all(doubled.reshape(2 * n_front * capacity, ELIMINATED), ('fro...  110 us
    ppermute x8, waiting for transfers between devices, shifted(): lax.ppermute(x, 'row', [(i, (i + shift) % count) for i in range(count)])  60.2 us
    pallas_call x1, Pallas kernels, factor(): pl.pallas_call(factor_kernel, out_shape=(jax.ShapeDtypeStruct((ELIMINATED...  49.2 us
    all_to_all x1, blocking collectives, body(): rows = lax.all_to_all(rows, 'row', split_axis=0, concat_axis=0, tiled=True)  30.1 us
    pallas_call x2, Pallas kernels, cross(): pl.pallas_call(cross_kernel, grid=(ELIMINATED // WIDE,), out_shape=jax.Sh...  29.5 us
    ppermute x1, waiting for transfers between devices, body(): passed = lax.ppermute(own_a, 'col', [(0, 1)])  18.6 us
    ppermute x8, starting transfers between devices, shifted(): lax.ppermute(x, 'row', [(i, (i + shift) % count) for i in range(count)])  14.3 us
    pallas_call x2, Pallas kernels, place(): pl.pallas_call(place_kernel, grid=(ELIMINATED // WIDE,), out_shape=jax.Sh...  14.1 us
  transfers between devices with their start and end apart: 13, of which 6 were waited for; matrix products, arithmetic and copies ran while one was open for 1% of the time, Pallas kernels for 20%

profile of v3, /device:TPU:0, one launch (start us, length us, event | category | flops | bytes accessed | tf_op | source)
XLA Modules:
  0.0 389.8 jit_solution(1824426889563678471)
XLA Ops:
  6.5 1.5 slice.28
  8.1 4.0 %collective-permute-start = (f32[384,1024]{1,0:T(8,128)S(1)}, f32[384,1024]{1,0:T(8,128)S(1)}, u32[]{:S(2)}, u32[]{:S(2)}) collective-permute-start(f32[384,1024]{1,0:T(8,128)S(1)} %slice.28), channel_id=1, source_target_pairs={{0,1},{2,3},{4,5},{6,7},{8,9},{10,11},{12,13},{14,15},{16,17},{18,... | collective-permute-start | bytes 4718600 | tf_op jit(solution)/shard_map/ppermute | solution.py:400
  12.1 0.9 copy.5.stair_ref
  13.0 6.7 %shard_map.47 = f32[16,1,64,1024]{3,2,1,0:T(8,128)} custom-call(s32[1,1]{1,0:T(1,128)} %bitcast.6.first_ref, s32[1,512]{1,0:T(1,128)} %bitcast.17, s32[512,1]{1,0:T(8,128)} %copy.5.stair_ref, f32[512,2048]{1,0:T(8,128)} %rows_ref.3), custom_call_target="tpu_custom_call" | custom-call | flops 1 | bytes 1 | tf_op jit(solution)/shard_map/pallas_call | solution.py:126
  19.6 7.4 %shard_map.46 = f32[16,2,64,1024]{3,2,1,0:T(8,128)} custom-call(s32[1,1]{1,0:T(1,128)} %bitcast.3.first_ref, s32[1,512]{1,0:T(1,128)} %bitcast.18, s32[512,1]{1,0:T(8,128)} %copy.5.stair_ref, f32[512,2048]{1,0:T(8,128)} %rows_ref.3), custom_call_target="tpu_custom_call" | custom-call | flops 1 | bytes 1 | tf_op jit(solution)/shard_map/pallas_call | solution.py:126
  27.0 18.6 %collective-permute-done = f32[384,1024]{1,0:T(8,128)S(1)} collective-permute-done((f32[384,1024]{1,0:T(8,128)S(1)}, f32[384,1024]{1,0:T(8,128)S(1)}, u32[]{:S(2)}, u32[]{:S(2)}) %collective-permute-start) | collective-permute-done | bytes 1572896 | tf_op jit(solution)/shard_map/ppermute | solution.py:400
  45.6 1.1 copy-done.2
  46.8 9.3 %all-to-all-start = ((f32[32,64,1024]{2,1,0:T(8,128)}), f32[32,64,1024]{2,1,0:T(8,128)}, u32[]{:S(2)}, u32[]{:S(2)}) async-start(f32[32,64,1024]{2,1,0:T(8,128)} %bitcast.11), calls=%async_computation | async-start | bytes 16777216 | tf_op jit(solution)/shard_map/all_to_all | solution.py:407
  56.1 1.4 broadcast_select_fusion.own_ref
  57.5 110.2 %all-to-all-done = f32[32,64,1024]{2,1,0:T(8,128)} async-done(((f32[32,64,1024]{2,1,0:T(8,128)}), f32[32,64,1024]{2,1,0:T(8,128)}, u32[]{:S(2)}, u32[]{:S(2)}) %all-to-all-start) | async-done | bytes 8388640 | tf_op jit(solution)/shard_map/all_to_all | solution.py:407
  167.7 10.9 %shard_map.48 = (f32[128,1280]{1,0:T(8,128)}, f32[128,1280]{1,0:T(8,128)}, f32[128,1280]{1,0:T(8,128)}, f32[64,1280]{1,0:T(8,128)}, f32[64,1280]{1,0:T(8,128)}, ...) custom-call(s32[1,1]{1,0:T(1,128)} %bitcast.1.turn_ref, f32[384,1024]{1,0:T(8,128)} %broadcast_select_fusion.own_ref, ...), custom_call_target="tpu_custom_call" | custom-call | flops 1 | bytes 1 | tf_op jit(solution)/shard_map/pallas_call | solution.py:176
  178.5 14.8 %shard_map.49 = f32[1024,1024]{1,0:T(8,128)} custom-call(bf16[1408,1024]{1,0:T(8,128)(2,1)} %get-tuple-element.33.high_ref, bf16[1408,1024]{1,0:T(8,128)(2,1)} %get-tuple-element.34.low_ref, f32[384,2048]{1,0:T(8,128)} %bitcast.13, f32[16,2,64,1024]{3,2,1,0:T(8,128)} %bitcast.8.child_ref), custom_call_target="tpu_custom_call" | custom-call | flops 1 | bytes 1 | tf_op jit(solution)/shard_map/pallas_call | solution.py:208
  193.3 1.1 copy-done.12
  194.4 1.5 collective-permute-start.1
  195.9 8.9 %all-to-all-start.1 = ((f32[16,64,1024]{2,1,0:T(8,128)}), f32[16,64,1024]{2,1,0:T(8,128)}, u32[]{:S(2)}, u32[]{:S(2)}) async-start(f32[16,64,1024]{2,1,0:T(8,128)} %bitcast.16), calls=%async_computation.1 | async-start | bytes 8388608 | tf_op jit(solution)/shard_map/all_to_all | solution.py:414
  204.9 1.8 collective-permute-start.3
  206.7 10.1 %collective-permute-done.1 = f32[128,1280]{1,0:T(8,128)S(1)} collective-permute-done((f32[128,1280]{1,0:T(8,128)S(1)}, f32[128,1280]{1,0:T(8,128)S(1)}, u32[]{:S(2)}, u32[]{:S(2)}) %collective-permute-start.1) | collective-permute-done | bytes 655392 | tf_op jit(solution)/shard_map/ppermute | solution.py:387
  216.8 1.7 collective-permute-start.2
  218.6 17.5 %collective-permute-done.3 = f32[128,1280]{1,0:T(8,128)S(1)} collective-permute-done((f32[128,1280]{1,0:T(8,128)S(1)}, f32[128,1280]{1,0:T(8,128)S(1)}, u32[]{:S(2)}, u32[]{:S(2)}) %collective-permute-start.3) | collective-permute-done | bytes 655392 | tf_op jit(solution)/shard_map/ppermute | solution.py:387
  236.1 3.3 collective-permute-start.4
  239.5 14.8 %collective-permute-done.4 = f32[64,1280]{1,0:T(8,128)S(1)} collective-permute-done((f32[64,1280]{1,0:T(8,128)S(1)}, f32[64,1280]{1,0:T(8,128)S(1)}, u32[]{:S(2)}, u32[]{:S(2)}) %collective-permute-start.4) | collective-permute-done | bytes 327712 | tf_op jit(solution)/shard_map/ppermute | solution.py:387
  254.4 3.8 collective-permute-start.6
  258.2 17.8 %collective-permute-done.6.after_ref = f32[128,1280]{1,0:T(8,128)S(1)} collective-permute-done((f32[128,1280]{1,0:T(8,128)S(1)}, f32[128,1280]{1,0:T(8,128)S(1)}, u32[]{:S(2)}, u32[]{:S(2)}) %collective-permute-start.6) | collective-permute-done | bytes 655392 | tf_op jit(solution)/shard_map/ppermute | solution.py:387
  276.0 1.6 collective-permute-start.8
  277.7 0.6 collective-permute-start.7
  278.2 14.7 %shard_map.50 = f32[1024,1024]{1,0:T(8,128)} custom-call(bf16[1408,1024]{1,0:T(8,128)(2,1)} %get-tuple-element.33.high_ref, bf16[1408,1024]{1,0:T(8,128)(2,1)} %get-tuple-element.34.low_ref, f32[384,2048]{1,0:T(8,128)} %bitcast.14, f32[16,1,64,1024]{3,2,1,0:T(8,128)} %bitcast.10.child_ref), custom_call_target="tpu_custom_call" | custom-call | flops 1 | bytes 1 | tf_op jit(solution)/shard_map/pallas_call | solution.py:208
  293.1 0.7 copy-done.8
  293.7 0.1 copy-done.9
  293.9 49.2 %shard_map.51 = (bf16[1024,1024]{1,0:T(8,128)(2,1)}, bf16[1024,1024]{1,0:T(8,128)(2,1)}, f32[256,1024]{1,0:T(8,128)}) custom-call(s32[1,1]{1,0:T(1,128)} %bitcast.1.turn_ref, f32[128,1280]{1,0:T(8,128)} %copy-done.1, f32[128,1280]{1,0:T(8,128)} %copy-done.4, f32[128,1280]{1,0:T(8,128)} %copy-done.3, f32[64,1280]{1,0:T(8,128)} %copy-done.9, f32[64,1280]{1,0:T(8,128)} %copy-done.8), custom_call_target="tpu_custom_call" | custom-call | flops 1 | bytes 1 | tf_op jit(solution)/shard_map/pallas_call | solution.py:316
  343.0 6.4 %shard_map.52 = f32[4,256,512]{2,1,0:T(8,128)} custom-call(bf16[1024,1024]{1,0:T(8,128)(2,1)} %get-tuple-element.47.high_ref, bf16[1024,1024]{1,0:T(8,128)(2,1)} %get-tuple-element.48.low_ref, f32[256,1024]{1,0:T(8,128)} %reduce-scatter.3.cloned.1.call-done.first_ref, f32[256,1024]{1,0:T(8,128)} %reduce-scatter.5.cloned.1.call-done.second_ref), custom_call_target="tpu_custom_call" | custom-call | flops 1 | bytes 1 | tf_op jit(solution)/shard_map/pallas_call | solution.py:353
  349.4 30.1 %all_to_all.23.rows_ref = f32[4,256,512]{2,1,0:T(8,128)} all-to-all(f32[4,256,512]{2,1,0:T(8,128)} %shard_map.52), channel_id=1, replica_groups=mesh['front'=16,'row'=4,'col'=2] {'row'}, dimensions={0} | all-to-all | bytes 4194304 | tf_op jit(solution)/shard_map/all_to_all | solution.py:441
  379.5 3.5 shard_map.53
  (40 shorter events, 0.4 us)
Async XLA Ops:
  6.5 5.5 %copy-start.10 = (s32[512]{0:T(512)S(1)}, s32[512]{0:T(512)}, u32[]{:S(2)}) copy-start(s32[512]{0:T(512)} %param.7) | copy-start | bytes 6148
  8.1 37.5 %collective-permute-start = (f32[384,1024]{1,0:T(8,128)S(1)}, f32[384,1024]{1,0:T(8,128)S(1)}, u32[]{:S(2)}, u32[]{:S(2)}) collective-permute-start(f32[384,1024]{1,0:T(8,128)S(1)} %slice.28), channel_id=1, source_target_pairs={{0,1},{2,3},{4,5},{6,7},{8,9},{10,11},{12,13},{14,15},{16,17},{18,... | collective-permute-start | bytes 4718600 | tf_op jit(solution)/shard_map/ppermute | solution.py:400
  45.6 1.1 copy-start.2
  46.8 9.4 %copy-start = (f32[1,384,2048]{2,1,0:T(8,128)S(1)}, f32[1,384,2048]{2,1,0:T(8,128)}, u32[]{:S(2)}) copy-start(f32[1,384,2048]{2,1,0:T(8,128)} %param.4) | copy-start | bytes 9437188
  46.8 120.9 %all-to-all-start = ((f32[32,64,1024]{2,1,0:T(8,128)}), f32[32,64,1024]{2,1,0:T(8,128)}, u32[]{:S(2)}, u32[]{:S(2)}) async-start(f32[32,64,1024]{2,1,0:T(8,128)} %bitcast.11), calls=%async_computation | async-start | bytes 16777216 | tf_op jit(solution)/shard_map/all_to_all | solution.py:407
  56.1 287.0 %reduce-scatter.3.cloned.1.call-start = ((), (), s32[]{:S(2)}) async-start(), calls=%async_computation.5 | async-start | bytes 5242880 | tf_op jit(solution)/shard_map/reduce_scatter | solution.py:435
  193.3 1.1 copy-start.12
  194.4 22.4 %collective-permute-start.1 = (f32[128,1280]{1,0:T(8,128)S(1)}, f32[128,1280]{1,0:T(8,128)S(1)}, u32[]{:S(2)}, u32[]{:S(2)}) collective-permute-start(f32[128,1280]{1,0:T(8,128)S(1)} %copy-done.12), channel_id=1, source_target_pairs={{0,2},{2,4},{4,6},{6,0},{1,3},{3,5},{5,7},{7,1},{8,10},{10,12},{12... | collective-permute-start | bytes 1966088 | tf_op jit(solution)/shard_map/ppermute | solution.py:387
  195.9 9.0 %copy-start.11 = (f32[128,1280]{1,0:T(8,128)S(1)}, f32[128,1280]{1,0:T(8,128)}, u32[]{:S(2)}) copy-start(f32[128,1280]{1,0:T(8,128)} %get-tuple-element.38) | copy-start | bytes 1966084
  195.9 20.9 %copy-start.6 = (f32[64,1280]{1,0:T(8,128)S(1)}, f32[64,1280]{1,0:T(8,128)}, u32[]{:S(2)}) copy-start(f32[64,1280]{1,0:T(8,128)} %get-tuple-element.36) | copy-start | bytes 983044
  195.9 40.1 %copy-start.7 = (f32[64,1280]{1,0:T(8,128)S(1)}, f32[64,1280]{1,0:T(8,128)}, u32[]{:S(2)}) copy-start(f32[64,1280]{1,0:T(8,128)} %get-tuple-element.39) | copy-start | bytes 983044
  195.9 82.3 %all-to-all-start.1 = ((f32[16,64,1024]{2,1,0:T(8,128)}), f32[16,64,1024]{2,1,0:T(8,128)}, u32[]{:S(2)}, u32[]{:S(2)}) async-start(f32[16,64,1024]{2,1,0:T(8,128)} %bitcast.16), calls=%async_computation.1 | async-start | bytes 8388608 | tf_op jit(solution)/shard_map/all_to_all | solution.py:414
  204.8 49.5 %copy-start.5 = (f32[128,1280]{1,0:T(8,128)S(1)}, f32[128,1280]{1,0:T(8,128)}, u32[]{:S(2)}) copy-start(f32[128,1280]{1,0:T(8,128)} %get-tuple-element.35) | copy-start | bytes 1966084
  204.8 138.2 %reduce-scatter.5.cloned.1.call-start = ((), (), s32[]{:S(2)}) async-start(), calls=%async_computation.6 | async-start | bytes 5242880 | tf_op jit(solution)/shard_map/reduce_scatter | solution.py:435
  204.9 31.2 %collective-permute-start.3 = (f32[128,1280]{1,0:T(8,128)S(1)}, f32[128,1280]{1,0:T(8,128)S(1)}, u32[]{:S(2)}, u32[]{:S(2)}) collective-permute-start(f32[128,1280]{1,0:T(8,128)S(1)} %copy-done.11), channel_id=1, source_target_pairs={{0,6},{2,0},{4,2},{6,4},{1,7},{3,1},{5,3},{7,5},{8,14},{10,8},{12,... | collective-permute-start | bytes 1966088 | tf_op jit(solution)/shard_map/ppermute | solution.py:387
  216.8 19.2 %collective-permute-start.2 = (f32[64,1280]{1,0:T(8,128)S(1)}, f32[64,1280]{1,0:T(8,128)S(1)}, u32[]{:S(2)}, u32[]{:S(2)}) collective-permute-start(f32[64,1280]{1,0:T(8,128)S(1)} %slice_add_fusion.3), channel_id=1, source_target_pairs={{0,2},{2,4},{4,6},{6,0},{1,3},{3,5},{5,7},{7,1},{8,10},{10,12},{12... | collective-permute-start | bytes 983048 | tf_op jit(solution)/shard_map/ppermute | solution.py:387
  236.1 18.2 %collective-permute-start.4 = (f32[64,1280]{1,0:T(8,128)S(1)}, f32[64,1280]{1,0:T(8,128)S(1)}, u32[]{:S(2)}, u32[]{:S(2)}) collective-permute-start(f32[64,1280]{1,0:T(8,128)S(1)} %get-tuple-element.52), channel_id=1, source_target_pairs={{0,6},{2,0},{4,2},{6,4},{1,7},{3,1},{5,3},{7,5},{8,14},{10,8},{12,... | collective-permute-start | bytes 983048 | tf_op jit(solution)/shard_map/ppermute | solution.py:387
  254.4 38.6 %copy-start.1 = (f32[128,1280]{1,0:T(8,128)}, f32[128,1280]{1,0:T(8,128)S(1)}, u32[]{:S(2)}) copy-start(f32[128,1280]{1,0:T(8,128)S(1)} %maximum_add_fusion.piece_ref) | copy-start | bytes 1966084
  254.4 21.6 %collective-permute-start.6 = (f32[128,1280]{1,0:T(8,128)S(1)}, f32[128,1280]{1,0:T(8,128)S(1)}, u32[]{:S(2)}, u32[]{:S(2)}) collective-permute-start(f32[128,1280]{1,0:T(8,128)S(1)} %maximum_add_fusion.piece_ref), channel_id=1, source_target_pairs={{0,6},{2,0},{4,2},{6,4},{1,7},{3,1},{5,3},{7,5},{8,14},{10,8},{12,... | collective-permute-start | bytes 1966088 | tf_op jit(solution)/shard_map/ppermute | solution.py:387
  258.2 19.5 %collective-permute-start.5 = (f32[128,1280]{1,0:T(8,128)S(1)}, f32[128,1280]{1,0:T(8,128)S(1)}, u32[]{:S(2)}, u32[]{:S(2)}) collective-permute-start(f32[128,1280]{1,0:T(8,128)S(1)} %maximum_add_fusion.piece_ref), channel_id=1, source_target_pairs={{0,2},{2,4},{4,6},{6,0},{1,3},{3,5},{5,7},{7,1},{8,10},{10,12},{12... | collective-permute-start | bytes 1966088 | tf_op jit(solution)/shard_map/ppermute | solution.py:387
  276.0 17.0 %copy-start.3 = (f32[128,1280]{1,0:T(8,128)}, f32[128,1280]{1,0:T(8,128)S(1)}, u32[]{:S(2)}) copy-start(f32[128,1280]{1,0:T(8,128)S(1)} %collective-permute-done.6.after_ref) | copy-start | bytes 1966084
  276.0 17.0 %collective-permute-start.8 = (f32[64,1280]{1,0:T(8,128)S(1)}, f32[64,1280]{1,0:T(8,128)S(1)}, u32[]{:S(2)}, u32[]{:S(2)}) collective-permute-start(f32[64,1280]{1,0:T(8,128)S(1)} %slice.34), channel_id=1, source_target_pairs={{0,6},{2,0},{4,2},{6,4},{1,7},{3,1},{5,3},{7,5},{8,14},{10,8},{12,... | collective-permute-start | bytes 983048 | tf_op jit(solution)/shard_map/ppermute | solution.py:387
  277.6 15.3 %copy-start.4 = (f32[128,1280]{1,0:T(8,128)}, f32[128,1280]{1,0:T(8,128)S(1)}, u32[]{:S(2)}) copy-start(f32[128,1280]{1,0:T(8,128)S(1)} %collective-permute-done.5.before_ref) | copy-start | bytes 1966084
  277.7 15.3 %collective-permute-start.7 = (f32[64,1280]{1,0:T(8,128)S(1)}, f32[64,1280]{1,0:T(8,128)S(1)}, u32[]{:S(2)}, u32[]{:S(2)}) collective-permute-start(f32[64,1280]{1,0:T(8,128)S(1)} %slice.33), channel_id=1, source_target_pairs={{0,2},{2,4},{4,6},{6,0},{1,3},{3,5},{5,7},{7,1},{8,10},{10,12},{12... | collective-permute-start | bytes 983048 | tf_op jit(solution)/shard_map/ppermute | solution.py:387
  293.0 0.7 copy-start.8
  293.0 0.9 copy-start.9
Sparse Core Ops, SparseCore 0:
  193.5 75.2 reduce-scatter.2
  293.2 48.0 reduce-scatter.4

commit v4 on v3

--- a/solution.py
+++ b/solution.py
@@ -140,20 +140,35 @@
     )((first_col + start).reshape(1, 1), dest, stair, rows)
 
 
+def stacked_halves(out_ref, *parts):
+    count = out_ref.shape[0] // 2
+    first = 0
+    for x in parts:
+        rows = x.shape[0]
+        high, low = halves(x)
+        out_ref[first : first + rows] = low
+        out_ref[count + first : count + first + rows] = high
+        first += rows
+
+
+def turned_dot(turned, other):
+    count = other.shape[0] // 2
+    return jnp.dot(turned, other, preferred_element_type=jnp.float32) + jnp.dot(
+        turned[:, :count], other[count:], preferred_element_type=jnp.float32
+    )
+
+
 def gram_kernel(turn_ref, own_ref, child_ref, *outs):
-    high_ref, low_ref, packed_ref = outs[5:]
-    own_count = own_ref.shape[0]
-    child = child_ref[:, 0].reshape(-1, ELIMINATED)
-    high_ref[:own_count], low_ref[:own_count] = halves(own_ref[...])
-    high_ref[own_count:], low_ref[own_count:] = halves(child)
-    dims = (((0,), (0,)), ((), ()))
+    turned_ref, both_ref, packed_ref = outs[5:]
+    count = both_ref.shape[0] // 2
+    stacked_halves(both_ref, own_ref[...], child_ref[:, 0].reshape(-1, ELIMINATED))
+    for start in range(0, ELIMINATED, WIDE):
+        cols = slice(start, start + WIDE)
+        turned_ref[cols, :count] = both_ref[count:, cols].T
+        turned_ref[cols, count:] = both_ref[:count, cols].T
     for block, pair, offset in offsets():
         start = WIDE * block
-        left_high, left_low = high_ref[:, start : start + WIDE], low_ref[:, start : start + WIDE]
-        right_high, right_low = high_ref[:, start:], low_ref[:, start:]
-        total = lax.dot_general(left_high, right_high, dims, preferred_element_type=jnp.float32)
-        total += lax.dot_general(left_high, right_low, dims, preferred_element_type=jnp.float32)
-        total += lax.dot_general(left_low, right_high, dims, preferred_element_type=jnp.float32)
+        total = turned_dot(turned_ref[start : start + WIDE, :], both_ref[:, start:])
         for half in range(2):
             packed_ref[2 * pair + half, :, offset : offset + ELIMINATED - start] = total[
                 BLK * half : BLK * (half + 1)
@@ -178,47 +193,41 @@
         grid=(1,),
         out_shape=[jax.ShapeDtypeStruct((BLK, PACKED), jnp.float32)] * 3
         + [jax.ShapeDtypeStruct((BLK // 2, PACKED), jnp.float32)] * 2
-        + [jax.ShapeDtypeStruct((rows, ELIMINATED), jnp.bfloat16)] * 2,
+        + [jax.ShapeDtypeStruct((ELIMINATED, 2 * rows), jnp.bfloat16)],
         in_specs=[
             pl.BlockSpec(memory_space=pltpu.SMEM),
             vmem,
             pl.BlockSpec((fronts, 1, capacity, ELIMINATED), lambda j: (0, 0, 0, 0)),
         ],
-        out_specs=[vmem] * 7,
-        scratch_shapes=[pltpu.VMEM((4, BLK, PACKED), jnp.float32)],
+        out_specs=[vmem] * 6,
+        scratch_shapes=[pltpu.VMEM((2 * rows, ELIMINATED), jnp.bfloat16), pltpu.VMEM((4, BLK, PACKED), jnp.float32)],
         compiler_params=pltpu.CompilerParams(vmem_limit_bytes=VMEM_BYTES),
         cost_estimate=LIGHT,
     )(turn, own_panel, arrived)
 
 
-def cross_kernel(high_ref, low_ref, own_ref, child_ref, out_ref):
-    child = child_ref[:, 0].reshape(-1, WIDE)
-    high, low = halves(jnp.concatenate([own_ref[...], child], axis=0))
-    dims = (((0,), (0,)), ((), ()))
-    total = lax.dot_general(high, high_ref[...], dims, preferred_element_type=jnp.float32)
-    total += lax.dot_general(high, low_ref[...], dims, preferred_element_type=jnp.float32)
-    total += lax.dot_general(low, high_ref[...], dims, preferred_element_type=jnp.float32)
-    out_ref[...] = total
-
-
-def cross(high, low, own, start, child, part):
+def cross_kernel(turned_ref, own_ref, child_ref, out_ref, both_ref):
+    stacked_halves(both_ref, own_ref[...], child_ref[:, 0].reshape(-1, WIDE))
+    out_ref[0] = turned_dot(turned_ref[...], both_ref[...])
+
+
+def cross(turned, own, start, child, part):
     fronts, _, capacity, _ = child.shape
     skipped = start // WIDE
-    vmem = pl.BlockSpec(memory_space=pltpu.VMEM)
     return pl.pallas_call(
         cross_kernel,
         grid=(ELIMINATED // WIDE,),
-        out_shape=jax.ShapeDtypeStruct((ELIMINATED, ELIMINATED), jnp.float32),
+        out_shape=jax.ShapeDtypeStruct((ELIMINATED // WIDE, ELIMINATED, WIDE), jnp.float32),
         in_specs=[
-            vmem,
-            vmem,
+            pl.BlockSpec(memory_space=pltpu.VMEM),
             pl.BlockSpec((own.shape[0], WIDE), lambda j: (0, skipped + j)),
             pl.BlockSpec((fronts, 1, capacity, WIDE), lambda j: (0, part, 0, j)),
         ],
-        out_specs=pl.BlockSpec((WIDE, ELIMINATED), lambda j: (j, 0)),
-        compiler_params=pltpu.CompilerParams(vmem_limit_bytes=VMEM_BYTES),
-        cost_estimate=LIGHT,
-    )(high, low, own, child)
+        out_specs=pl.BlockSpec((1, ELIMINATED, WIDE), lambda j: (j, 0, 0)),
+        scratch_shapes=[pltpu.VMEM((turned.shape[1], WIDE), jnp.bfloat16)],
+        compiler_params=pltpu.CompilerParams(vmem_limit_bytes=VMEM_BYTES),
+        cost_estimate=LIGHT,
+    )(turned, own, child)
 
 
 def sharp_dot(a, b, dims):
@@ -337,19 +346,19 @@
 def solve_kernel(high_ref, low_ref, first_ref, second_ref, out_ref):
     parts, quarter, _ = out_ref.shape
     for j, sums_ref in enumerate((first_ref, second_ref)):
-        sums = halves(sums_ref[...])
+        sums = halves(sums_ref[0])
         for i in range(parts):
             rows, depth = slice(quarter * i, quarter * (i + 1)), quarter * (i + 1)
             out_ref[i, :, quarter * j : quarter * (j + 1)] = sharp_dot(
                 (high_ref[rows, :depth], low_ref[rows, :depth]),
-                tuple(x[:, :depth] for x in sums),
-                ((1,), (1,)),
+                tuple(x[:depth] for x in sums),
+                PLAIN,
             )
 
 
 def solve(high, low, first, second):
     vmem = pl.BlockSpec(memory_space=pltpu.VMEM)
-    quarter = first.shape[0]
+    quarter = first.shape[2]
     return pl.pallas_call(
         solve_kernel,
         out_shape=jax.ShapeDtypeStruct((ELIMINATED // quarter, quarter, 2 * quarter), jnp.float32),
@@ -397,7 +406,9 @@
     quarter = ELIMINATED // row_count
     own = own_rows[0]
     own_a = own[:, :ELIMINATED]
-    passed = lax.ppermute(own_a, "col", [(0, 1)])
+    split = own_a.shape[0] // 2
+    passed = lax.ppermute(own_a[:split], "col", [(0, 1)])
+    passed_rest = lax.ppermute(own_a[split:], "col", [(0, 1)])
 
     first_col = col_index * half_cols
     dest, stair = child_dest.reshape(1, source_rows), child_stair.reshape(source_rows, 1)
@@ -414,11 +425,11 @@
     child_b = lax.all_to_all(
         single.reshape(n_front * capacity, ELIMINATED), "front", split_axis=0, concat_axis=0, tiled=True
     ).reshape(n_front, 1, capacity, ELIMINATED)
-    own_panel = jnp.where(col_index == 0, own_a, passed)
+    own_panel = jnp.where(col_index == 0, own_a, jnp.concatenate([passed, passed_rest], axis=0))
 
     turn = row_index.reshape(1, 1)
-    mine, right, left, right_rest, left_rest, high, low = packed_gram(turn, own_panel, arrived)
-    products_a = cross(high, low, own, 0, arrived, 1)
+    mine, right, left, right_rest, left_rest, turned = packed_gram(turn, own_panel, arrived)
+    products_a = cross(turned, own, 0, arrived, 1)
     mine, right, left, products_a = lax.optimization_barrier((mine, right, left, products_a))
     middle = BLK // 2
     from_left, from_right = shifted(right, 1, row_count), shifted(left, -1, row_count)
@@ -434,7 +445,7 @@
     def summed(products):
         return lax.psum_scatter(products, "row", scatter_dimension=0, tiled=True)
 
-    products_b = cross(high, low, own, ELIMINATED, child_b, 0)
+    products_b = cross(turned, own, ELIMINATED, child_b, 0)
     pieces, products_b = lax.optimization_barrier((pieces, products_b))
     inverse_high, inverse_low, leading = factor(turn, *pieces)
     rows = solve(inverse_high, inverse_low, summed(products_a), summed(products_b))

time: 390 us -> 385 us (0.987)
  waiting for transfers between devices: 189 us -> 175 us
  starting transfers between devices: 36.6 us -> 44.9 us
    all_to_all x1, waiting for transfers between devices: 110 us -> 0.01 us  [body(): lax.all_to_all(doubled.reshape(2 * n_front * capacity, ELIMINATED), ('fro...]
    ppermute x1 -> x2, waiting for transfers between devices: 18.6 us -> 114 us  [the longest x1 113 us: body(): passed_rest = lax.ppermute(own_a[split:], 'col', [(0, 1)])]
    ppermute x1 -> x2, starting transfers between devices: 4 us -> 8.51 us  [the longest x1 4.56 us: body(): passed_rest = lax.ppermute(own_a[split:], 'col', [(0, 1)])]
  transfers between devices with their start and end apart: 13 -> 14, of which waited for: 6 -> 6; matrix products, arithmetic and copies ran while one was open for 1% -> 1% of each run, Pallas kernels for 20% -> 20%
where the time goes in v4:
time: 385 us; the launch traced here: 384 us
  waiting for transfers between devices  175 us (45%)
  Pallas kernels  112 us (29%)
  starting transfers between devices  44.9 us (12%)
  blocking collectives  30.1 us (8%)
  between operations  13.6 us (4%)
  local copies, waits for them, and re-layouts  6.07 us (2%)
    ppermute x1, waiting for transfers between devices, body(): passed_rest = lax.ppermute(own_a[split:], 'col', [(0, 1)])  113 us
    ppermute x8, waiting for transfers between devices, shifted(): lax.ppermute(x, 'row', [(i, (i + shift) % count) for i in range(count)])  60.2 us
    pallas_call x1, Pallas kernels, factor(): pl.pallas_call(factor_kernel, out_shape=(jax.ShapeDtypeStruct((ELIMINATED...  49.1 us
    all_to_all x1, blocking collectives, body(): rows = lax.all_to_all(rows, 'row', split_axis=0, concat_axis=0, tiled=True)  30.1 us
    pallas_call x2, Pallas kernels, cross(): pl.pallas_call(cross_kernel, grid=(ELIMINATED // WIDE,), out_shape=jax.Sh...  28.2 us
    ppermute x8, starting transfers between devices, shifted(): lax.ppermute(x, 'row', [(i, (i + shift) % count) for i in range(count)])  15.2 us
    pallas_call x2, Pallas kernels, place(): pl.pallas_call(place_kernel, grid=(ELIMINATED // WIDE,), out_shape=jax.Sh...  14.1 us
    all_to_all x1, starting transfers between devices, body(): lax.all_to_all(single.reshape(n_front * capacity, ELIMINATED), 'front', s...  11.8 us
  transfers between devices with their start and end apart: 14, of which 6 were waited for; matrix products, arithmetic and copies ran while one was open for 1% of the time, Pallas kernels for 20%

profile of v4, /device:TPU:0, one launch (start us, length us, event | category | flops | bytes accessed | tf_op | source)
XLA Modules:
  0.0 384.3 jit_solution(14866016163592297338)
XLA Ops:
  6.5 2.4 fusion
  8.9 3.9 %collective-permute-start = (f32[192,1024]{1,0:T(8,128)S(1)}, f32[192,1024]{1,0:T(8,128)S(1)}, u32[]{:S(2)}, u32[]{:S(2)}) collective-permute-start(f32[192,1024]{1,0:T(8,128)S(1)} %get-tuple-element.49), channel_id=1, source_target_pairs={{0,1},{2,3},{4,5},{6,7},{8,9},{10,11},{12,13},{14,15},{16,17},{18,... | collective-permute-start | bytes 2359304 | tf_op jit(solution)/shard_map/ppermute | solution.py:410
  12.9 0.9 copy.5.stair_ref
  13.8 6.7 %shard_map.47 = f32[16,1,64,1024]{3,2,1,0:T(8,128)} custom-call(s32[1,1]{1,0:T(1,128)} %bitcast.6.first_ref, s32[1,512]{1,0:T(1,128)} %bitcast.17, s32[512,1]{1,0:T(8,128)} %copy.5.stair_ref, f32[512,2048]{1,0:T(8,128)} %rows_ref.3), custom_call_target="tpu_custom_call" | custom-call | flops 1 | bytes 1 | tf_op jit(solution)/shard_map/pallas_call | solution.py:126
  20.4 7.4 %shard_map.46 = f32[16,2,64,1024]{3,2,1,0:T(8,128)} custom-call(s32[1,1]{1,0:T(1,128)} %bitcast.3.first_ref, s32[1,512]{1,0:T(1,128)} %bitcast.18, s32[512,1]{1,0:T(8,128)} %copy.5.stair_ref, f32[512,2048]{1,0:T(8,128)} %rows_ref.3), custom_call_target="tpu_custom_call" | custom-call | flops 1 | bytes 1 | tf_op jit(solution)/shard_map/pallas_call | solution.py:126
  27.8 1.8 collective-permute-done
  29.6 0.9 copy-done.4
  30.5 9.3 %all-to-all-start = ((f32[32,64,1024]{2,1,0:T(8,128)}), f32[32,64,1024]{2,1,0:T(8,128)}, u32[]{:S(2)}, u32[]{:S(2)}) async-start(f32[32,64,1024]{2,1,0:T(8,128)} %bitcast.11), calls=%async_computation | async-start | bytes 16777216 | tf_op jit(solution)/shard_map/all_to_all | solution.py:418
  39.9 4.6 %collective-permute-start.1 = (f32[192,1024]{1,0:T(8,128)}, f32[192,1024]{1,0:T(8,128)}, u32[]{:S(2)}, u32[]{:S(2)}) collective-permute-start(f32[192,1024]{1,0:T(8,128)} %get-tuple-element.50), channel_id=1, source_target_pairs={{0,1},{2,3},{4,5},{6,7},{8,9},{10,11},{12,13},{14,15},{16,17},{18,... | collective-permute-start | bytes 2359304 | tf_op jit(solution)/shard_map/ppermute | solution.py:411
  44.4 112.5 %collective-permute-done.1 = f32[192,1024]{1,0:T(8,128)} collective-permute-done((f32[192,1024]{1,0:T(8,128)}, f32[192,1024]{1,0:T(8,128)}, u32[]{:S(2)}, u32[]{:S(2)}) %collective-permute-start.1) | collective-permute-done | bytes 786464 | tf_op jit(solution)/shard_map/ppermute | solution.py:411
  157.0 2.8 slice_select_fusion.own_ref
  159.8 10.9 %shard_map.48 = (f32[128,1280]{1,0:T(8,128)}, f32[128,1280]{1,0:T(8,128)}, f32[128,1280]{1,0:T(8,128)}, f32[64,1280]{1,0:T(8,128)}, f32[64,1280]{1,0:T(8,128)}, /*index=5*/bf16[1024,2816]{1,0:T(8,128)(2,1)}) custom-call(s32[1,1]{1,0:T(1,128)} %bitcast.1.turn_ref, f32[384,1024]{1,0:T(8,128)} %slice_select_fusion.own_ref, f32[16,2,64,1024]{3,2,1,0:T(8,128)} %bitcast.8.child_ref), custom_call_target="tpu_custom_call" | custom-call | flops 1 | bytes 1 | tf_op jit(solution)/shard_map/pallas_call | solution.py:191
  170.6 14.1 %shard_map.49 = f32[4,1024,256]{2,1,0:T(8,128)} custom-call(bf16[1024,2816]{1,0:T(8,128)(2,1)} %get-tuple-element.32.turned_ref, f32[384,2048]{1,0:T(8,128)} %bitcast.13, f32[16,2,64,1024]{3,2,1,0:T(8,128)} %bitcast.8.child_ref), custom_call_target="tpu_custom_call" | custom-call | flops 1 | bytes 1 | tf_op jit(solution)/shard_map/pallas_call | solution.py:217
  184.8 1.1 copy-done.12
  185.8 1.5 collective-permute-start.2
  187.3 11.8 %all-to-all-start.1 = ((f32[16,64,1024]{2,1,0:T(8,128)}), f32[16,64,1024]{2,1,0:T(8,128)}, u32[]{:S(2)}, u32[]{:S(2)}) async-start(f32[16,64,1024]{2,1,0:T(8,128)} %bitcast.16), calls=%async_computation.1 | async-start | bytes 8388608 | tf_op jit(solution)/shard_map/all_to_all | solution.py:425
  199.2 2.0 collective-permute-start.4
  201.2 2.3 collective-permute-done.2
  203.6 2.4 collective-permute-start.3
  206.0 24.5 %collective-permute-done.4 = f32[128,1280]{1,0:T(8,128)S(1)} collective-permute-done((f32[128,1280]{1,0:T(8,128)S(1)}, f32[128,1280]{1,0:T(8,128)S(1)}, u32[]{:S(2)}, u32[]{:S(2)}) %collective-permute-start.4) | collective-permute-done | bytes 655392 | tf_op jit(solution)/shard_map/ppermute | solution.py:396
  230.6 3.3 collective-permute-start.5
  233.9 14.8 %collective-permute-done.5 = f32[64,1280]{1,0:T(8,128)S(1)} collective-permute-done((f32[64,1280]{1,0:T(8,128)S(1)}, f32[64,1280]{1,0:T(8,128)S(1)}, u32[]{:S(2)}, u32[]{:S(2)}) %collective-permute-start.5) | collective-permute-done | bytes 327712 | tf_op jit(solution)/shard_map/ppermute | solution.py:396
  248.8 3.8 collective-permute-start.7
  252.6 18.6 %collective-permute-done.7.after_ref = f32[128,1280]{1,0:T(8,128)S(1)} collective-permute-done((f32[128,1280]{1,0:T(8,128)S(1)}, f32[128,1280]{1,0:T(8,128)S(1)}, u32[]{:S(2)}, u32[]{:S(2)}) %collective-permute-start.7) | collective-permute-done | bytes 655392 | tf_op jit(solution)/shard_map/ppermute | solution.py:396
  271.3 1.6 collective-permute-start.9
  272.9 0.6 collective-permute-start.8
  273.5 14.1 %shard_map.50 = f32[4,1024,256]{2,1,0:T(8,128)} custom-call(bf16[1024,2816]{1,0:T(8,128)(2,1)} %get-tuple-element.32.turned_ref, f32[384,2048]{1,0:T(8,128)} %bitcast.14, f32[16,1,64,1024]{3,2,1,0:T(8,128)} %bitcast.10.child_ref), custom_call_target="tpu_custom_call" | custom-call | flops 1 | bytes 1 | tf_op jit(solution)/shard_map/pallas_call | solution.py:217
  287.6 0.7 copy-done.8
  288.4 49.1 %shard_map.51 = (bf16[1024,1024]{1,0:T(8,128)(2,1)}, bf16[1024,1024]{1,0:T(8,128)(2,1)}, f32[256,1024]{1,0:T(8,128)}) custom-call(s32[1,1]{1,0:T(1,128)} %bitcast.1.turn_ref, f32[128,1280]{1,0:T(8,128)} %copy-done.1, f32[128,1280]{1,0:T(8,128)} %copy-done.3, f32[128,1280]{1,0:T(8,128)} %copy-done.2, f32[64,1280]{1,0:T(8,128)} %copy-done.9, f32[64,1280]{1,0:T(8,128)} %copy-done.8), custom_call_target="tpu_custom_call" | custom-call | flops 1 | bytes 1 | tf_op jit(solution)/shard_map/pallas_call | solution.py:325
  337.5 6.4 %shard_map.52 = f32[4,256,512]{2,1,0:T(8,128)} custom-call(bf16[1024,1024]{1,0:T(8,128)(2,1)} %get-tuple-element.45.high_ref, bf16[1024,1024]{1,0:T(8,128)(2,1)} %get-tuple-element.46.low_ref, f32[1,1024,256]{2,1,0:T(8,128)} %reduce-scatter.3.cloned.1.call-done.first_ref, f32[1,1024,256]{2,1,0:T(8,128)} %reduce-scatter.5.cloned.1.call-done.second_ref), custom_call_target="tpu_custom_call" | custom-call | flops 1 | bytes 1 | tf_op jit(solution)/shard_map/pallas_call | solution.py:362
  343.9 30.1 %all_to_all.23.rows_ref = f32[4,256,512]{2,1,0:T(8,128)} all-to-all(f32[4,256,512]{2,1,0:T(8,128)} %shard_map.52), channel_id=1, replica_groups=mesh['front'=16,'row'=4,'col'=2] {'row'}, dimensions={0} | all-to-all | bytes 4194304 | tf_op jit(solution)/shard_map/all_to_all | solution.py:452
  374.0 3.5 shard_map.53
  (42 shorter events, 0.5 us)
Async XLA Ops:
  6.5 6.4 %copy-start.10 = (s32[512]{0:T(512)S(1)}, s32[512]{0:T(512)}, u32[]{:S(2)}) copy-start(s32[512]{0:T(512)} %param.7) | copy-start | bytes 6148
  8.9 20.7 %collective-permute-start = (f32[192,1024]{1,0:T(8,128)S(1)}, f32[192,1024]{1,0:T(8,128)S(1)}, u32[]{:S(2)}, u32[]{:S(2)}) collective-permute-start(f32[192,1024]{1,0:T(8,128)S(1)} %get-tuple-element.49), channel_id=1, source_target_pairs={{0,1},{2,3},{4,5},{6,7},{8,9},{10,11},{12,13},{14,15},{16,17},{18,... | collective-permute-start | bytes 2359304 | tf_op jit(solution)/shard_map/ppermute | solution.py:410
  29.6 0.9 copy-start.4
  30.5 126.5 %copy-start = (f32[1,384,2048]{2,1,0:T(8,128)S(1)}, f32[1,384,2048]{2,1,0:T(8,128)}, u32[]{:S(2)}) copy-start(f32[1,384,2048]{2,1,0:T(8,128)} %param.4) | copy-start | bytes 9437188
  30.5 129.2 %all-to-all-start = ((f32[32,64,1024]{2,1,0:T(8,128)}), f32[32,64,1024]{2,1,0:T(8,128)}, u32[]{:S(2)}, u32[]{:S(2)}) async-start(f32[32,64,1024]{2,1,0:T(8,128)} %bitcast.11), calls=%async_computation | async-start | bytes 16777216 | tf_op jit(solution)/shard_map/all_to_all | solution.py:418
  39.8 297.7 %reduce-scatter.3.cloned.1.call-start = ((), (), s32[]{:S(2)}) async-start(), calls=%async_computation.5 | async-start | bytes 5242880 | tf_op jit(solution)/shard_map/reduce_scatter | solution.py:446
  39.9 117.1 %collective-permute-start.1 = (f32[192,1024]{1,0:T(8,128)}, f32[192,1024]{1,0:T(8,128)}, u32[]{:S(2)}, u32[]{:S(2)}) collective-permute-start(f32[192,1024]{1,0:T(8,128)} %get-tuple-element.50), channel_id=1, source_target_pairs={{0,1},{2,3},{4,5},{6,7},{8,9},{10,11},{12,13},{14,15},{16,17},{18,... | collective-permute-start | bytes 2359304 | tf_op jit(solution)/shard_map/ppermute | solution.py:411
  184.7 1.1 copy-start.12
  185.8 17.7 %collective-permute-start.2 = (f32[128,1280]{1,0:T(8,128)S(1)}, f32[128,1280]{1,0:T(8,128)S(1)}, u32[]{:S(2)}, u32[]{:S(2)}) collective-permute-start(f32[128,1280]{1,0:T(8,128)S(1)} %copy-done.12), channel_id=1, source_target_pairs={{0,2},{2,4},{4,6},{6,0},{1,3},{3,5},{5,7},{7,1},{8,10},{10,12},{12... | collective-permute-start | bytes 1966088 | tf_op jit(solution)/shard_map/ppermute | solution.py:396
  187.3 11.9 %copy-start.11 = (f32[128,1280]{1,0:T(8,128)S(1)}, f32[128,1280]{1,0:T(8,128)}, u32[]{:S(2)}) copy-start(f32[128,1280]{1,0:T(8,128)} %get-tuple-element.36) | copy-start | bytes 1966084
  187.3 16.2 %copy-start.6 = (f32[64,1280]{1,0:T(8,128)S(1)}, f32[64,1280]{1,0:T(8,128)}, u32[]{:S(2)}) copy-start(f32[64,1280]{1,0:T(8,128)} %get-tuple-element.34) | copy-start | bytes 983044
  187.3 43.2 %copy-start.7 = (f32[64,1280]{1,0:T(8,128)S(1)}, f32[64,1280]{1,0:T(8,128)}, u32[]{:S(2)}) copy-start(f32[64,1280]{1,0:T(8,128)} %get-tuple-element.37) | copy-start | bytes 983044
  187.3 86.1 %all-to-all-start.1 = ((f32[16,64,1024]{2,1,0:T(8,128)}), f32[16,64,1024]{2,1,0:T(8,128)}, u32[]{:S(2)}, u32[]{:S(2)}) async-start(f32[16,64,1024]{2,1,0:T(8,128)} %bitcast.16), calls=%async_computation.1 | async-start | bytes 8388608 | tf_op jit(solution)/shard_map/all_to_all | solution.py:425
  199.2 49.6 %copy-start.5 = (f32[128,1280]{1,0:T(8,128)S(1)}, f32[128,1280]{1,0:T(8,128)}, u32[]{:S(2)}) copy-start(f32[128,1280]{1,0:T(8,128)} %get-tuple-element.33) | copy-start | bytes 1966084
  199.2 138.4 %reduce-scatter.5.cloned.1.call-start = ((), (), s32[]{:S(2)}) async-start(), calls=%async_computation.6 | async-start | bytes 5242880 | tf_op jit(solution)/shard_map/reduce_scatter | solution.py:446
  199.2 31.3 %collective-permute-start.4 = (f32[128,1280]{1,0:T(8,128)S(1)}, f32[128,1280]{1,0:T(8,128)S(1)}, u32[]{:S(2)}, u32[]{:S(2)}) collective-permute-start(f32[128,1280]{1,0:T(8,128)S(1)} %copy-done.11), channel_id=1, source_target_pairs={{0,6},{2,0},{4,2},{6,4},{1,7},{3,1},{5,3},{7,5},{8,14},{10,8},{12,... | collective-permute-start | bytes 1966088 | tf_op jit(solution)/shard_map/ppermute | solution.py:396
  203.6 26.9 %collective-permute-start.3 = (f32[64,1280]{1,0:T(8,128)S(1)}, f32[64,1280]{1,0:T(8,128)S(1)}, u32[]{:S(2)}, u32[]{:S(2)}) collective-permute-start(f32[64,1280]{1,0:T(8,128)S(1)} %slice_add_fusion.3), channel_id=1, source_target_pairs={{0,2},{2,4},{4,6},{6,0},{1,3},{3,5},{5,7},{7,1},{8,10},{10,12},{12... | collective-permute-start | bytes 983048 | tf_op jit(solution)/shard_map/ppermute | solution.py:396
  230.6 18.1 %collective-permute-start.5 = (f32[64,1280]{1,0:T(8,128)S(1)}, f32[64,1280]{1,0:T(8,128)S(1)}, u32[]{:S(2)}, u32[]{:S(2)}) collective-permute-start(f32[64,1280]{1,0:T(8,128)S(1)} %get-tuple-element.52), channel_id=1, source_target_pairs={{0,6},{2,0},{4,2},{6,4},{1,7},{3,1},{5,3},{7,5},{8,14},{10,8},{12,... | collective-permute-start | bytes 983048 | tf_op jit(solution)/shard_map/ppermute | solution.py:396
  248.8 38.7 %copy-start.1 = (f32[128,1280]{1,0:T(8,128)}, f32[128,1280]{1,0:T(8,128)S(1)}, u32[]{:S(2)}) copy-start(f32[128,1280]{1,0:T(8,128)S(1)} %maximum_add_fusion.piece_ref) | copy-start | bytes 1966084
  248.8 22.4 %collective-permute-start.7 = (f32[128,1280]{1,0:T(8,128)S(1)}, f32[128,1280]{1,0:T(8,128)S(1)}, u32[]{:S(2)}, u32[]{:S(2)}) collective-permute-start(f32[128,1280]{1,0:T(8,128)S(1)} %maximum_add_fusion.piece_ref), channel_id=1, source_target_pairs={{0,6},{2,0},{4,2},{6,4},{1,7},{3,1},{5,3},{7,5},{8,14},{10,8},{12,... | collective-permute-start | bytes 1966088 | tf_op jit(solution)/shard_map/ppermute | solution.py:396
  252.6 20.2 %collective-permute-start.6 = (f32[128,1280]{1,0:T(8,128)S(1)}, f32[128,1280]{1,0:T(8,128)S(1)}, u32[]{:S(2)}, u32[]{:S(2)}) collective-permute-start(f32[128,1280]{1,0:T(8,128)S(1)} %maximum_add_fusion.piece_ref), channel_id=1, source_target_pairs={{0,2},{2,4},{4,6},{6,0},{1,3},{3,5},{5,7},{7,1},{8,10},{10,12},{12... | collective-permute-start | bytes 1966088 | tf_op jit(solution)/shard_map/ppermute | solution.py:396
  271.2 16.3 %copy-start.2 = (f32[128,1280]{1,0:T(8,128)}, f32[128,1280]{1,0:T(8,128)S(1)}, u32[]{:S(2)}) copy-start(f32[128,1280]{1,0:T(8,128)S(1)} %collective-permute-done.7.after_ref) | copy-start | bytes 1966084
  271.3 16.3 %collective-permute-start.9 = (f32[64,1280]{1,0:T(8,128)S(1)}, f32[64,1280]{1,0:T(8,128)S(1)}, u32[]{:S(2)}, u32[]{:S(2)}) collective-permute-start(f32[64,1280]{1,0:T(8,128)S(1)} %slice.46), channel_id=1, source_target_pairs={{0,6},{2,0},{4,2},{6,4},{1,7},{3,1},{5,3},{7,5},{8,14},{10,8},{12,... | collective-permute-start | bytes 983048 | tf_op jit(solution)/shard_map/ppermute | solution.py:396
  272.9 14.7 %copy-start.3 = (f32[128,1280]{1,0:T(8,128)}, f32[128,1280]{1,0:T(8,128)S(1)}, u32[]{:S(2)}) copy-start(f32[128,1280]{1,0:T(8,128)S(1)} %collective-permute-done.6.before_ref) | copy-start | bytes 1966084
  272.9 14.7 %collective-permute-start.8 = (f32[64,1280]{1,0:T(8,128)S(1)}, f32[64,1280]{1,0:T(8,128)S(1)}, u32[]{:S(2)}, u32[]{:S(2)}) collective-permute-start(f32[64,1280]{1,0:T(8,128)S(1)} %slice.45), channel_id=1, source_target_pairs={{0,2},{2,4},{4,6},{6,0},{1,3},{3,5},{5,7},{7,1},{8,10},{10,12},{12... | collective-permute-start | bytes 983048 | tf_op jit(solution)/shard_map/ppermute | solution.py:396
  287.6 0.7 copy-start.8
  287.6 0.8 copy-start.9
Sparse Core Ops, SparseCore 0:
  184.9 79.5 reduce-scatter.2
  287.7 48.0 reduce-scatter.4

commit v5 on v4

--- a/solution.py
+++ b/solution.py
@@ -230,6 +230,35 @@
     )(turned, own, child)
 
 
+def shared_kernel(_, turned_ref, own_ref, child_ref, out_ref, both_ref):
+    stacked_halves(both_ref, own_ref[...], child_ref[:, 0].reshape(-1, WIDE))
+    total = turned_dot(turned_ref[...], both_ref[...])
+    for half in range(2):
+        out_ref[half] = total[:, BLK * half : BLK * (half + 1)]
+
+
+def shared_cross(col, turned, own, child):
+    fronts, _, capacity, _ = child.shape
+    steps = own.shape[1] // WIDE
+    return pl.pallas_call(
+        shared_kernel,
+        grid_spec=pltpu.PrefetchScalarGridSpec(
+            num_scalar_prefetch=1,
+            grid=(steps,),
+            in_specs=[
+                pl.BlockSpec(memory_space=pltpu.VMEM),
+                pl.BlockSpec((own.shape[0], WIDE), lambda j, c: (0, j)),
+                pl.BlockSpec((fronts, 1, capacity, WIDE), lambda j, c: (0, 1, 0, c[0] * steps + j)),
+            ],
+            out_specs=pl.BlockSpec((2, ELIMINATED, BLK), lambda j, c: (j, 0, 0)),
+            scratch_shapes=[pltpu.VMEM((turned.shape[1], WIDE), jnp.bfloat16)],
+        ),
+        out_shape=jax.ShapeDtypeStruct((own.shape[1] // BLK, ELIMINATED, BLK), jnp.float32),
+        compiler_params=pltpu.CompilerParams(vmem_limit_bytes=VMEM_BYTES),
+        cost_estimate=LIGHT,
+    )(col, turned, own, child)
+
+
 def sharp_dot(a, b, dims):
     (high, low), (other_high, other_low) = a, b
     dims = (dims, ((), ()))
@@ -343,53 +372,50 @@
     )(turn, piece, before, after, across, across_rest)
 
 
-def solve_kernel(high_ref, low_ref, first_ref, second_ref, out_ref):
+def solve_kernel(high_ref, low_ref, sums_ref, out_ref):
     parts, quarter, _ = out_ref.shape
-    for j, sums_ref in enumerate((first_ref, second_ref)):
-        sums = halves(sums_ref[0])
-        for i in range(parts):
-            rows, depth = slice(quarter * i, quarter * (i + 1)), quarter * (i + 1)
-            out_ref[i, :, quarter * j : quarter * (j + 1)] = sharp_dot(
-                (high_ref[rows, :depth], low_ref[rows, :depth]),
-                tuple(x[:depth] for x in sums),
-                PLAIN,
+    sums = halves(sums_ref[0])
+    for i in range(parts):
+        rows, depth = slice(quarter * i, quarter * (i + 1)), quarter * (i + 1)
+        out_ref[i] = sharp_dot(
+            (high_ref[rows, :depth], low_ref[rows, :depth]), tuple(x[:depth] for x in sums), PLAIN
+        )
+
+
+def solve(high, low, sums):
+    vmem = pl.BlockSpec(memory_space=pltpu.VMEM)
+    return pl.pallas_call(
+        solve_kernel,
+        out_shape=jax.ShapeDtypeStruct((4, ELIMINATED // 4, sums.shape[2]), jnp.float32),
+        in_specs=[vmem] * 3,
+        out_specs=vmem,
+        compiler_params=pltpu.CompilerParams(vmem_limit_bytes=VMEM_BYTES),
+        cost_estimate=LIGHT,
+    )(high, low, sums)
+
+
+def join_kernel(col_ref, leading_ref, first_ref, second_ref, out_ref):
+    parts, _, width = second_ref.shape
+    for half in range(2):
+        for j in range(parts):
+            cols = slice(ELIMINATED // 2 * half + BLK * j, ELIMINATED // 2 * half + BLK * (j + 1))
+            out_ref[0, :, cols] = jnp.where(
+                col_ref[0, 0] == 0, leading_ref[:, cols], first_ref[j, :, BLK * half : BLK * (half + 1)]
             )
-
-
-def solve(high, low, first, second):
-    vmem = pl.BlockSpec(memory_space=pltpu.VMEM)
-    quarter = first.shape[2]
-    return pl.pallas_call(
-        solve_kernel,
-        out_shape=jax.ShapeDtypeStruct((ELIMINATED // quarter, quarter, 2 * quarter), jnp.float32),
-        in_specs=[vmem] * 4,
-        out_specs=vmem,
-        compiler_params=pltpu.CompilerParams(vmem_limit_bytes=VMEM_BYTES),
-        cost_estimate=LIGHT,
-    )(high, low, first, second)
-
-
-def join_kernel(col_ref, leading_ref, rows_ref, out_ref):
-    parts, _, both = rows_ref.shape
-    width = both // 2
     for j in range(parts):
-        cols = slice(width * j, width * (j + 1))
-        out_ref[0, :, cols] = jnp.where(
-            col_ref[0, 0] == 0, leading_ref[:, cols], rows_ref[j, :, :width]
-        )
-        out_ref[0, :, ELIMINATED + width * j : ELIMINATED + width * (j + 1)] = rows_ref[j, :, width:]
-
-
-def join(col, leading, rows):
+        out_ref[0, :, ELIMINATED + width * j : ELIMINATED + width * (j + 1)] = second_ref[j]
+
+
+def join(col, leading, first, second):
     vmem = pl.BlockSpec(memory_space=pltpu.VMEM)
     return pl.pallas_call(
         join_kernel,
         out_shape=jax.ShapeDtypeStruct((1, leading.shape[0], 2 * ELIMINATED), jnp.float32),
-        in_specs=[pl.BlockSpec(memory_space=pltpu.SMEM)] + [vmem] * 2,
+        in_specs=[pl.BlockSpec(memory_space=pltpu.SMEM)] + [vmem] * 3,
         out_specs=vmem,
         compiler_params=pltpu.CompilerParams(vmem_limit_bytes=VMEM_BYTES),
         cost_estimate=LIGHT,
-    )(col, leading, rows)
+    )(col, leading, first, second)
 
 
 def shifted(x, shift, count):
@@ -406,15 +432,15 @@
     quarter = ELIMINATED // row_count
     own = own_rows[0]
     own_a = own[:, :ELIMINATED]
-    split = own_a.shape[0] // 2
-    passed = lax.ppermute(own_a[:split], "col", [(0, 1)])
-    passed_rest = lax.ppermute(own_a[split:], "col", [(0, 1)])
+    split = own_a.shape[0] // 4
+    passed = lax.ppermute(own_a[:split], "col", [(0, 1), (1, 0)])
+    passed_rest = lax.ppermute(own_a[split:], "col", [(0, 1), (1, 0)])
 
     first_col = col_index * half_cols
     dest, stair = child_dest.reshape(1, source_rows), child_stair.reshape(source_rows, 1)
     doubled = place(first_col, dest, stair, child_rows, 0, 2, n_front, capacity)
     single = place(first_col, dest, stair, child_rows, ELIMINATED, 1, n_front, capacity)
-    doubled, single, passed = lax.optimization_barrier((doubled, single, passed))
+    doubled, passed = lax.optimization_barrier((doubled, passed))
     arrived = lax.all_to_all(
         doubled.reshape(2 * n_front * capacity, ELIMINATED),
         ("front", "col"),
@@ -422,14 +448,19 @@
         concat_axis=0,
         tiled=True,
     ).reshape(n_front, 2, capacity, ELIMINATED)
+    passed = jnp.concatenate([passed, passed_rest], axis=0)
+    own_panel = jnp.where(col_index == 0, own_a, passed)
+    own_shared = jnp.where(
+        col_index == 0, passed[:, : ELIMINATED // 2], own_a[:, ELIMINATED // 2 :]
+    )
+
+    own_panel, single = lax.optimization_barrier((own_panel, single))
     child_b = lax.all_to_all(
         single.reshape(n_front * capacity, ELIMINATED), "front", split_axis=0, concat_axis=0, tiled=True
     ).reshape(n_front, 1, capacity, ELIMINATED)
-    own_panel = jnp.where(col_index == 0, own_a, jnp.concatenate([passed, passed_rest], axis=0))
-
     turn = row_index.reshape(1, 1)
     mine, right, left, right_rest, left_rest, turned = packed_gram(turn, own_panel, arrived)
-    products_a = cross(turned, own, 0, arrived, 1)
+    products_a = shared_cross(col_index.reshape(1), turned, own_shared, arrived)
     mine, right, left, products_a = lax.optimization_barrier((mine, right, left, products_a))
     middle = BLK // 2
     from_left, from_right = shifted(right, 1, row_count), shifted(left, -1, row_count)
@@ -448,9 +479,14 @@
     products_b = cross(turned, own, ELIMINATED, child_b, 0)
     pieces, products_b = lax.optimization_barrier((pieces, products_b))
     inverse_high, inverse_low, leading = factor(turn, *pieces)
-    rows = solve(inverse_high, inverse_low, summed(products_a), summed(products_b))
-    rows = lax.all_to_all(rows, "row", split_axis=0, concat_axis=0, tiled=True)
-    return join(col_index.reshape(1, 1), leading, rows)
+    first = solve(inverse_high, inverse_low, summed(products_a))
+    handed = lax.ppermute(first, "col", [(0, 1)])
+    second = solve(inverse_high, inverse_low, summed(products_b))
+    handed, later = lax.optimization_barrier((handed, second))
+    second = lax.all_to_all(later, "row", split_axis=0, concat_axis=0, tiled=True)
+    first = jnp.concatenate([handed, first], axis=2)
+    first = lax.all_to_all(first, "row", split_axis=0, concat_axis=0, tiled=True)
+    return join(col_index.reshape(1, 1), leading, first, second)
 
 
 def solution(mesh):

time: 385 us -> 376 us (0.977)
  waiting for transfers between devices: 175 us -> 168 us
    pallas_call x2 -> x1, Pallas kernels: 28.2 us -> 14.1 us  [cross(): pl.pallas_call(cross_kernel, grid=(ELIMINATED // WIDE,), out_shape=jax.Sh...]
    ppermute x8, waiting for transfers between devices: 60.2 us -> 48 us  [shifted(): lax.ppermute(x, 'row', [(i, (i + shift) % count) for i in range(count)])]
    pallas_call x1 -> x3, Pallas kernels: 6.35 us -> 18.2 us  [the longest x1 9.13 us: shared_cross(): pl.pallas_call(shared_kernel, grid_spec=pltpu.PrefetchScalarGridSpec(num_...]
    ppermute x2 -> x3, waiting for transfers between devices: 114 us -> 120 us  [the longest x1 116 us: body(): passed_rest = lax.ppermute(own_a[split:], 'col', [(0, 1), (1, 0)])]
    ppermute x2 -> x3, starting transfers between devices: 8.51 us -> 7.56 us  [the longest x1 3.77 us: body(): handed = lax.ppermute(first, 'col', [(0, 1)])]
    all_to_all x1 -> x2, blocking collectives: 30.1 us -> 29.9 us  [the longest x1 15.9 us: body(): lax.all_to_all(first, 'row', split_axis=0, concat_axis=0, tiled=True)]
  transfers between devices with their start and end apart: 14 -> 15, of which waited for: 6 -> 7; matrix products, arithmetic and copies ran while one was open for 1% -> 2% of each run, Pallas kernels for 20% -> 23%
where the time goes in v5:
time: 376 us; the launch traced here: 372 us
  waiting for transfers between devices  168 us (45%)
  Pallas kernels  110 us (29%)
  starting transfers between devices  41.8 us (11%)
  blocking collectives  29.9 us (8%)
  between operations  13.6 us (4%)
  local copies, waits for them, and re-layouts  5.88 us (2%)
    ppermute x1, waiting for transfers between devices, body(): passed_rest = lax.ppermute(own_a[split:], 'col', [(0, 1), (1, 0)])  116 us
    pallas_call x1, Pallas kernels, factor(): pl.pallas_call(factor_kernel, out_shape=(jax.ShapeDtypeStruct((ELIMINATED...  49.2 us
    ppermute x8, waiting for transfers between devices, shifted(): lax.ppermute(x, 'row', [(i, (i + shift) % count) for i in range(count)])  48 us
    all_to_all x1, blocking collectives, body(): lax.all_to_all(first, 'row', split_axis=0, concat_axis=0, tiled=True)  15.9 us
    pallas_call x1, Pallas kernels, cross(): pl.pallas_call(cross_kernel, grid=(ELIMINATED // WIDE,), out_shape=jax.Sh...  14.1 us
    pallas_call x2, Pallas kernels, place(): pl.pallas_call(place_kernel, grid=(ELIMINATED // WIDE,), out_shape=jax.Sh...  14.1 us
    all_to_all x1, blocking collectives, body(): lax.all_to_all(later, 'row', split_axis=0, concat_axis=0, tiled=True)  14 us
    ppermute x8, starting transfers between devices, shifted(): lax.ppermute(x, 'row', [(i, (i + shift) % count) for i in range(count)])  13.8 us
  transfers between devices with their start and end apart: 15, of which 7 were waited for; matrix products, arithmetic and copies ran while one was open for 2% of the time, Pallas kernels for 23%

profile of v5, /device:TPU:0, one launch (start us, length us, event | category | flops | bytes accessed | tf_op | source)
XLA Modules:
  0.0 372.3 jit_solution(18433500739140122204)
XLA Ops:
  7.6 2.1 collective-permute-start
  9.6 1.5 copy.5.stair_ref
  11.2 7.4 %shard_map.46 = f32[16,2,64,1024]{3,2,1,0:T(8,128)} custom-call(s32[1,1]{1,0:T(1,128)} %bitcast.3.first_ref, s32[1,512]{1,0:T(1,128)} %bitcast.19, s32[512,1]{1,0:T(8,128)} %copy.5.stair_ref, f32[512,2048]{1,0:T(8,128)} %rows_ref.3), custom_call_target="tpu_custom_call" | custom-call | flops 1 | bytes 1 | tf_op jit(solution)/shard_map/pallas_call | solution.py:126
  18.8 8.6 %all-to-all-start = ((f32[32,64,1024]{2,1,0:T(8,128)}), f32[32,64,1024]{2,1,0:T(8,128)}, u32[]{:S(2)}, u32[]{:S(2)}) async-start(f32[32,64,1024]{2,1,0:T(8,128)} %bitcast.12), calls=%async_computation | async-start | bytes 16777216 | tf_op jit(solution)/shard_map/all_to_all | solution.py:444
  27.4 1.1 slice.49
  28.5 1.7 collective-permute-start.1
  30.2 6.7 %shard_map.47 = f32[16,1,64,1024]{3,2,1,0:T(8,128)} custom-call(s32[1,1]{1,0:T(1,128)} %bitcast.6.first_ref, s32[1,512]{1,0:T(1,128)} %bitcast.20, s32[512,1]{1,0:T(8,128)} %copy.5.stair_ref, f32[512,2048]{1,0:T(8,128)} %rows_ref.3), custom_call_target="tpu_custom_call" | custom-call | flops 1 | bytes 1 | tf_op jit(solution)/shard_map/pallas_call | solution.py:126
  36.9 116.0 %collective-permute-done.1 = f32[288,1024]{1,0:T(8,128)} collective-permute-done((f32[288,1024]{1,0:T(8,128)}, f32[288,1024]{1,0:T(8,128)}, u32[]{:S(2)}, u32[]{:S(2)}) %collective-permute-start.1) | collective-permute-done | bytes 1179680 | tf_op jit(solution)/shard_map/ppermute | solution.py:437
  152.9 1.3 constant_dynamic-update-slice_fusion
  154.3 1.4 slice_select_fusion.own_ref
  155.7 1.0 slice_select_fusion.1.own_ref
  156.7 11.0 %shard_map.48 = (f32[128,1280]{1,0:T(8,128)}, f32[128,1280]{1,0:T(8,128)}, f32[128,1280]{1,0:T(8,128)}, f32[64,1280]{1,0:T(8,128)}, f32[64,1280]{1,0:T(8,128)}, /*index=5*/bf16[1024,2816]{1,0:T(8,128)(2,1)}) custom-call(s32[1,1]{1,0:T(1,128)} %bitcast.1.turn_ref, f32[384,1024]{1,0:T(8,128)} %slice_select_fusion.own_ref, f32[16,2,64,1024]{3,2,1,0:T(8,128)} %bitcast.8.child_ref), custom_call_target="tpu_custom_call" | custom-call | flops 1 | bytes 1 | tf_op jit(solution)/shard_map/pallas_call | solution.py:191
  167.7 9.1 %shard_map.49 = f32[4,1024,128]{2,1,0:T(8,128)} custom-call(s32[1]{0:T(128)} %bitcast.9._, bf16[1024,2816]{1,0:T(8,128)(2,1)} %get-tuple-element.36.turned_ref, f32[384,512]{1,0:T(8,128)} %slice_select_fusion.1.own_ref, f32[16,2,64,1024]{3,2,1,0:T(8,128)} %bitcast.8.child_ref), custom_call_target="tpu_custom_call" | custom-call | flops 1 | bytes 1 | tf_op jit(solution)/shard_map/pallas_call | solution.py:243
  176.8 1.5 collective-permute-start.2
  178.4 11.9 %all-to-all-start.1 = ((f32[16,64,1024]{2,1,0:T(8,128)}), f32[16,64,1024]{2,1,0:T(8,128)}, u32[]{:S(2)}, u32[]{:S(2)}) async-start(f32[16,64,1024]{2,1,0:T(8,128)} %bitcast.13), calls=%async_computation.1 | async-start | bytes 8388608 | tf_op jit(solution)/shard_map/all_to_all | solution.py:458
  190.3 1.8 collective-permute-start.4
  192.1 2.4 collective-permute-done.2
  194.9 25.3 %collective-permute-done.4 = f32[128,1280]{1,0:T(8,128)S(1)} collective-permute-done((f32[128,1280]{1,0:T(8,128)S(1)}, f32[128,1280]{1,0:T(8,128)S(1)}, u32[]{:S(2)}, u32[]{:S(2)}) %collective-permute-start.4) | collective-permute-done | bytes 655392 | tf_op jit(solution)/shard_map/ppermute | solution.py:422
  220.3 3.8 %collective-permute-start.5 = (f32[64,1280]{1,0:T(8,128)S(1)}, f32[64,1280]{1,0:T(8,128)S(1)}, u32[]{:S(2)}, u32[]{:S(2)}) collective-permute-start(f32[64,1280]{1,0:T(8,128)S(1)} %get-tuple-element.56), channel_id=1, source_target_pairs={{0,6},{2,0},{4,2},{6,4},{1,7},{3,1},{5,3},{7,5},{8,14},{10,8},{12,... | collective-permute-start | bytes 983048 | tf_op jit(solution)/shard_map/ppermute | solution.py:422
  224.1 7.1 %collective-permute-done.5 = f32[64,1280]{1,0:T(8,128)S(1)} collective-permute-done((f32[64,1280]{1,0:T(8,128)S(1)}, f32[64,1280]{1,0:T(8,128)S(1)}, u32[]{:S(2)}, u32[]{:S(2)}) %collective-permute-start.5) | collective-permute-done | bytes 327712 | tf_op jit(solution)/shard_map/ppermute | solution.py:422
  231.4 3.0 collective-permute-start.7
  234.4 13.1 %collective-permute-done.7.after_ref = f32[128,1280]{1,0:T(8,128)S(1)} collective-permute-done((f32[128,1280]{1,0:T(8,128)S(1)}, f32[128,1280]{1,0:T(8,128)S(1)}, u32[]{:S(2)}, u32[]{:S(2)}) %collective-permute-start.7) | collective-permute-done | bytes 655392 | tf_op jit(solution)/shard_map/ppermute | solution.py:422
  247.5 3.3 collective-permute-start.9
  250.9 14.1 %shard_map.50 = f32[4,1024,256]{2,1,0:T(8,128)} custom-call(bf16[1024,2816]{1,0:T(8,128)(2,1)} %get-tuple-element.36.turned_ref, f32[384,2048]{1,0:T(8,128)} %bitcast.15, f32[16,1,64,1024]{3,2,1,0:T(8,128)} %bitcast.11.child_ref), custom_call_target="tpu_custom_call" | custom-call | flops 1 | bytes 1 | tf_op jit(solution)/shard_map/pallas_call | solution.py:217
  265.9 49.2 %shard_map.51 = (bf16[1024,1024]{1,0:T(8,128)(2,1)}, bf16[1024,1024]{1,0:T(8,128)(2,1)}, f32[256,1024]{1,0:T(8,128)}) custom-call(s32[1,1]{1,0:T(1,128)} %bitcast.1.turn_ref, f32[128,1280]{1,0:T(8,128)} %copy-done.2, f32[128,1280]{1,0:T(8,128)} %copy-done.5, f32[128,1280]{1,0:T(8,128)} %copy-done.4, f32[64,1280]{1,0:T(8,128)} %copy-done.10, f32[64,1280]{1,0:T(8,128)} %copy-done.9), custom_call_target="tpu_custom_call" | custom-call | flops 1 | bytes 1 | tf_op jit(solution)/shard_map/pallas_call | solution.py:354
  315.0 4.4 %shard_map.52 = f32[4,256,128]{2,1,0:T(8,128)} custom-call(bf16[1024,1024]{1,0:T(8,128)(2,1)} %get-tuple-element.49.high_ref, bf16[1024,1024]{1,0:T(8,128)(2,1)} %get-tuple-element.50.low_ref, f32[1,1024,128]{2,1,0:T(8,128)} %reduce-scatter.3.cloned.1.call-done.sums_ref), custom_call_target="tpu_custom_call" | custom-call | flops 1 | bytes 1 | tf_op jit(solution)/shard_map/pallas_call | solution.py:387
  319.5 3.8 %collective-permute-start.10 = (f32[4,256,128]{2,1,0:T(8,128)}, f32[4,256,128]{2,1,0:T(8,128)S(1)}, u32[]{:S(2)}, u32[]{:S(2)}) collective-permute-start(f32[4,256,128]{2,1,0:T(8,128)} %shard_map.52), channel_id=1, source_target_pairs={{0,1},{2,3},{4,5},{6,7},{8,9},{10,11},{12,13},{14,15},{16,17},{18,... | collective-permute-start | bytes 1572872 | tf_op jit(solution)/shard_map/ppermute | solution.py:483
  323.3 4.6 %shard_map.53 = f32[4,256,256]{2,1,0:T(8,128)} custom-call(bf16[1024,1024]{1,0:T(8,128)(2,1)} %get-tuple-element.49.high_ref, bf16[1024,1024]{1,0:T(8,128)(2,1)} %get-tuple-element.50.low_ref, f32[1,1024,256]{2,1,0:T(8,128)} %reduce-scatter.5.cloned.1.call-done.sums_ref), custom_call_target="tpu_custom_call" | custom-call | flops 1 | bytes 1 | tf_op jit(solution)/shard_map/pallas_call | solution.py:387
  327.9 4.0 %collective-permute-done.10 = f32[4,256,128]{2,1,0:T(8,128)S(1)} collective-permute-done((f32[4,256,128]{2,1,0:T(8,128)}, f32[4,256,128]{2,1,0:T(8,128)S(1)}, u32[]{:S(2)}, u32[]{:S(2)}) %collective-permute-start.10) | collective-permute-done | bytes 524320 | tf_op jit(solution)/shard_map/ppermute | solution.py:483
  332.1 15.9 %all_to_all.28.first_ref = f32[4,256,256]{2,1,0:T(8,128)} all-to-all(f32[4,256,256]{2,1,0:T(8,128)S(1)} %pad_maximum_fusion), channel_id=1, replica_groups=mesh['front'=16,'row'=4,'col'=2] {'row'}, dimensions={0} | all-to-all | bytes 2097152 | tf_op jit(solution)/shard_map/all_to_all | solution.py:488
  348.0 14.0 %all_to_all.29.second_ref = f32[4,256,256]{2,1,0:T(8,128)} all-to-all(f32[4,256,256]{2,1,0:T(8,128)S(1)} %copy-done.1), channel_id=1, replica_groups=mesh['front'=16,'row'=4,'col'=2] {'row'}, dimensions={0} | all-to-all | bytes 2097152 | tf_op jit(solution)/shard_map/all_to_all | solution.py:486
  362.0 3.4 shard_map.54
  (51 shorter events, 3.0 us)
Async XLA Ops:
  7.6 11.2 %collective-permute-start = (f32[96,1024]{1,0:T(8,128)S(1)}, f32[96,1024]{1,0:T(8,128)S(1)}, u32[]{:S(2)}, u32[]{:S(2)}) collective-permute-start(f32[96,1024]{1,0:T(8,128)S(1)} %slice.48), channel_id=1, source_target_pairs={{0,1},{1,0},{2,3},{3,2},{4,5},{5,4},{6,7},{7,6},{8,9},{9,8},{10,11... | collective-permute-start | bytes 1179656 | tf_op jit(solution)/shard_map/ppermute | solution.py:436
  18.8 8.6 %copy-start = (f32[1,384,2048]{2,1,0:T(8,128)S(1)}, f32[1,384,2048]{2,1,0:T(8,128)}, u32[]{:S(2)}) copy-start(f32[1,384,2048]{2,1,0:T(8,128)} %param.4) | copy-start | bytes 9437188
  18.8 137.9 %all-to-all-start = ((f32[32,64,1024]{2,1,0:T(8,128)}), f32[32,64,1024]{2,1,0:T(8,128)}, u32[]{:S(2)}, u32[]{:S(2)}) async-start(f32[32,64,1024]{2,1,0:T(8,128)} %bitcast.12), calls=%async_computation | async-start | bytes 16777216 | tf_op jit(solution)/shard_map/all_to_all | solution.py:444
  27.3 287.7 %reduce-scatter.3.cloned.1.call-start = ((), (), s32[]{:S(2)}) async-start(), calls=%async_computation.6 | async-start | bytes 2621440 | tf_op jit(solution)/shard_map/reduce_scatter | solution.py:477
  28.5 124.4 %collective-permute-start.1 = (f32[288,1024]{1,0:T(8,128)}, f32[288,1024]{1,0:T(8,128)}, u32[]{:S(2)}, u32[]{:S(2)}) collective-permute-start(f32[288,1024]{1,0:T(8,128)} %slice.49), channel_id=1, source_target_pairs={{0,1},{1,0},{2,3},{3,2},{4,5},{5,4},{6,7},{7,6},{8,9},{9,8},{10,11... | collective-permute-start | bytes 3538952 | tf_op jit(solution)/shard_map/ppermute | solution.py:437
  167.7 9.1 %copy-start.12 = (f32[128,1280]{1,0:T(8,128)S(1)}, f32[128,1280]{1,0:T(8,128)}, u32[]{:S(2)}) copy-start(f32[128,1280]{1,0:T(8,128)} %get-tuple-element.39) | copy-start | bytes 1966084
  176.8 17.7 %collective-permute-start.2 = (f32[128,1280]{1,0:T(8,128)S(1)}, f32[128,1280]{1,0:T(8,128)S(1)}, u32[]{:S(2)}, u32[]{:S(2)}) collective-permute-start(f32[128,1280]{1,0:T(8,128)S(1)} %copy-done.12), channel_id=1, source_target_pairs={{0,2},{2,4},{4,6},{6,0},{1,3},{3,5},{5,7},{7,1},{8,10},{10,12},{12... | collective-permute-start | bytes 1966088 | tf_op jit(solution)/shard_map/ppermute | solution.py:422
  178.3 11.9 %copy-start.11 = (f32[128,1280]{1,0:T(8,128)S(1)}, f32[128,1280]{1,0:T(8,128)}, u32[]{:S(2)}) copy-start(f32[128,1280]{1,0:T(8,128)} %get-tuple-element.40) | copy-start | bytes 1966084
  178.3 16.2 %copy-start.7 = (f32[64,1280]{1,0:T(8,128)S(1)}, f32[64,1280]{1,0:T(8,128)}, u32[]{:S(2)}) copy-start(f32[64,1280]{1,0:T(8,128)} %get-tuple-element.38) | copy-start | bytes 983044
  178.4 41.9 %copy-start.8 = (f32[64,1280]{1,0:T(8,128)S(1)}, f32[64,1280]{1,0:T(8,128)}, u32[]{:S(2)}) copy-start(f32[64,1280]{1,0:T(8,128)} %get-tuple-element.41) | copy-start | bytes 983044
  178.4 72.5 %all-to-all-start.1 = ((f32[16,64,1024]{2,1,0:T(8,128)}), f32[16,64,1024]{2,1,0:T(8,128)}, u32[]{:S(2)}, u32[]{:S(2)}) async-start(f32[16,64,1024]{2,1,0:T(8,128)} %bitcast.13), calls=%async_computation.1 | async-start | bytes 8388608 | tf_op jit(solution)/shard_map/all_to_all | solution.py:458
  190.2 41.0 %copy-start.6 = (f32[128,1280]{1,0:T(8,128)S(1)}, f32[128,1280]{1,0:T(8,128)}, u32[]{:S(2)}) copy-start(f32[128,1280]{1,0:T(8,128)} %get-tuple-element.37) | copy-start | bytes 1966084
  190.2 133.1 %reduce-scatter.5.cloned.1.call-start = ((), (), s32[]{:S(2)}) async-start(), calls=%async_computation.7 | async-start | bytes 5242880 | tf_op jit(solution)/shard_map/reduce_scatter | solution.py:477
  190.3 30.0 %collective-permute-start.4 = (f32[128,1280]{1,0:T(8,128)S(1)}, f32[128,1280]{1,0:T(8,128)S(1)}, u32[]{:S(2)}, u32[]{:S(2)}) collective-permute-start(f32[128,1280]{1,0:T(8,128)S(1)} %copy-done.11), channel_id=1, source_target_pairs={{0,6},{2,0},{4,2},{6,4},{1,7},{3,1},{5,3},{7,5},{8,14},{10,8},{12,... | collective-permute-start | bytes 1966088 | tf_op jit(solution)/shard_map/ppermute | solution.py:422
  194.6 25.7 %collective-permute-start.3 = (f32[64,1280]{1,0:T(8,128)S(1)}, f32[64,1280]{1,0:T(8,128)S(1)}, u32[]{:S(2)}, u32[]{:S(2)}) collective-permute-start(f32[64,1280]{1,0:T(8,128)S(1)} %slice_add_fusion.3), channel_id=1, source_target_pairs={{0,2},{2,4},{4,6},{6,0},{1,3},{3,5},{5,7},{7,1},{8,10},{10,12},{12... | collective-permute-start | bytes 983048 | tf_op jit(solution)/shard_map/ppermute | solution.py:422
  220.3 10.9 %collective-permute-start.5 = (f32[64,1280]{1,0:T(8,128)S(1)}, f32[64,1280]{1,0:T(8,128)S(1)}, u32[]{:S(2)}, u32[]{:S(2)}) collective-permute-start(f32[64,1280]{1,0:T(8,128)S(1)} %get-tuple-element.56), channel_id=1, source_target_pairs={{0,6},{2,0},{4,2},{6,4},{1,7},{3,1},{5,3},{7,5},{8,14},{10,8},{12,... | collective-permute-start | bytes 983048 | tf_op jit(solution)/shard_map/ppermute | solution.py:422
  231.4 33.6 %copy-start.2 = (f32[128,1280]{1,0:T(8,128)}, f32[128,1280]{1,0:T(8,128)S(1)}, u32[]{:S(2)}) copy-start(f32[128,1280]{1,0:T(8,128)S(1)} %maximum_add_fusion.piece_ref) | copy-start | bytes 1966084
  231.4 16.1 %collective-permute-start.7 = (f32[128,1280]{1,0:T(8,128)S(1)}, f32[128,1280]{1,0:T(8,128)S(1)}, u32[]{:S(2)}, u32[]{:S(2)}) collective-permute-start(f32[128,1280]{1,0:T(8,128)S(1)} %maximum_add_fusion.piece_ref), channel_id=1, source_target_pairs={{0,6},{2,0},{4,2},{6,4},{1,7},{3,1},{5,3},{7,5},{8,14},{10,8},{12,... | collective-permute-start | bytes 1966088 | tf_op jit(solution)/shard_map/ppermute | solution.py:422
  234.4 16.4 %collective-permute-start.6 = (f32[128,1280]{1,0:T(8,128)S(1)}, f32[128,1280]{1,0:T(8,128)S(1)}, u32[]{:S(2)}, u32[]{:S(2)}) collective-permute-start(f32[128,1280]{1,0:T(8,128)S(1)} %maximum_add_fusion.piece_ref), channel_id=1, source_target_pairs={{0,2},{2,4},{4,6},{6,0},{1,3},{3,5},{5,7},{7,1},{8,10},{10,12},{12... | collective-permute-start | bytes 1966088 | tf_op jit(solution)/shard_map/ppermute | solution.py:422
  247.4 17.6 %copy-start.4 = (f32[128,1280]{1,0:T(8,128)}, f32[128,1280]{1,0:T(8,128)S(1)}, u32[]{:S(2)}) copy-start(f32[128,1280]{1,0:T(8,128)S(1)} %collective-permute-done.7.after_ref) | copy-start | bytes 1966084
  247.5 17.6 %collective-permute-start.9 = (f32[64,1280]{1,0:T(8,128)S(1)}, f32[64,1280]{1,0:T(8,128)S(1)}, u32[]{:S(2)}, u32[]{:S(2)}) collective-permute-start(f32[64,1280]{1,0:T(8,128)S(1)} %slice.57), channel_id=1, source_target_pairs={{0,6},{2,0},{4,2},{6,4},{1,7},{3,1},{5,3},{7,5},{8,14},{10,8},{12,... | collective-permute-start | bytes 983048 | tf_op jit(solution)/shard_map/ppermute | solution.py:422
  250.8 14.2 %copy-start.5 = (f32[128,1280]{1,0:T(8,128)}, f32[128,1280]{1,0:T(8,128)S(1)}, u32[]{:S(2)}) copy-start(f32[128,1280]{1,0:T(8,128)S(1)} %collective-permute-done.6.before_ref) | copy-start | bytes 1966084
  250.8 14.2 %collective-permute-start.8 = (f32[64,1280]{1,0:T(8,128)S(1)}, f32[64,1280]{1,0:T(8,128)S(1)}, u32[]{:S(2)}, u32[]{:S(2)}) collective-permute-start(f32[64,1280]{1,0:T(8,128)S(1)} %slice.56), channel_id=1, source_target_pairs={{0,2},{2,4},{4,6},{6,0},{1,3},{3,5},{5,7},{7,1},{8,10},{10,12},{12... | collective-permute-start | bytes 983048 | tf_op jit(solution)/shard_map/ppermute | solution.py:422
  265.0 0.7 copy-start.9
  265.0 0.8 copy-start.10
  319.5 12.5 %copy-start.3 = (f32[4,256,128]{2,1,0:T(8,128)S(1)}, f32[4,256,128]{2,1,0:T(8,128)}, u32[]{:S(2)}) copy-start(f32[4,256,128]{2,1,0:T(8,128)} %shard_map.52) | copy-start | bytes 1572868
  319.5 12.5 %collective-permute-start.10 = (f32[4,256,128]{2,1,0:T(8,128)}, f32[4,256,128]{2,1,0:T(8,128)S(1)}, u32[]{:S(2)}, u32[]{:S(2)}) collective-permute-start(f32[4,256,128]{2,1,0:T(8,128)} %shard_map.52), channel_id=1, source_target_pairs={{0,1},{2,3},{4,5},{6,7},{8,9},{10,11},{12,13},{14,15},{16,17},{18,... | collective-permute-start | bytes 1572872 | tf_op jit(solution)/shard_map/ppermute | solution.py:483
  327.9 20.0 %copy-start.1 = (f32[4,256,256]{2,1,0:T(8,128)S(1)}, f32[4,256,256]{2,1,0:T(8,128)}, u32[]{:S(2)}) copy-start(f32[4,256,256]{2,1,0:T(8,128)} %shard_map.53) | copy-start | bytes 3145732
Sparse Core Ops, SparseCore 0:
  178.5 48.5 reduce-scatter.2
  265.2 51.0 reduce-scatter.4

commit v6 on v5

--- a/solution.py
+++ b/solution.py
@@ -271,8 +271,9 @@
 
 
 def factor_kernel(
-    turn_ref, piece_ref, before_ref, after_ref, across_ref, across_rest_ref,
-    high_ref, low_ref, leading_ref, work_ref, diag_ref, packed_ref, panel_high_ref, panel_low_ref,
+    turn_ref, piece_ref, before_ref, after_ref, across_ref, across_rest_ref, sums_ref,
+    high_ref, low_ref, leading_ref, solved_ref,
+    work_ref, diag_ref, packed_ref, panel_high_ref, panel_low_ref, found_ref,
 ):
     turn = turn_ref[0, 0]
     middle = BLK // 2
@@ -296,6 +297,12 @@
     chunk_of = lax.broadcasted_iota(jnp.int32, (BLK, WIDE), 1) // BLK
     deferred = [(i, c) for i in range(2, STEPS) for c in range(ELIMINATED // WIDE)]
 
+    sums = halves(sums_ref[0])
+
+    def solve_rows(k):
+        rows = pl.ds(pl.multiple_of(k * BLK, BLK), BLK)
+        found_ref[rows, :] = sharp_dot((high_ref[rows, :], low_ref[rows, :]), sums, PLAIN)
+
     def step(k, _):
         here = pl.ds(pl.multiple_of(k * BLK, BLK), BLK)
         block = work_ref[here, here]
@@ -319,12 +326,15 @@
             for i, c in deferred[len(deferred) * b // count : len(deferred) * (b + 1) // count]:
                 update(i, c)
 
+        solve_rows(jnp.maximum(k - 1, 0))
         inverse = lower_inverse(block, beside)
         rows = sharp_dot(halves(inverse), halves(work_ref[here, :]), PLAIN)
         work_ref[here, :] = rows
         diag_ref[here, :] = jnp.where(row <= col, work_ref[here, here], 0.0)
         work_ref[here, here] = inverse
-        panel_high_ref[...], panel_low_ref[...] = halves(work_ref[here, :])
+        rows = work_ref[here, :]
+        panel_high_ref[...], panel_low_ref[...] = halves(rows)
+        high_ref[here, :], low_ref[here, :] = halves(jnp.where(place_of <= k, rows, 0.0))
 
         @pl.when(k < STEPS - 1)
         def _():
@@ -344,12 +354,14 @@
         leading_ref[BLK * b : BLK * (b + 1), :] = jnp.where(
             place_of > block, work_ref[here, :], jnp.where(place_of == block, diag, 0.0)
         )
-    for k in range(STEPS):
-        rows = slice(BLK * k, BLK * (k + 1))
-        high_ref[rows, :], low_ref[rows, :] = halves(jnp.where(place_of <= k, work_ref[rows, :], 0.0))
-
-
-def factor(turn, piece, before, after, across, across_rest):
+    solve_rows(STEPS - 1)
+    parts, copies, quarter, _ = solved_ref.shape
+    for i in range(parts):
+        for copy in range(copies):
+            solved_ref[i, copy] = found_ref[quarter * i : quarter * (i + 1), :]
+
+
+def factor(turn, piece, before, after, across, across_rest, sums):
     vmem = pl.BlockSpec(memory_space=pltpu.VMEM)
     return pl.pallas_call(
         factor_kernel,
@@ -357,19 +369,21 @@
             jax.ShapeDtypeStruct((ELIMINATED, ELIMINATED), jnp.bfloat16),
             jax.ShapeDtypeStruct((ELIMINATED, ELIMINATED), jnp.bfloat16),
             jax.ShapeDtypeStruct((ELIMINATED // 4, ELIMINATED), jnp.float32),
+            jax.ShapeDtypeStruct((4, 2, ELIMINATED // 4, BLK), jnp.float32),
         ),
-        in_specs=[pl.BlockSpec(memory_space=pltpu.SMEM)] + [vmem] * 5,
-        out_specs=(vmem, vmem, vmem),
+        in_specs=[pl.BlockSpec(memory_space=pltpu.SMEM)] + [vmem] * 6,
+        out_specs=(vmem, vmem, vmem, vmem),
         scratch_shapes=[
             pltpu.VMEM((ELIMINATED, ELIMINATED), jnp.float32),
             pltpu.VMEM((ELIMINATED, BLK), jnp.float32),
             pltpu.VMEM((4, BLK, PACKED), jnp.float32),
             pltpu.VMEM((BLK, ELIMINATED), jnp.bfloat16),
             pltpu.VMEM((BLK, ELIMINATED), jnp.bfloat16),
+            pltpu.VMEM((ELIMINATED, BLK), jnp.float32),
         ],
         compiler_params=pltpu.CompilerParams(vmem_limit_bytes=VMEM_BYTES),
         cost_estimate=LIGHT,
-    )(turn, piece, before, after, across, across_rest)
+    )(turn, piece, before, after, across, across_rest, sums)
 
 
 def solve_kernel(high_ref, low_ref, sums_ref, out_ref):
@@ -396,11 +410,12 @@
 
 def join_kernel(col_ref, leading_ref, first_ref, second_ref, out_ref):
     parts, _, width = second_ref.shape
-    for half in range(2):
-        for j in range(parts):
-            cols = slice(ELIMINATED // 2 * half + BLK * j, ELIMINATED // 2 * half + BLK * (j + 1))
+    for j in range(parts):
+        for half in range(2):
+            start = ELIMINATED // 2 * half + BLK * j
+            cols = slice(start, start + BLK)
             out_ref[0, :, cols] = jnp.where(
-                col_ref[0, 0] == 0, leading_ref[:, cols], first_ref[j, :, BLK * half : BLK * (half + 1)]
+                col_ref[0, 0] == 0, leading_ref[:, cols], first_ref[j, half]
             )
     for j in range(parts):
         out_ref[0, :, ELIMINATED + width * j : ELIMINATED + width * (j + 1)] = second_ref[j]
@@ -461,7 +476,6 @@
     turn = row_index.reshape(1, 1)
     mine, right, left, right_rest, left_rest, turned = packed_gram(turn, own_panel, arrived)
     products_a = shared_cross(col_index.reshape(1), turned, own_shared, arrived)
-    mine, right, left, products_a = lax.optimization_barrier((mine, right, left, products_a))
     middle = BLK // 2
     from_left, from_right = shifted(right, 1, row_count), shifted(left, -1, row_count)
     rest_left = shifted(right_rest + from_left[:middle], 1, row_count)
@@ -469,6 +483,7 @@
     piece = mine + jnp.concatenate(
         [rest_left + from_right[middle:], from_left[middle:] + rest_right], axis=0
     )
+    piece, child_b = lax.optimization_barrier((piece, child_b))
     before, after = shifted(piece, 1, row_count), shifted(piece, -1, row_count)
     across, across_rest = shifted(before[:middle], 1, row_count), shifted(after[middle:], -1, row_count)
     pieces = (piece, before, after, across, across_rest)
@@ -478,14 +493,12 @@
 
     products_b = cross(turned, own, ELIMINATED, child_b, 0)
     pieces, products_b = lax.optimization_barrier((pieces, products_b))
-    inverse_high, inverse_low, leading = factor(turn, *pieces)
-    first = solve(inverse_high, inverse_low, summed(products_a))
-    handed = lax.ppermute(first, "col", [(0, 1)])
+    inverse_high, inverse_low, leading, first = factor(turn, *pieces, summed(products_a))
+    first = lax.all_to_all(
+        first.reshape(2 * row_count, quarter, BLK), ("row", "col"), split_axis=0, concat_axis=0, tiled=True
+    ).reshape(row_count, 2, quarter, BLK)
     second = solve(inverse_high, inverse_low, summed(products_b))
-    handed, later = lax.optimization_barrier((handed, second))
-    second = lax.all_to_all(later, "row", split_axis=0, concat_axis=0, tiled=True)
-    first = jnp.concatenate([handed, first], axis=2)
-    first = lax.all_to_all(first, "row", split_axis=0, concat_axis=0, tiled=True)
+    second = lax.all_to_all(second, "row", split_axis=0, concat_axis=0, tiled=True)
     return join(col_index.reshape(1, 1), leading, first, second)
 
 

time: 376 us -> 367 us (0.976)
  blocking collectives: 29.9 us -> 15.7 us
    all_to_all x2 -> x1, blocking collectives: 29.9 us -> 15.7 us  [body(): lax.all_to_all(second, 'row', split_axis=0, concat_axis=0, tiled=True)]
    all_to_all x0 -> x1, waiting for transfers between devices: none -> 7.65 us  [body(): lax.all_to_all(first.reshape(2 * row_count, quarter, BLK), ('row', 'col')...]
    all_to_all x0 -> x1, starting transfers between devices: none -> 5.68 us  [body(): lax.all_to_all(first.reshape(2 * row_count, quarter, BLK), ('row', 'col')...]
    pallas_call x2 -> x1, Pallas kernels: 9.08 us -> 4.67 us  [solve(): pl.pallas_call(solve_kernel, out_shape=jax.ShapeDtypeStruct((4, ELIMINATE...]
    ppermute x1 -> x0, waiting for transfers between devices: 4.04 us -> none  [body(): handed = lax.ppermute(first, 'col', [(0, 1)])]
    ppermute x1 -> x0, starting transfers between devices: 3.77 us -> none  [body(): handed = lax.ppermute(first, 'col', [(0, 1)])]
  transfers between devices with their start and end apart: 15 -> 15, of which waited for: 7 -> 7; matrix products, arithmetic and copies ran while one was open for 2% -> 3% of each run, Pallas kernels for 23% -> 29%
where the time goes in v6:
time: 367 us; the launch traced here: 365 us
  waiting for transfers between devices  169 us (46%)
  Pallas kernels  108 us (29%)
  starting transfers between devices  44.8 us (12%)
  blocking collectives  15.7 us (4%)
  between operations  13.6 us (4%)
  local copies, waits for them, and re-layouts  8.11 us (2%)
  other arithmetic  5.72 us (2%)
    ppermute x1, waiting for transfers between devices, body(): passed_rest = lax.ppermute(own_a[split:], 'col', [(0, 1), (1, 0)])  116 us
    pallas_call x1, Pallas kernels, factor(): pl.pallas_call(factor_kernel, out_shape=(jax.ShapeDtypeStruct((ELIMINATED...  51.6 us
    ppermute x8, waiting for transfers between devices, shifted(): lax.ppermute(x, 'row', [(i, (i + shift) % count) for i in range(count)])  45.2 us
    all_to_all x1, blocking collectives, body(): lax.all_to_all(second, 'row', split_axis=0, concat_axis=0, tiled=True)  15.7 us
    ppermute x8, starting transfers between devices, shifted(): lax.ppermute(x, 'row', [(i, (i + shift) % count) for i in range(count)])  15 us
    pallas_call x1, Pallas kernels, cross(): pl.pallas_call(cross_kernel, grid=(ELIMINATED // WIDE,), out_shape=jax.Sh...  14.2 us
    pallas_call x2, Pallas kernels, place(): pl.pallas_call(place_kernel, grid=(ELIMINATED // WIDE,), out_shape=jax.Sh...  14.1 us
    all_to_all x1, starting transfers between devices, body(): lax.all_to_all(single.reshape(n_front * capacity, ELIMINATED), 'front', s...  11.7 us
  transfers between devices with their start and end apart: 15, of which 7 were waited for; matrix products, arithmetic and copies ran while one was open for 3% of the time, Pallas kernels for 29%

profile of v6, /device:TPU:0, one launch (start us, length us, event | category | flops | bytes accessed | tf_op | source)
XLA Modules:
  0.0 364.9 jit_solution(17309901841206866089)
XLA Ops:
  6.5 1.0 slice.48
  7.6 2.1 collective-permute-start
  9.6 1.5 copy.5.stair_ref
  11.2 7.4 %shard_map.46 = f32[16,2,64,1024]{3,2,1,0:T(8,128)} custom-call(s32[1,1]{1,0:T(1,128)} %bitcast.3.first_ref, s32[1,512]{1,0:T(1,128)} %bitcast.23, s32[512,1]{1,0:T(8,128)} %copy.5.stair_ref, f32[512,2048]{1,0:T(8,128)} %rows_ref.3), custom_call_target="tpu_custom_call" | custom-call | flops 1 | bytes 1 | tf_op jit(solution)/shard_map/pallas_call | solution.py:126
  18.8 8.6 %all-to-all-start = ((f32[32,64,1024]{2,1,0:T(8,128)}), f32[32,64,1024]{2,1,0:T(8,128)}, u32[]{:S(2)}, u32[]{:S(2)}) async-start(f32[32,64,1024]{2,1,0:T(8,128)} %bitcast.14), calls=%async_computation | async-start | bytes 16777216 | tf_op jit(solution)/shard_map/all_to_all | solution.py:459
  27.3 1.1 slice.49
  28.4 1.7 collective-permute-start.1
  30.1 6.7 %shard_map.47 = f32[16,1,64,1024]{3,2,1,0:T(8,128)} custom-call(s32[1,1]{1,0:T(1,128)} %bitcast.6.first_ref, s32[1,512]{1,0:T(1,128)} %bitcast.24, s32[512,1]{1,0:T(8,128)} %copy.5.stair_ref, f32[512,2048]{1,0:T(8,128)} %rows_ref.3), custom_call_target="tpu_custom_call" | custom-call | flops 1 | bytes 1 | tf_op jit(solution)/shard_map/pallas_call | solution.py:126
  36.8 116.1 %collective-permute-done.1 = f32[288,1024]{1,0:T(8,128)} collective-permute-done((f32[288,1024]{1,0:T(8,128)}, f32[288,1024]{1,0:T(8,128)}, u32[]{:S(2)}, u32[]{:S(2)}) %collective-permute-start.1) | collective-permute-done | bytes 1179680 | tf_op jit(solution)/shard_map/ppermute | solution.py:452
  152.9 1.3 constant_dynamic-update-slice_fusion
  154.3 1.2 copy-done.1
  155.5 1.4 slice_select_fusion.own_ref
  156.9 11.7 %all-to-all-start.1 = ((f32[16,64,1024]{2,1,0:T(8,128)}), f32[16,64,1024]{2,1,0:T(8,128)}, u32[]{:S(2)}, u32[]{:S(2)}) async-start(f32[16,64,1024]{2,1,0:T(8,128)} %bitcast.15), calls=%async_computation.1 | async-start | bytes 8388608 | tf_op jit(solution)/shard_map/all_to_all | solution.py:473
  168.6 10.9 %shard_map.48 = (f32[128,1280]{1,0:T(8,128)}, f32[128,1280]{1,0:T(8,128)}, f32[128,1280]{1,0:T(8,128)}, f32[64,1280]{1,0:T(8,128)}, f32[64,1280]{1,0:T(8,128)}, /*index=5*/bf16[1024,2816]{1,0:T(8,128)(2,1)}) custom-call(s32[1,1]{1,0:T(1,128)} %bitcast.1.turn_ref, f32[384,1024]{1,0:T(8,128)} %slice_select_fusion.own_ref, f32[16,2,64,1024]{3,2,1,0:T(8,128)} %bitcast.8.child_ref), custom_call_target="tpu_custom_call" | custom-call | flops 1 | bytes 1 | tf_op jit(solution)/shard_map/pallas_call | solution.py:191
  179.6 1.5 collective-permute-start.2
  181.1 2.2 slice_select_fusion.1.own_ref
  183.2 9.0 %shard_map.50 = f32[4,1024,128]{2,1,0:T(8,128)} custom-call(s32[1]{0:T(128)} %bitcast.11._, bf16[1024,2816]{1,0:T(8,128)(2,1)} %get-tuple-element.37.turned_ref, f32[384,512]{1,0:T(8,128)} %slice_select_fusion.1.own_ref, f32[16,2,64,1024]{3,2,1,0:T(8,128)} %bitcast.8.child_ref), custom_call_target="tpu_custom_call" | custom-call | flops 1 | bytes 1 | tf_op jit(solution)/shard_map/pallas_call | solution.py:243
  193.3 1.7 collective-permute-start.4
  195.1 3.0 collective-permute-done.2
  199.5 16.9 %collective-permute-done.4 = f32[128,1280]{1,0:T(8,128)S(1)} collective-permute-done((f32[128,1280]{1,0:T(8,128)S(1)}, f32[128,1280]{1,0:T(8,128)S(1)}, u32[]{:S(2)}, u32[]{:S(2)}) %collective-permute-start.4) | collective-permute-done | bytes 655392 | tf_op jit(solution)/shard_map/ppermute | solution.py:437
  216.5 3.8 %collective-permute-start.5 = (f32[64,1280]{1,0:T(8,128)S(1)}, f32[64,1280]{1,0:T(8,128)S(1)}, u32[]{:S(2)}, u32[]{:S(2)}) collective-permute-start(f32[64,1280]{1,0:T(8,128)S(1)} %get-tuple-element.50), channel_id=1, source_target_pairs={{0,6},{2,0},{4,2},{6,4},{1,7},{3,1},{5,3},{7,5},{8,14},{10,8},{12,... | collective-permute-start | bytes 983048 | tf_op jit(solution)/shard_map/ppermute | solution.py:437
  220.2 13.0 %collective-permute-done.5 = f32[64,1280]{1,0:T(8,128)S(1)} collective-permute-done((f32[64,1280]{1,0:T(8,128)S(1)}, f32[64,1280]{1,0:T(8,128)S(1)}, u32[]{:S(2)}, u32[]{:S(2)}) %collective-permute-start.5) | collective-permute-done | bytes 327712 | tf_op jit(solution)/shard_map/ppermute | solution.py:437
  234.3 3.8 %collective-permute-start.7 = (f32[128,1280]{1,0:T(8,128)S(1)}, f32[128,1280]{1,0:T(8,128)S(1)}, u32[]{:S(2)}, u32[]{:S(2)}) collective-permute-start(f32[128,1280]{1,0:T(8,128)S(1)} %maximum_add_fusion.piece_ref), channel_id=1, source_target_pairs={{0,6},{2,0},{4,2},{6,4},{1,7},{3,1},{5,3},{7,5},{8,14},{10,8},{12,... | collective-permute-start | bytes 1966088 | tf_op jit(solution)/shard_map/ppermute | solution.py:437
  238.1 12.2 %collective-permute-done.7.after_ref = f32[128,1280]{1,0:T(8,128)S(1)} collective-permute-done((f32[128,1280]{1,0:T(8,128)S(1)}, f32[128,1280]{1,0:T(8,128)S(1)}, u32[]{:S(2)}, u32[]{:S(2)}) %collective-permute-start.7) | collective-permute-done | bytes 655392 | tf_op jit(solution)/shard_map/ppermute | solution.py:437
  250.4 3.8 %collective-permute-start.9 = (f32[64,1280]{1,0:T(8,128)S(1)}, f32[64,1280]{1,0:T(8,128)S(1)}, u32[]{:S(2)}, u32[]{:S(2)}) collective-permute-start(f32[64,1280]{1,0:T(8,128)S(1)} %slice.55), channel_id=1, source_target_pairs={{0,6},{2,0},{4,2},{6,4},{1,7},{3,1},{5,3},{7,5},{8,14},{10,8},{12,... | collective-permute-start | bytes 983048 | tf_op jit(solution)/shard_map/ppermute | solution.py:437
  254.2 14.2 %shard_map.49 = f32[4,1024,256]{2,1,0:T(8,128)} custom-call(bf16[1024,2816]{1,0:T(8,128)(2,1)} %get-tuple-element.37.turned_ref, f32[384,2048]{1,0:T(8,128)} %bitcast.17, f32[16,1,64,1024]{3,2,1,0:T(8,128)} %bitcast.10.child_ref), custom_call_target="tpu_custom_call" | custom-call | flops 1 | bytes 1 | tf_op jit(solution)/shard_map/pallas_call | solution.py:217
  269.3 51.6 %shard_map.51 = (bf16[1024,1024]{1,0:T(8,128)(2,1)}, bf16[1024,1024]{1,0:T(8,128)(2,1)}, f32[256,1024]{1,0:T(8,128)}, f32[4,2,256,128]{3,2,1,0:T(8,128)}) custom-call(s32[1,1]{1,0:T(1,128)} %bitcast.1.turn_ref, f32[128,1280]{1,0:T(8,128)} %copy-done.3, f32[128,1280]{1,0:T(8,128)} %copy-done.5, f32[128,1280]{1,0:T(8,128)} %copy-done.4, ...), custom_call_target="tpu_custom_call" | custom-call | flops 1 | bytes 1 | tf_op jit(solution)/shard_map/pallas_call | solution.py:366
  320.9 5.7 %all-to-all-start.2 = ((f32[8,256,128]{2,1,0:T(8,128)}), f32[8,256,128]{2,1,0:T(8,128)S(1)}, u32[]{:S(2)}, u32[]{:S(2)}) async-start(f32[8,256,128]{2,1,0:T(8,128)} %bitcast.22), calls=%async_computation.3 | async-start | bytes 2097152 | tf_op jit(solution)/shard_map/all_to_all | solution.py:497
  326.6 4.7 %shard_map.52 = f32[4,256,256]{2,1,0:T(8,128)} custom-call(bf16[1024,1024]{1,0:T(8,128)(2,1)} %get-tuple-element.46.high_ref, bf16[1024,1024]{1,0:T(8,128)(2,1)} %get-tuple-element.47.low_ref, f32[1,1024,256]{2,1,0:T(8,128)} %reduce-scatter.5.cloned.1.call-done.sums_ref), custom_call_target="tpu_custom_call" | custom-call | flops 1 | bytes 1 | tf_op jit(solution)/shard_map/pallas_call | solution.py:401
  331.3 7.6 %all-to-all-done.2 = f32[8,256,128]{2,1,0:T(8,128)S(1)} async-done(((f32[8,256,128]{2,1,0:T(8,128)}), f32[8,256,128]{2,1,0:T(8,128)S(1)}, u32[]{:S(2)}, u32[]{:S(2)}) %all-to-all-start.2) | async-done | bytes 1048608 | tf_op jit(solution)/shard_map/all_to_all | solution.py:497
  338.9 15.7 %all_to_all.28.second_ref = f32[4,256,256]{2,1,0:T(8,128)} all-to-all(f32[4,256,256]{2,1,0:T(8,128)} %shard_map.52), channel_id=1, replica_groups=mesh['front'=16,'row'=4,'col'=2] {'row'}, dimensions={0} | all-to-all | bytes 2097152 | tf_op jit(solution)/shard_map/all_to_all | solution.py:501
  354.7 3.4 shard_map.53
  (46 shorter events, 4.9 us)
Async XLA Ops:
  7.6 11.2 %collective-permute-start = (f32[96,1024]{1,0:T(8,128)S(1)}, f32[96,1024]{1,0:T(8,128)S(1)}, u32[]{:S(2)}, u32[]{:S(2)}) collective-permute-start(f32[96,1024]{1,0:T(8,128)S(1)} %slice.48), channel_id=1, source_target_pairs={{0,1},{1,0},{2,3},{3,2},{4,5},{5,4},{6,7},{7,6},{8,9},{9,8},{10,11... | collective-permute-start | bytes 1179656 | tf_op jit(solution)/shard_map/ppermute | solution.py:451
  18.8 8.6 %copy-start = (f32[1,384,2048]{2,1,0:T(8,128)S(1)}, f32[1,384,2048]{2,1,0:T(8,128)}, u32[]{:S(2)}) copy-start(f32[1,384,2048]{2,1,0:T(8,128)} %param.4) | copy-start | bytes 9437188
  18.8 138.1 %all-to-all-start = ((f32[32,64,1024]{2,1,0:T(8,128)}), f32[32,64,1024]{2,1,0:T(8,128)}, u32[]{:S(2)}, u32[]{:S(2)}) async-start(f32[32,64,1024]{2,1,0:T(8,128)} %bitcast.14), calls=%async_computation | async-start | bytes 16777216 | tf_op jit(solution)/shard_map/all_to_all | solution.py:459
  28.4 124.5 %collective-permute-start.1 = (f32[288,1024]{1,0:T(8,128)}, f32[288,1024]{1,0:T(8,128)}, u32[]{:S(2)}, u32[]{:S(2)}) collective-permute-start(f32[288,1024]{1,0:T(8,128)} %slice.49), channel_id=1, source_target_pairs={{0,1},{1,0},{2,3},{3,2},{4,5},{5,4},{6,7},{7,6},{8,9},{9,8},{10,11... | collective-permute-start | bytes 3538952 | tf_op jit(solution)/shard_map/ppermute | solution.py:452
  154.3 1.2 copy-start.1
  156.9 77.5 %all-to-all-start.1 = ((f32[16,64,1024]{2,1,0:T(8,128)}), f32[16,64,1024]{2,1,0:T(8,128)}, u32[]{:S(2)}, u32[]{:S(2)}) async-start(f32[16,64,1024]{2,1,0:T(8,128)} %bitcast.15), calls=%async_computation.1 | async-start | bytes 8388608 | tf_op jit(solution)/shard_map/all_to_all | solution.py:473
  168.6 100.8 %reduce-scatter.3.cloned.1.call-start = ((), (), s32[]{:S(2)}) async-start(), calls=%async_computation.6 | async-start | bytes 2621440 | tf_op jit(solution)/shard_map/reduce_scatter | solution.py:492
  179.6 18.5 %collective-permute-start.2 = (f32[128,1280]{1,0:T(8,128)}, f32[128,1280]{1,0:T(8,128)}, u32[]{:S(2)}, u32[]{:S(2)}) collective-permute-start(f32[128,1280]{1,0:T(8,128)} %get-tuple-element.32), channel_id=1, source_target_pairs={{0,2},{2,4},{4,6},{6,0},{1,3},{3,5},{5,7},{7,1},{8,10},{10,12},{12... | collective-permute-start | bytes 1966088 | tf_op jit(solution)/shard_map/ppermute | solution.py:437
  192.2 1.1 copy-start.11
  192.3 5.8 %copy-start.7 = (f32[64,1280]{1,0:T(8,128)S(1)}, f32[64,1280]{1,0:T(8,128)}, u32[]{:S(2)}) copy-start(f32[64,1280]{1,0:T(8,128)} %get-tuple-element.31) | copy-start | bytes 983044
  192.3 24.2 %copy-start.8 = (f32[64,1280]{1,0:T(8,128)S(1)}, f32[64,1280]{1,0:T(8,128)}, u32[]{:S(2)}) copy-start(f32[64,1280]{1,0:T(8,128)} %get-tuple-element.34) | copy-start | bytes 983044
  192.3 41.9 %copy-start.6 = (f32[128,1280]{1,0:T(8,128)S(1)}, f32[128,1280]{1,0:T(8,128)}, u32[]{:S(2)}) copy-start(f32[128,1280]{1,0:T(8,128)} %get-tuple-element.30) | copy-start | bytes 1966084
  192.3 134.3 %reduce-scatter.5.cloned.1.call-start = ((), (), s32[]{:S(2)}) async-start(), calls=%async_computation.7 | async-start | bytes 5242880 | tf_op jit(solution)/shard_map/reduce_scatter | solution.py:492
  193.3 23.1 %collective-permute-start.4 = (f32[128,1280]{1,0:T(8,128)S(1)}, f32[128,1280]{1,0:T(8,128)S(1)}, u32[]{:S(2)}, u32[]{:S(2)}) collective-permute-start(f32[128,1280]{1,0:T(8,128)S(1)} %copy-done.11), channel_id=1, source_target_pairs={{0,6},{2,0},{4,2},{6,4},{1,7},{3,1},{5,3},{7,5},{8,14},{10,8},{12,... | collective-permute-start | bytes 1966088 | tf_op jit(solution)/shard_map/ppermute | solution.py:437
  199.1 17.3 %collective-permute-start.3 = (f32[64,1280]{1,0:T(8,128)S(1)}, f32[64,1280]{1,0:T(8,128)S(1)}, u32[]{:S(2)}, u32[]{:S(2)}) collective-permute-start(f32[64,1280]{1,0:T(8,128)S(1)} %slice_add_fusion.3), channel_id=1, source_target_pairs={{0,2},{2,4},{4,6},{6,0},{1,3},{3,5},{5,7},{7,1},{8,10},{10,12},{12... | collective-permute-start | bytes 983048 | tf_op jit(solution)/shard_map/ppermute | solution.py:437
  216.5 16.7 %collective-permute-start.5 = (f32[64,1280]{1,0:T(8,128)S(1)}, f32[64,1280]{1,0:T(8,128)S(1)}, u32[]{:S(2)}, u32[]{:S(2)}) collective-permute-start(f32[64,1280]{1,0:T(8,128)S(1)} %get-tuple-element.50), channel_id=1, source_target_pairs={{0,6},{2,0},{4,2},{6,4},{1,7},{3,1},{5,3},{7,5},{8,14},{10,8},{12,... | collective-permute-start | bytes 983048 | tf_op jit(solution)/shard_map/ppermute | solution.py:437
  234.3 34.1 %copy-start.3 = (f32[128,1280]{1,0:T(8,128)}, f32[128,1280]{1,0:T(8,128)S(1)}, u32[]{:S(2)}) copy-start(f32[128,1280]{1,0:T(8,128)S(1)} %maximum_add_fusion.piece_ref) | copy-start | bytes 1966084
  234.3 16.0 %collective-permute-start.7 = (f32[128,1280]{1,0:T(8,128)S(1)}, f32[128,1280]{1,0:T(8,128)S(1)}, u32[]{:S(2)}, u32[]{:S(2)}) collective-permute-start(f32[128,1280]{1,0:T(8,128)S(1)} %maximum_add_fusion.piece_ref), channel_id=1, source_target_pairs={{0,6},{2,0},{4,2},{6,4},{1,7},{3,1},{5,3},{7,5},{8,14},{10,8},{12,... | collective-permute-start | bytes 1966088 | tf_op jit(solution)/shard_map/ppermute | solution.py:437
  238.1 16.0 %collective-permute-start.6 = (f32[128,1280]{1,0:T(8,128)S(1)}, f32[128,1280]{1,0:T(8,128)S(1)}, u32[]{:S(2)}, u32[]{:S(2)}) collective-permute-start(f32[128,1280]{1,0:T(8,128)S(1)} %maximum_add_fusion.piece_ref), channel_id=1, source_target_pairs={{0,2},{2,4},{4,6},{6,0},{1,3},{3,5},{5,7},{7,1},{8,10},{10,12},{12... | collective-permute-start | bytes 1966088 | tf_op jit(solution)/shard_map/ppermute | solution.py:437
  250.3 18.1 %copy-start.4 = (f32[128,1280]{1,0:T(8,128)}, f32[128,1280]{1,0:T(8,128)S(1)}, u32[]{:S(2)}) copy-start(f32[128,1280]{1,0:T(8,128)S(1)} %collective-permute-done.7.after_ref) | copy-start | bytes 1966084
  250.4 18.1 %collective-permute-start.9 = (f32[64,1280]{1,0:T(8,128)S(1)}, f32[64,1280]{1,0:T(8,128)S(1)}, u32[]{:S(2)}, u32[]{:S(2)}) collective-permute-start(f32[64,1280]{1,0:T(8,128)S(1)} %slice.55), channel_id=1, source_target_pairs={{0,6},{2,0},{4,2},{6,4},{1,7},{3,1},{5,3},{7,5},{8,14},{10,8},{12,... | collective-permute-start | bytes 983048 | tf_op jit(solution)/shard_map/ppermute | solution.py:437
  254.1 14.3 %copy-start.5 = (f32[128,1280]{1,0:T(8,128)}, f32[128,1280]{1,0:T(8,128)S(1)}, u32[]{:S(2)}) copy-start(f32[128,1280]{1,0:T(8,128)S(1)} %collective-permute-done.6.before_ref) | copy-start | bytes 1966084
  254.1 14.3 %collective-permute-start.8 = (f32[64,1280]{1,0:T(8,128)S(1)}, f32[64,1280]{1,0:T(8,128)S(1)}, u32[]{:S(2)}, u32[]{:S(2)}) collective-permute-start(f32[64,1280]{1,0:T(8,128)S(1)} %slice.54), channel_id=1, source_target_pairs={{0,2},{2,4},{4,6},{6,0},{1,3},{3,5},{5,7},{7,1},{8,10},{10,12},{12... | collective-permute-start | bytes 983048 | tf_op jit(solution)/shard_map/ppermute | solution.py:437
  268.4 0.7 copy-start.9
  268.5 0.9 copy-start.10
  320.9 18.0 %all-to-all-start.2 = ((f32[8,256,128]{2,1,0:T(8,128)}), f32[8,256,128]{2,1,0:T(8,128)S(1)}, u32[]{:S(2)}, u32[]{:S(2)}) async-start(f32[8,256,128]{2,1,0:T(8,128)} %bitcast.22), calls=%async_computation.3 | async-start | bytes 2097152 | tf_op jit(solution)/shard_map/all_to_all | solution.py:497
  338.9 15.7 %copy-start.2 = (f32[8,256,128]{2,1,0:T(8,128)}, f32[8,256,128]{2,1,0:T(8,128)S(1)}, u32[]{:S(2)}) copy-start(f32[8,256,128]{2,1,0:T(8,128)S(1)} %all-to-all-done.2) | copy-start | bytes 3145732
Sparse Core Ops, SparseCore 0:
  192.4 42.5 reduce-scatter.2
  268.6 49.3 reduce-scatter.4

commit v7 on v6

--- a/solution.py
+++ b/solution.py
@@ -475,16 +475,18 @@
     ).reshape(n_front, 1, capacity, ELIMINATED)
     turn = row_index.reshape(1, 1)
     mine, right, left, right_rest, left_rest, turned = packed_gram(turn, own_panel, arrived)
-    products_a = shared_cross(col_index.reshape(1), turned, own_shared, arrived)
     middle = BLK // 2
     from_left, from_right = shifted(right, 1, row_count), shifted(left, -1, row_count)
+    from_left, from_right, turned_later = lax.optimization_barrier((from_left, from_right, turned))
+    products_a = shared_cross(col_index.reshape(1), turned_later, own_shared, arrived)
     rest_left = shifted(right_rest + from_left[:middle], 1, row_count)
     rest_right = shifted(left_rest + from_right[:middle], -1, row_count)
+    rest_left, rest_right = lax.optimization_barrier((rest_left, rest_right))
     piece = mine + jnp.concatenate(
         [rest_left + from_right[middle:], from_left[middle:] + rest_right], axis=0
     )
-    piece, child_b = lax.optimization_barrier((piece, child_b))
     before, after = shifted(piece, 1, row_count), shifted(piece, -1, row_count)
+    before, after, child_b = lax.optimization_barrier((before, after, child_b))
     across, across_rest = shifted(before[:middle], 1, row_count), shifted(after[middle:], -1, row_count)
     pieces = (piece, before, after, across, across_rest)
 

time: 367 us -> 359 us (0.978)
  waiting for transfers between devices: 169 us -> 163 us
  starting transfers between devices: 44.8 us -> 39.5 us
    ppermute x8, waiting for transfers between devices: 45.2 us -> 13.8 us  [shifted(): lax.ppermute(x, 'row', [(i, (i + shift) % count) for i in range(count)])]
    all_to_all x1, waiting for transfers between devices: 0.01 us -> 25.5 us  [body(): lax.all_to_all(single.reshape(n_front * capacity, ELIMINATED), 'front', s...]
    ppermute x8, starting transfers between devices: 15 us -> 10.5 us  [shifted(): lax.ppermute(x, 'row', [(i, (i + shift) % count) for i in range(count)])]
  transfers between devices with their start and end apart: 15 -> 15, of which waited for: 7 -> 9; matrix products, arithmetic and copies ran while one was open for 3% -> 3% of each run, Pallas kernels for 29% -> 26%
where the time goes in v7:
time: 359 us; the launch traced here: 355 us
  waiting for transfers between devices  163 us (45%)
  Pallas kernels  108 us (30%)
  starting transfers between devices  39.5 us (11%)
  blocking collectives  15.7 us (4%)
  between operations  13.6 us (4%)
  local copies, waits for them, and re-layouts  8.04 us (2%)
  other arithmetic  6.9 us (2%)
    ppermute x1, waiting for transfers between devices, body(): passed_rest = lax.ppermute(own_a[split:], 'col', [(0, 1), (1, 0)])  116 us
    pallas_call x1, Pallas kernels, factor(): pl.pallas_call(factor_kernel, out_shape=(jax.ShapeDtypeStruct((ELIMINATED...  51.5 us
    all_to_all x1, waiting for transfers between devices, body(): lax.all_to_all(single.reshape(n_front * capacity, ELIMINATED), 'front', s...  25.5 us
    all_to_all x1, blocking collectives, body(): lax.all_to_all(second, 'row', split_axis=0, concat_axis=0, tiled=True)  15.7 us
    pallas_call x1, Pallas kernels, cross(): pl.pallas_call(cross_kernel, grid=(ELIMINATED // WIDE,), out_shape=jax.Sh...  14.1 us
    pallas_call x2, Pallas kernels, place(): pl.pallas_call(place_kernel, grid=(ELIMINATED // WIDE,), out_shape=jax.Sh...  14 us
    ppermute x8, waiting for transfers between devices, shifted(): lax.ppermute(x, 'row', [(i, (i + shift) % count) for i in range(count)])  13.8 us
    all_to_all x1, starting transfers between devices, body(): lax.all_to_all(single.reshape(n_front * capacity, ELIMINATED), 'front', s...  11.7 us
  transfers between devices with their start and end apart: 15, of which 9 were waited for; matrix products, arithmetic and copies ran while one was open for 3% of the time, Pallas kernels for 26%

profile of v7, /device:TPU:0, one launch (start us, length us, event | category | flops | bytes accessed | tf_op | source)
XLA Modules:
  0.0 354.7 jit_solution(8922328572263597684)
XLA Ops:
  7.6 2.1 collective-permute-start
  9.6 1.5 copy.5.stair_ref
  11.2 7.4 %shard_map.46 = f32[16,2,64,1024]{3,2,1,0:T(8,128)} custom-call(s32[1,1]{1,0:T(1,128)} %bitcast.3.first_ref, s32[1,512]{1,0:T(1,128)} %bitcast.23, s32[512,1]{1,0:T(8,128)} %copy.5.stair_ref, f32[512,2048]{1,0:T(8,128)} %rows_ref.3), custom_call_target="tpu_custom_call" | custom-call | flops 1 | bytes 1 | tf_op jit(solution)/shard_map/pallas_call | solution.py:126
  18.8 8.6 %all-to-all-start = ((f32[32,64,1024]{2,1,0:T(8,128)}), f32[32,64,1024]{2,1,0:T(8,128)}, u32[]{:S(2)}, u32[]{:S(2)}) async-start(f32[32,64,1024]{2,1,0:T(8,128)} %bitcast.14), calls=%async_computation | async-start | bytes 16777216 | tf_op jit(solution)/shard_map/all_to_all | solution.py:459
  28.4 1.7 collective-permute-start.1
  30.1 6.6 %shard_map.47 = f32[16,1,64,1024]{3,2,1,0:T(8,128)} custom-call(s32[1,1]{1,0:T(1,128)} %bitcast.6.first_ref, s32[1,512]{1,0:T(1,128)} %bitcast.24, s32[512,1]{1,0:T(8,128)} %copy.5.stair_ref, f32[512,2048]{1,0:T(8,128)} %rows_ref.3), custom_call_target="tpu_custom_call" | custom-call | flops 1 | bytes 1 | tf_op jit(solution)/shard_map/pallas_call | solution.py:126
  36.8 116.1 %collective-permute-done.1 = f32[288,1024]{1,0:T(8,128)} collective-permute-done((f32[288,1024]{1,0:T(8,128)}, f32[288,1024]{1,0:T(8,128)}, u32[]{:S(2)}, u32[]{:S(2)}) %collective-permute-start.1) | collective-permute-done | bytes 1179680 | tf_op jit(solution)/shard_map/ppermute | solution.py:452
  152.9 1.3 constant_dynamic-update-slice_fusion
  154.3 1.2 copy-done.1
  155.5 1.4 slice_select_fusion.own_ref
  156.9 10.9 %shard_map.48 = (f32[128,1280]{1,0:T(8,128)}, f32[128,1280]{1,0:T(8,128)}, f32[128,1280]{1,0:T(8,128)}, f32[64,1280]{1,0:T(8,128)}, f32[64,1280]{1,0:T(8,128)}, /*index=5*/bf16[1024,2816]{1,0:T(8,128)(2,1)}) custom-call(s32[1,1]{1,0:T(1,128)} %bitcast.1.turn_ref, f32[384,1024]{1,0:T(8,128)} %slice_select_fusion.own_ref, f32[16,2,64,1024]{3,2,1,0:T(8,128)} %bitcast.8.child_ref), custom_call_target="tpu_custom_call" | custom-call | flops 1 | bytes 1 | tf_op jit(solution)/shard_map/pallas_call | solution.py:191
  167.8 1.5 collective-permute-start.2
  169.3 1.7 collective-permute-start.3
  171.1 11.7 %all-to-all-start.1 = ((f32[16,64,1024]{2,1,0:T(8,128)}), f32[16,64,1024]{2,1,0:T(8,128)}, u32[]{:S(2)}, u32[]{:S(2)}) async-start(f32[16,64,1024]{2,1,0:T(8,128)} %bitcast.15), calls=%async_computation.1 | async-start | bytes 8388608 | tf_op jit(solution)/shard_map/all_to_all | solution.py:473
  183.0 2.2 slice_select_fusion.1.own_ref
  185.9 9.0 %shard_map.50 = f32[4,1024,128]{2,1,0:T(8,128)} custom-call(s32[1]{0:T(128)} %bitcast.11._, bf16[1024,2816]{1,0:T(8,128)(2,1)} %get-tuple-element.55.turned_ref, f32[384,512]{1,0:T(8,128)} %slice_select_fusion.1.own_ref, f32[16,2,64,1024]{3,2,1,0:T(8,128)} %bitcast.8.child_ref), custom_call_target="tpu_custom_call" | custom-call | flops 1 | bytes 1 | tf_op jit(solution)/shard_map/pallas_call | solution.py:243
  196.9 3.0 collective-permute-start.5
  201.0 5.3 %collective-permute-done.5 = f32[64,1280]{1,0:T(8,128)S(1)} collective-permute-done((f32[64,1280]{1,0:T(8,128)S(1)}, f32[64,1280]{1,0:T(8,128)S(1)}, u32[]{:S(2)}, u32[]{:S(2)}) %collective-permute-start.5) | collective-permute-done | bytes 327712 | tf_op jit(solution)/shard_map/ppermute | solution.py:437
  206.3 3.9 %collective-permute-done.4 = f32[64,1280]{1,0:T(8,128)S(1)} collective-permute-done((f32[64,1280]{1,0:T(8,128)S(1)}, f32[64,1280]{1,0:T(8,128)S(1)}, u32[]{:S(2)}, u32[]{:S(2)}) %collective-permute-start.4) | collective-permute-done | bytes 327712 | tf_op jit(solution)/shard_map/ppermute | solution.py:437
  210.2 1.2 slice_add_fusion
  211.6 2.0 collective-permute-start.6
  213.6 25.5 %all-to-all-done.1 = f32[16,64,1024]{2,1,0:T(8,128)} async-done(((f32[16,64,1024]{2,1,0:T(8,128)}), f32[16,64,1024]{2,1,0:T(8,128)}, u32[]{:S(2)}, u32[]{:S(2)}) %all-to-all-start.1) | async-done | bytes 4194336 | tf_op jit(solution)/shard_map/all_to_all | solution.py:473
  239.1 2.6 collective-permute-done.7.after_ref
  241.7 1.3 collective-permute-done.6.before_ref
  243.2 2.0 collective-permute-start.8
  245.2 14.1 %shard_map.49 = f32[4,1024,256]{2,1,0:T(8,128)} custom-call(bf16[1024,2816]{1,0:T(8,128)(2,1)} %get-tuple-element.55.turned_ref, f32[384,2048]{1,0:T(8,128)} %bitcast.17, f32[16,1,64,1024]{3,2,1,0:T(8,128)} %bitcast.10.child_ref), custom_call_target="tpu_custom_call" | custom-call | flops 1 | bytes 1 | tf_op jit(solution)/shard_map/pallas_call | solution.py:217
  260.2 51.5 %shard_map.51 = (bf16[1024,1024]{1,0:T(8,128)(2,1)}, bf16[1024,1024]{1,0:T(8,128)(2,1)}, f32[256,1024]{1,0:T(8,128)}, f32[4,2,256,128]{3,2,1,0:T(8,128)}) custom-call(s32[1,1]{1,0:T(1,128)} %bitcast.1.turn_ref, f32[128,1280]{1,0:T(8,128)} %copy-done.3, f32[128,1280]{1,0:T(8,128)} %copy-done.5, f32[128,1280]{1,0:T(8,128)} %copy-done.4, ...), custom_call_target="tpu_custom_call" | custom-call | flops 1 | bytes 1 | tf_op jit(solution)/shard_map/pallas_call | solution.py:366
  311.7 4.7 %all-to-all-start.2 = ((f32[8,256,128]{2,1,0:T(8,128)}), f32[8,256,128]{2,1,0:T(8,128)S(1)}, u32[]{:S(2)}, u32[]{:S(2)}) async-start(f32[8,256,128]{2,1,0:T(8,128)} %bitcast.22), calls=%async_computation.3 | async-start | bytes 2097152 | tf_op jit(solution)/shard_map/all_to_all | solution.py:499
  316.4 4.7 %shard_map.52 = f32[4,256,256]{2,1,0:T(8,128)} custom-call(bf16[1024,1024]{1,0:T(8,128)(2,1)} %get-tuple-element.58.high_ref, bf16[1024,1024]{1,0:T(8,128)(2,1)} %get-tuple-element.59.low_ref, f32[1,1024,256]{2,1,0:T(8,128)} %reduce-scatter.5.cloned.1.call-done.sums_ref), custom_call_target="tpu_custom_call" | custom-call | flops 1 | bytes 1 | tf_op jit(solution)/shard_map/pallas_call | solution.py:401
  321.1 7.6 %all-to-all-done.2 = f32[8,256,128]{2,1,0:T(8,128)S(1)} async-done(((f32[8,256,128]{2,1,0:T(8,128)}), f32[8,256,128]{2,1,0:T(8,128)S(1)}, u32[]{:S(2)}, u32[]{:S(2)}) %all-to-all-start.2) | async-done | bytes 1048608 | tf_op jit(solution)/shard_map/all_to_all | solution.py:499
  328.7 15.7 %all_to_all.28.second_ref = f32[4,256,256]{2,1,0:T(8,128)} all-to-all(f32[4,256,256]{2,1,0:T(8,128)} %shard_map.52), channel_id=1, replica_groups=mesh['front'=16,'row'=4,'col'=2] {'row'}, dimensions={0} | all-to-all | bytes 2097152 | tf_op jit(solution)/shard_map/all_to_all | solution.py:503
  344.4 3.4 shard_map.53
  (44 shorter events, 7.4 us)
Async XLA Ops:
  7.6 11.2 %collective-permute-start = (f32[96,1024]{1,0:T(8,128)S(1)}, f32[96,1024]{1,0:T(8,128)S(1)}, u32[]{:S(2)}, u32[]{:S(2)}) collective-permute-start(f32[96,1024]{1,0:T(8,128)S(1)} %slice.48), channel_id=1, source_target_pairs={{0,1},{1,0},{2,3},{3,2},{4,5},{5,4},{6,7},{7,6},{8,9},{9,8},{10,11... | collective-permute-start | bytes 1179656 | tf_op jit(solution)/shard_map/ppermute | solution.py:451
  18.8 8.6 %copy-start = (f32[1,384,2048]{2,1,0:T(8,128)S(1)}, f32[1,384,2048]{2,1,0:T(8,128)}, u32[]{:S(2)}) copy-start(f32[1,384,2048]{2,1,0:T(8,128)} %param.4) | copy-start | bytes 9437188
  18.8 138.1 %all-to-all-start = ((f32[32,64,1024]{2,1,0:T(8,128)}), f32[32,64,1024]{2,1,0:T(8,128)}, u32[]{:S(2)}, u32[]{:S(2)}) async-start(f32[32,64,1024]{2,1,0:T(8,128)} %bitcast.14), calls=%async_computation | async-start | bytes 16777216 | tf_op jit(solution)/shard_map/all_to_all | solution.py:459
  28.4 124.5 %collective-permute-start.1 = (f32[288,1024]{1,0:T(8,128)}, f32[288,1024]{1,0:T(8,128)}, u32[]{:S(2)}, u32[]{:S(2)}) collective-permute-start(f32[288,1024]{1,0:T(8,128)} %slice.49), channel_id=1, source_target_pairs={{0,1},{1,0},{2,3},{3,2},{4,5},{5,4},{6,7},{7,6},{8,9},{9,8},{10,11... | collective-permute-start | bytes 3538952 | tf_op jit(solution)/shard_map/ppermute | solution.py:452
  154.3 1.2 copy-start.1
  167.8 18.0 %collective-permute-start.2 = (f32[128,1280]{1,0:T(8,128)}, f32[128,1280]{1,0:T(8,128)}, u32[]{:S(2)}, u32[]{:S(2)}) collective-permute-start(f32[128,1280]{1,0:T(8,128)} %get-tuple-element.38), channel_id=1, source_target_pairs={{0,2},{2,4},{4,6},{6,0},{1,3},{3,5},{5,7},{7,1},{8,10},{10,12},{12... | collective-permute-start | bytes 1966088 | tf_op jit(solution)/shard_map/ppermute | solution.py:437
  169.3 16.5 %collective-permute-start.3 = (f32[128,1280]{1,0:T(8,128)}, f32[128,1280]{1,0:T(8,128)}, u32[]{:S(2)}, u32[]{:S(2)}) collective-permute-start(f32[128,1280]{1,0:T(8,128)} %get-tuple-element.39), channel_id=1, source_target_pairs={{0,6},{2,0},{4,2},{6,4},{1,7},{3,1},{5,3},{7,5},{8,14},{10,8},{12,... | collective-permute-start | bytes 1966088 | tf_op jit(solution)/shard_map/ppermute | solution.py:437
  171.1 68.1 %all-to-all-start.1 = ((f32[16,64,1024]{2,1,0:T(8,128)}), f32[16,64,1024]{2,1,0:T(8,128)}, u32[]{:S(2)}, u32[]{:S(2)}) async-start(f32[16,64,1024]{2,1,0:T(8,128)} %bitcast.15), calls=%async_computation.1 | async-start | bytes 8388608 | tf_op jit(solution)/shard_map/all_to_all | solution.py:473
  182.8 77.4 %reduce-scatter.3.cloned.1.call-start = ((), (), s32[]{:S(2)}) async-start(), calls=%async_computation.6 | async-start | bytes 2621440 | tf_op jit(solution)/shard_map/reduce_scatter | solution.py:494
  194.9 1.0 copy-start.8
  194.9 5.0 %copy-start.7 = (f32[64,1280]{1,0:T(8,128)S(1)}, f32[64,1280]{1,0:T(8,128)}, u32[]{:S(2)}) copy-start(f32[64,1280]{1,0:T(8,128)} %get-tuple-element.37) | copy-start | bytes 983044
  194.9 16.5 %copy-start.6 = (f32[128,1280]{1,0:T(8,128)S(1)}, f32[128,1280]{1,0:T(8,128)}, u32[]{:S(2)}) copy-start(f32[128,1280]{1,0:T(8,128)} %get-tuple-element.36) | copy-start | bytes 1966084
  194.9 121.5 %reduce-scatter.5.cloned.1.call-start = ((), (), s32[]{:S(2)}) async-start(), calls=%async_computation.7 | async-start | bytes 5242880 | tf_op jit(solution)/shard_map/reduce_scatter | solution.py:494
  196.9 9.4 %collective-permute-start.5 = (f32[64,1280]{1,0:T(8,128)S(1)}, f32[64,1280]{1,0:T(8,128)S(1)}, u32[]{:S(2)}, u32[]{:S(2)}) collective-permute-start(f32[64,1280]{1,0:T(8,128)S(1)} %slice_add_fusion.2), channel_id=1, source_target_pairs={{0,6},{2,0},{4,2},{6,4},{1,7},{3,1},{5,3},{7,5},{8,14},{10,8},{12,... | collective-permute-start | bytes 983048 | tf_op jit(solution)/shard_map/ppermute | solution.py:437
  200.9 9.3 %collective-permute-start.4 = (f32[64,1280]{1,0:T(8,128)S(1)}, f32[64,1280]{1,0:T(8,128)S(1)}, u32[]{:S(2)}, u32[]{:S(2)}) collective-permute-start(f32[64,1280]{1,0:T(8,128)S(1)} %slice_add_fusion.3), channel_id=1, source_target_pairs={{0,2},{2,4},{4,6},{6,0},{1,3},{3,5},{5,7},{7,1},{8,10},{10,12},{12... | collective-permute-start | bytes 983048 | tf_op jit(solution)/shard_map/ppermute | solution.py:437
  211.5 47.8 %copy-start.3 = (f32[128,1280]{1,0:T(8,128)}, f32[128,1280]{1,0:T(8,128)S(1)}, u32[]{:S(2)}) copy-start(f32[128,1280]{1,0:T(8,128)S(1)} %maximum_add_fusion.piece_ref) | copy-start | bytes 1966084
  211.5 30.2 %collective-permute-start.7 = (f32[128,1280]{1,0:T(8,128)S(1)}, f32[128,1280]{1,0:T(8,128)S(1)}, u32[]{:S(2)}, u32[]{:S(2)}) collective-permute-start(f32[128,1280]{1,0:T(8,128)S(1)} %maximum_add_fusion.piece_ref), channel_id=1, source_target_pairs={{0,6},{2,0},{4,2},{6,4},{1,7},{3,1},{5,3},{7,5},{8,14},{10,8},{12,... | collective-permute-start | bytes 1966088 | tf_op jit(solution)/shard_map/ppermute | solution.py:437
  211.6 31.4 %collective-permute-start.6 = (f32[128,1280]{1,0:T(8,128)S(1)}, f32[128,1280]{1,0:T(8,128)S(1)}, u32[]{:S(2)}, u32[]{:S(2)}) collective-permute-start(f32[128,1280]{1,0:T(8,128)S(1)} %maximum_add_fusion.piece_ref), channel_id=1, source_target_pairs={{0,2},{2,4},{4,6},{6,0},{1,3},{3,5},{5,7},{7,1},{8,10},{10,12},{12... | collective-permute-start | bytes 1966088 | tf_op jit(solution)/shard_map/ppermute | solution.py:437
  241.7 17.6 %copy-start.4 = (f32[128,1280]{1,0:T(8,128)}, f32[128,1280]{1,0:T(8,128)S(1)}, u32[]{:S(2)}) copy-start(f32[128,1280]{1,0:T(8,128)S(1)} %collective-permute-done.7.after_ref) | copy-start | bytes 1966084
  243.0 16.3 %copy-start.5 = (f32[128,1280]{1,0:T(8,128)}, f32[128,1280]{1,0:T(8,128)S(1)}, u32[]{:S(2)}) copy-start(f32[128,1280]{1,0:T(8,128)S(1)} %collective-permute-done.6.before_ref) | copy-start | bytes 1966084
  243.1 16.2 %collective-permute-start.9 = (f32[64,1280]{1,0:T(8,128)S(1)}, f32[64,1280]{1,0:T(8,128)S(1)}, u32[]{:S(2)}, u32[]{:S(2)}) collective-permute-start(f32[64,1280]{1,0:T(8,128)S(1)} %slice.44), channel_id=1, source_target_pairs={{0,6},{2,0},{4,2},{6,4},{1,7},{3,1},{5,3},{7,5},{8,14},{10,8},{12,... | collective-permute-start | bytes 983048 | tf_op jit(solution)/shard_map/ppermute | solution.py:437
  243.2 16.2 %collective-permute-start.8 = (f32[64,1280]{1,0:T(8,128)S(1)}, f32[64,1280]{1,0:T(8,128)S(1)}, u32[]{:S(2)}, u32[]{:S(2)}) collective-permute-start(f32[64,1280]{1,0:T(8,128)S(1)} %slice.43), channel_id=1, source_target_pairs={{0,2},{2,4},{4,6},{6,0},{1,3},{3,5},{5,7},{7,1},{8,10},{10,12},{12... | collective-permute-start | bytes 983048 | tf_op jit(solution)/shard_map/ppermute | solution.py:437
  259.3 0.8 copy-start.9
  259.3 0.9 copy-start.10
  311.7 17.0 %all-to-all-start.2 = ((f32[8,256,128]{2,1,0:T(8,128)}), f32[8,256,128]{2,1,0:T(8,128)S(1)}, u32[]{:S(2)}, u32[]{:S(2)}) async-start(f32[8,256,128]{2,1,0:T(8,128)} %bitcast.22), calls=%async_computation.3 | async-start | bytes 2097152 | tf_op jit(solution)/shard_map/all_to_all | solution.py:499
  328.7 15.7 %copy-start.2 = (f32[8,256,128]{2,1,0:T(8,128)}, f32[8,256,128]{2,1,0:T(8,128)S(1)}, u32[]{:S(2)}) copy-start(f32[8,256,128]{2,1,0:T(8,128)S(1)} %all-to-all-done.2) | copy-start | bytes 3145732
Sparse Core Ops, SparseCore 0:
  195.0 49.8 reduce-scatter.2
  259.5 49.6 reduce-scatter.4

commit v8 on v7

--- a/solution.py
+++ b/solution.py
@@ -31,18 +31,29 @@
             [jnp.broadcast_to(column[t][i : i + 1, :], (LINES, BLK)) for t in range(i + 1)]
             for i in range(LINES)
         ]
+        unit = [lax.rsqrt(entry[t][t]) for t in range(LINES)]
+        for i in range(LINES):
+            for t in range(i + 1):
+                entry[i][t] = entry[i][t] * unit[i] * unit[t]
         scale = []
-        for t in range(LINES):
-            scale.append(lax.rsqrt(entry[t][t]))
+        for t in range(0, LINES, 2):
+            top, side, last = entry[t][t], entry[t + 1][t], entry[t + 1][t + 1]
+            root = lax.rsqrt(top)
+            scale.append(root)
+            scale.append(top * root * lax.rsqrt(top * last - side * side))
             for i in range(t + 1, LINES):
-                entry[i][t] = entry[i][t] * scale[t]
-            for u in range(t + 1, LINES):
+                entry[i][t] = entry[i][t] * root
+            for i in range(t + 2, LINES):
+                entry[i][t + 1] = (entry[i][t + 1] - entry[i][t] * entry[t + 1][t]) * scale[t + 1]
+            for u in range(t + 2, LINES):
                 for i in range(u, LINES):
-                    entry[i][u] = entry[i][u] - entry[i][t] * entry[u][t]
+                    entry[i][u] = (
+                        entry[i][u] - entry[i][t] * entry[u][t] - entry[i][t + 1] * entry[u][t + 1]
+                    )
         solved = []
         augmented = jnp.where(within, jnp.where(lane == sublane + first, 1.0, 0.0), strip)
         for t in range(LINES):
-            line = jnp.broadcast_to(augmented[t : t + 1, :], (LINES, BLK))
+            line = jnp.broadcast_to(augmented[t : t + 1, :], (LINES, BLK)) * unit[t]
             for s in range(t):
                 line = line - entry[t][s] * solved[s]
             solved.append(line * scale[t])
@@ -56,7 +67,7 @@
             rest = jnp.where(within, 0.0, below)
             factors = []
             for t in range(LINES):
-                value = jnp.broadcast_to(below[:, first + t : first + t + 1], (LINES, BLK))
+                value = jnp.broadcast_to(below[:, first + t : first + t + 1], (LINES, BLK)) * unit[t]
                 for s in range(t):
                     value = value - entry[t][s] * factors[s]
                 value = value * scale[t]

time: 359 us -> 358 us (level)
  no operation moved by 1% of the time
where the time goes in v8:
time: 358 us; the launch traced here: 354 us
  waiting for transfers between devices  163 us (46%)
  Pallas kernels  108 us (30%)
  starting transfers between devices  39.5 us (11%)
  blocking collectives  15.7 us (4%)
  between operations  13.6 us (4%)
  local copies, waits for them, and re-layouts  8.04 us (2%)
  other arithmetic  6.9 us (2%)
    ppermute x1, waiting for transfers between devices, body(): passed_rest = lax.ppermute(own_a[split:], 'col', [(0, 1), (1, 0)])  116 us
    pallas_call x1, Pallas kernels, factor(): pl.pallas_call(factor_kernel, out_shape=(jax.ShapeDtypeStruct((ELIMINATED...  51.3 us
    all_to_all x1, waiting for transfers between devices, body(): lax.all_to_all(single.reshape(n_front * capacity, ELIMINATED), 'front', s...  25.5 us
    all_to_all x1, blocking collectives, body(): lax.all_to_all(second, 'row', split_axis=0, concat_axis=0, tiled=True)  15.7 us
    pallas_call x1, Pallas kernels, cross(): pl.pallas_call(cross_kernel, grid=(ELIMINATED // WIDE,), out_shape=jax.Sh...  14.1 us
    pallas_call x2, Pallas kernels, place(): pl.pallas_call(place_kernel, grid=(ELIMINATED // WIDE,), out_shape=jax.Sh...  14 us
    ppermute x8, waiting for transfers between devices, shifted(): lax.ppermute(x, 'row', [(i, (i + shift) % count) for i in range(count)])  13.8 us
    all_to_all x1, starting transfers between devices, body(): lax.all_to_all(single.reshape(n_front * capacity, ELIMINATED), 'front', s...  11.7 us
  transfers between devices with their start and end apart: 15, of which 9 were waited for; matrix products, arithmetic and copies ran while one was open for 3% of the time, Pallas kernels for 26%

profile of v8, /device:TPU:0, one launch (start us, length us, event | category | flops | bytes accessed | tf_op | source)
XLA Modules:
  0.0 354.4 jit_solution(17023376906293220172)
XLA Ops:
  7.6 2.1 collective-permute-start
  9.6 1.5 copy.5.stair_ref
  11.2 7.4 %shard_map.46 = f32[16,2,64,1024]{3,2,1,0:T(8,128)} custom-call(s32[1,1]{1,0:T(1,128)} %bitcast.3.first_ref, s32[1,512]{1,0:T(1,128)} %bitcast.23, s32[512,1]{1,0:T(8,128)} %copy.5.stair_ref, f32[512,2048]{1,0:T(8,128)} %rows_ref.3), custom_call_target="tpu_custom_call" | custom-call | flops 1 | bytes 1 | tf_op jit(solution)/shard_map/pallas_call | solution.py:137
  18.8 8.6 %all-to-all-start = ((f32[32,64,1024]{2,1,0:T(8,128)}), f32[32,64,1024]{2,1,0:T(8,128)}, u32[]{:S(2)}, u32[]{:S(2)}) async-start(f32[32,64,1024]{2,1,0:T(8,128)} %bitcast.14), calls=%async_computation | async-start | bytes 16777216 | tf_op jit(solution)/shard_map/all_to_all | solution.py:470
  28.4 1.7 collective-permute-start.1
  30.1 6.6 %shard_map.47 = f32[16,1,64,1024]{3,2,1,0:T(8,128)} custom-call(s32[1,1]{1,0:T(1,128)} %bitcast.6.first_ref, s32[1,512]{1,0:T(1,128)} %bitcast.24, s32[512,1]{1,0:T(8,128)} %copy.5.stair_ref, f32[512,2048]{1,0:T(8,128)} %rows_ref.3), custom_call_target="tpu_custom_call" | custom-call | flops 1 | bytes 1 | tf_op jit(solution)/shard_map/pallas_call | solution.py:137
  36.8 116.1 %collective-permute-done.1 = f32[288,1024]{1,0:T(8,128)} collective-permute-done((f32[288,1024]{1,0:T(8,128)}, f32[288,1024]{1,0:T(8,128)}, u32[]{:S(2)}, u32[]{:S(2)}) %collective-permute-start.1) | collective-permute-done | bytes 1179680 | tf_op jit(solution)/shard_map/ppermute | solution.py:463
  152.9 1.3 constant_dynamic-update-slice_fusion
  154.3 1.2 copy-done.1
  155.5 1.4 slice_select_fusion.own_ref
  156.9 10.9 %shard_map.48 = (f32[128,1280]{1,0:T(8,128)}, f32[128,1280]{1,0:T(8,128)}, f32[128,1280]{1,0:T(8,128)}, f32[64,1280]{1,0:T(8,128)}, f32[64,1280]{1,0:T(8,128)}, /*index=5*/bf16[1024,2816]{1,0:T(8,128)(2,1)}) custom-call(s32[1,1]{1,0:T(1,128)} %bitcast.1.turn_ref, f32[384,1024]{1,0:T(8,128)} %slice_select_fusion.own_ref, f32[16,2,64,1024]{3,2,1,0:T(8,128)} %bitcast.8.child_ref), custom_call_target="tpu_custom_call" | custom-call | flops 1 | bytes 1 | tf_op jit(solution)/shard_map/pallas_call | solution.py:202
  167.8 1.5 collective-permute-start.2
  169.3 1.7 collective-permute-start.3
  171.1 11.7 %all-to-all-start.1 = ((f32[16,64,1024]{2,1,0:T(8,128)}), f32[16,64,1024]{2,1,0:T(8,128)}, u32[]{:S(2)}, u32[]{:S(2)}) async-start(f32[16,64,1024]{2,1,0:T(8,128)} %bitcast.15), calls=%async_computation.1 | async-start | bytes 8388608 | tf_op jit(solution)/shard_map/all_to_all | solution.py:484
  183.0 2.2 slice_select_fusion.1.own_ref
  185.9 9.0 %shard_map.50 = f32[4,1024,128]{2,1,0:T(8,128)} custom-call(s32[1]{0:T(128)} %bitcast.11._, bf16[1024,2816]{1,0:T(8,128)(2,1)} %get-tuple-element.55.turned_ref, f32[384,512]{1,0:T(8,128)} %slice_select_fusion.1.own_ref, f32[16,2,64,1024]{3,2,1,0:T(8,128)} %bitcast.8.child_ref), custom_call_target="tpu_custom_call" | custom-call | flops 1 | bytes 1 | tf_op jit(solution)/shard_map/pallas_call | solution.py:254
  196.9 3.0 collective-permute-start.5
  201.0 5.3 %collective-permute-done.5 = f32[64,1280]{1,0:T(8,128)S(1)} collective-permute-done((f32[64,1280]{1,0:T(8,128)S(1)}, f32[64,1280]{1,0:T(8,128)S(1)}, u32[]{:S(2)}, u32[]{:S(2)}) %collective-permute-start.5) | collective-permute-done | bytes 327712 | tf_op jit(solution)/shard_map/ppermute | solution.py:448
  206.3 3.9 %collective-permute-done.4 = f32[64,1280]{1,0:T(8,128)S(1)} collective-permute-done((f32[64,1280]{1,0:T(8,128)S(1)}, f32[64,1280]{1,0:T(8,128)S(1)}, u32[]{:S(2)}, u32[]{:S(2)}) %collective-permute-start.4) | collective-permute-done | bytes 327712 | tf_op jit(solution)/shard_map/ppermute | solution.py:448
  210.2 1.2 slice_add_fusion
  211.6 2.0 collective-permute-start.6
  213.6 25.5 %all-to-all-done.1 = f32[16,64,1024]{2,1,0:T(8,128)} async-done(((f32[16,64,1024]{2,1,0:T(8,128)}), f32[16,64,1024]{2,1,0:T(8,128)}, u32[]{:S(2)}, u32[]{:S(2)}) %all-to-all-start.1) | async-done | bytes 4194336 | tf_op jit(solution)/shard_map/all_to_all | solution.py:484
  239.1 2.6 collective-permute-done.7.after_ref
  241.7 1.3 collective-permute-done.6.before_ref
  243.2 2.0 collective-permute-start.8
  245.2 14.1 %shard_map.49 = f32[4,1024,256]{2,1,0:T(8,128)} custom-call(bf16[1024,2816]{1,0:T(8,128)(2,1)} %get-tuple-element.55.turned_ref, f32[384,2048]{1,0:T(8,128)} %bitcast.17, f32[16,1,64,1024]{3,2,1,0:T(8,128)} %bitcast.10.child_ref), custom_call_target="tpu_custom_call" | custom-call | flops 1 | bytes 1 | tf_op jit(solution)/shard_map/pallas_call | solution.py:228
  260.2 51.3 %shard_map.51 = (bf16[1024,1024]{1,0:T(8,128)(2,1)}, bf16[1024,1024]{1,0:T(8,128)(2,1)}, f32[256,1024]{1,0:T(8,128)}, f32[4,2,256,128]{3,2,1,0:T(8,128)}) custom-call(s32[1,1]{1,0:T(1,128)} %bitcast.1.turn_ref, f32[128,1280]{1,0:T(8,128)} %copy-done.3, f32[128,1280]{1,0:T(8,128)} %copy-done.5, f32[128,1280]{1,0:T(8,128)} %copy-done.4, ...), custom_call_target="tpu_custom_call" | custom-call | flops 1 | bytes 1 | tf_op jit(solution)/shard_map/pallas_call | solution.py:377
  311.5 4.7 %all-to-all-start.2 = ((f32[8,256,128]{2,1,0:T(8,128)}), f32[8,256,128]{2,1,0:T(8,128)S(1)}, u32[]{:S(2)}, u32[]{:S(2)}) async-start(f32[8,256,128]{2,1,0:T(8,128)} %bitcast.22), calls=%async_computation.3 | async-start | bytes 2097152 | tf_op jit(solution)/shard_map/all_to_all | solution.py:510
  316.2 4.7 %shard_map.52 = f32[4,256,256]{2,1,0:T(8,128)} custom-call(bf16[1024,1024]{1,0:T(8,128)(2,1)} %get-tuple-element.58.high_ref, bf16[1024,1024]{1,0:T(8,128)(2,1)} %get-tuple-element.59.low_ref, f32[1,1024,256]{2,1,0:T(8,128)} %reduce-scatter.5.cloned.1.call-done.sums_ref), custom_call_target="tpu_custom_call" | custom-call | flops 1 | bytes 1 | tf_op jit(solution)/shard_map/pallas_call | solution.py:412
  320.9 7.6 %all-to-all-done.2 = f32[8,256,128]{2,1,0:T(8,128)S(1)} async-done(((f32[8,256,128]{2,1,0:T(8,128)}), f32[8,256,128]{2,1,0:T(8,128)S(1)}, u32[]{:S(2)}, u32[]{:S(2)}) %all-to-all-start.2) | async-done | bytes 1048608 | tf_op jit(solution)/shard_map/all_to_all | solution.py:510
  328.5 15.7 %all_to_all.28.second_ref = f32[4,256,256]{2,1,0:T(8,128)} all-to-all(f32[4,256,256]{2,1,0:T(8,128)} %shard_map.52), channel_id=1, replica_groups=mesh['front'=16,'row'=4,'col'=2] {'row'}, dimensions={0} | all-to-all | bytes 2097152 | tf_op jit(solution)/shard_map/all_to_all | solution.py:514
  344.2 3.4 shard_map.53
  (44 shorter events, 7.4 us)
Async XLA Ops:
  7.6 11.2 %collective-permute-start = (f32[96,1024]{1,0:T(8,128)S(1)}, f32[96,1024]{1,0:T(8,128)S(1)}, u32[]{:S(2)}, u32[]{:S(2)}) collective-permute-start(f32[96,1024]{1,0:T(8,128)S(1)} %slice.48), channel_id=1, source_target_pairs={{0,1},{1,0},{2,3},{3,2},{4,5},{5,4},{6,7},{7,6},{8,9},{9,8},{10,11... | collective-permute-start | bytes 1179656 | tf_op jit(solution)/shard_map/ppermute | solution.py:462
  18.8 8.6 %copy-start = (f32[1,384,2048]{2,1,0:T(8,128)S(1)}, f32[1,384,2048]{2,1,0:T(8,128)}, u32[]{:S(2)}) copy-start(f32[1,384,2048]{2,1,0:T(8,128)} %param.4) | copy-start | bytes 9437188
  18.8 138.1 %all-to-all-start = ((f32[32,64,1024]{2,1,0:T(8,128)}), f32[32,64,1024]{2,1,0:T(8,128)}, u32[]{:S(2)}, u32[]{:S(2)}) async-start(f32[32,64,1024]{2,1,0:T(8,128)} %bitcast.14), calls=%async_computation | async-start | bytes 16777216 | tf_op jit(solution)/shard_map/all_to_all | solution.py:470
  28.4 124.5 %collective-permute-start.1 = (f32[288,1024]{1,0:T(8,128)}, f32[288,1024]{1,0:T(8,128)}, u32[]{:S(2)}, u32[]{:S(2)}) collective-permute-start(f32[288,1024]{1,0:T(8,128)} %slice.49), channel_id=1, source_target_pairs={{0,1},{1,0},{2,3},{3,2},{4,5},{5,4},{6,7},{7,6},{8,9},{9,8},{10,11... | collective-permute-start | bytes 3538952 | tf_op jit(solution)/shard_map/ppermute | solution.py:463
  154.3 1.2 copy-start.1
  167.8 18.0 %collective-permute-start.2 = (f32[128,1280]{1,0:T(8,128)}, f32[128,1280]{1,0:T(8,128)}, u32[]{:S(2)}, u32[]{:S(2)}) collective-permute-start(f32[128,1280]{1,0:T(8,128)} %get-tuple-element.38), channel_id=1, source_target_pairs={{0,2},{2,4},{4,6},{6,0},{1,3},{3,5},{5,7},{7,1},{8,10},{10,12},{12... | collective-permute-start | bytes 1966088 | tf_op jit(solution)/shard_map/ppermute | solution.py:448
  169.3 16.5 %collective-permute-start.3 = (f32[128,1280]{1,0:T(8,128)}, f32[128,1280]{1,0:T(8,128)}, u32[]{:S(2)}, u32[]{:S(2)}) collective-permute-start(f32[128,1280]{1,0:T(8,128)} %get-tuple-element.39), channel_id=1, source_target_pairs={{0,6},{2,0},{4,2},{6,4},{1,7},{3,1},{5,3},{7,5},{8,14},{10,8},{12,... | collective-permute-start | bytes 1966088 | tf_op jit(solution)/shard_map/ppermute | solution.py:448
  171.1 68.1 %all-to-all-start.1 = ((f32[16,64,1024]{2,1,0:T(8,128)}), f32[16,64,1024]{2,1,0:T(8,128)}, u32[]{:S(2)}, u32[]{:S(2)}) async-start(f32[16,64,1024]{2,1,0:T(8,128)} %bitcast.15), calls=%async_computation.1 | async-start | bytes 8388608 | tf_op jit(solution)/shard_map/all_to_all | solution.py:484
  182.8 77.4 %reduce-scatter.3.cloned.1.call-start = ((), (), s32[]{:S(2)}) async-start(), calls=%async_computation.6 | async-start | bytes 2621440 | tf_op jit(solution)/shard_map/reduce_scatter | solution.py:505
  194.9 1.0 copy-start.8
  194.9 5.0 %copy-start.7 = (f32[64,1280]{1,0:T(8,128)S(1)}, f32[64,1280]{1,0:T(8,128)}, u32[]{:S(2)}) copy-start(f32[64,1280]{1,0:T(8,128)} %get-tuple-element.37) | copy-start | bytes 983044
  194.9 16.5 %copy-start.6 = (f32[128,1280]{1,0:T(8,128)S(1)}, f32[128,1280]{1,0:T(8,128)}, u32[]{:S(2)}) copy-start(f32[128,1280]{1,0:T(8,128)} %get-tuple-element.36) | copy-start | bytes 1966084
  194.9 121.2 %reduce-scatter.5.cloned.1.call-start = ((), (), s32[]{:S(2)}) async-start(), calls=%async_computation.7 | async-start | bytes 5242880 | tf_op jit(solution)/shard_map/reduce_scatter | solution.py:505
  196.9 9.4 %collective-permute-start.5 = (f32[64,1280]{1,0:T(8,128)S(1)}, f32[64,1280]{1,0:T(8,128)S(1)}, u32[]{:S(2)}, u32[]{:S(2)}) collective-permute-start(f32[64,1280]{1,0:T(8,128)S(1)} %slice_add_fusion.2), channel_id=1, source_target_pairs={{0,6},{2,0},{4,2},{6,4},{1,7},{3,1},{5,3},{7,5},{8,14},{10,8},{12,... | collective-permute-start | bytes 983048 | tf_op jit(solution)/shard_map/ppermute | solution.py:448
  200.9 9.3 %collective-permute-start.4 = (f32[64,1280]{1,0:T(8,128)S(1)}, f32[64,1280]{1,0:T(8,128)S(1)}, u32[]{:S(2)}, u32[]{:S(2)}) collective-permute-start(f32[64,1280]{1,0:T(8,128)S(1)} %slice_add_fusion.3), channel_id=1, source_target_pairs={{0,2},{2,4},{4,6},{6,0},{1,3},{3,5},{5,7},{7,1},{8,10},{10,12},{12... | collective-permute-start | bytes 983048 | tf_op jit(solution)/shard_map/ppermute | solution.py:448
  211.5 47.8 %copy-start.3 = (f32[128,1280]{1,0:T(8,128)}, f32[128,1280]{1,0:T(8,128)S(1)}, u32[]{:S(2)}) copy-start(f32[128,1280]{1,0:T(8,128)S(1)} %maximum_add_fusion.piece_ref) | copy-start | bytes 1966084
  211.5 30.2 %collective-permute-start.7 = (f32[128,1280]{1,0:T(8,128)S(1)}, f32[128,1280]{1,0:T(8,128)S(1)}, u32[]{:S(2)}, u32[]{:S(2)}) collective-permute-start(f32[128,1280]{1,0:T(8,128)S(1)} %maximum_add_fusion.piece_ref), channel_id=1, source_target_pairs={{0,6},{2,0},{4,2},{6,4},{1,7},{3,1},{5,3},{7,5},{8,14},{10,8},{12,... | collective-permute-start | bytes 1966088 | tf_op jit(solution)/shard_map/ppermute | solution.py:448
  211.6 31.4 %collective-permute-start.6 = (f32[128,1280]{1,0:T(8,128)S(1)}, f32[128,1280]{1,0:T(8,128)S(1)}, u32[]{:S(2)}, u32[]{:S(2)}) collective-permute-start(f32[128,1280]{1,0:T(8,128)S(1)} %maximum_add_fusion.piece_ref), channel_id=1, source_target_pairs={{0,2},{2,4},{4,6},{6,0},{1,3},{3,5},{5,7},{7,1},{8,10},{10,12},{12... | collective-permute-start | bytes 1966088 | tf_op jit(solution)/shard_map/ppermute | solution.py:448
  241.7 17.6 %copy-start.4 = (f32[128,1280]{1,0:T(8,128)}, f32[128,1280]{1,0:T(8,128)S(1)}, u32[]{:S(2)}) copy-start(f32[128,1280]{1,0:T(8,128)S(1)} %collective-permute-done.7.after_ref) | copy-start | bytes 1966084
  243.0 16.3 %copy-start.5 = (f32[128,1280]{1,0:T(8,128)}, f32[128,1280]{1,0:T(8,128)S(1)}, u32[]{:S(2)}) copy-start(f32[128,1280]{1,0:T(8,128)S(1)} %collective-permute-done.6.before_ref) | copy-start | bytes 1966084
  243.1 16.2 %collective-permute-start.9 = (f32[64,1280]{1,0:T(8,128)S(1)}, f32[64,1280]{1,0:T(8,128)S(1)}, u32[]{:S(2)}, u32[]{:S(2)}) collective-permute-start(f32[64,1280]{1,0:T(8,128)S(1)} %slice.44), channel_id=1, source_target_pairs={{0,6},{2,0},{4,2},{6,4},{1,7},{3,1},{5,3},{7,5},{8,14},{10,8},{12,... | collective-permute-start | bytes 983048 | tf_op jit(solution)/shard_map/ppermute | solution.py:448
  243.2 16.2 %collective-permute-start.8 = (f32[64,1280]{1,0:T(8,128)S(1)}, f32[64,1280]{1,0:T(8,128)S(1)}, u32[]{:S(2)}, u32[]{:S(2)}) collective-permute-start(f32[64,1280]{1,0:T(8,128)S(1)} %slice.43), channel_id=1, source_target_pairs={{0,2},{2,4},{4,6},{6,0},{1,3},{3,5},{5,7},{7,1},{8,10},{10,12},{12... | collective-permute-start | bytes 983048 | tf_op jit(solution)/shard_map/ppermute | solution.py:448
  259.3 0.8 copy-start.9
  259.3 0.9 copy-start.10
  311.5 17.0 %all-to-all-start.2 = ((f32[8,256,128]{2,1,0:T(8,128)}), f32[8,256,128]{2,1,0:T(8,128)S(1)}, u32[]{:S(2)}, u32[]{:S(2)}) async-start(f32[8,256,128]{2,1,0:T(8,128)} %bitcast.22), calls=%async_computation.3 | async-start | bytes 2097152 | tf_op jit(solution)/shard_map/all_to_all | solution.py:510
  328.5 15.7 %copy-start.2 = (f32[8,256,128]{2,1,0:T(8,128)}, f32[8,256,128]{2,1,0:T(8,128)S(1)}, u32[]{:S(2)}) copy-start(f32[8,256,128]{2,1,0:T(8,128)S(1)} %all-to-all-done.2) | copy-start | bytes 3145732
Sparse Core Ops, SparseCore 0:
  195.0 49.8 reduce-scatter.2
  259.5 49.6 reduce-scatter.4

commit v9 on v7

--- a/solution.py
+++ b/solution.py
@@ -485,16 +485,16 @@
     piece = mine + jnp.concatenate(
         [rest_left + from_right[middle:], from_left[middle:] + rest_right], axis=0
     )
+    piece, child_b = lax.optimization_barrier((piece, child_b))
+    products_b = cross(turned, own, ELIMINATED, child_b, 0)
     before, after = shifted(piece, 1, row_count), shifted(piece, -1, row_count)
-    before, after, child_b = lax.optimization_barrier((before, after, child_b))
+    before, after, products_b = lax.optimization_barrier((before, after, products_b))
     across, across_rest = shifted(before[:middle], 1, row_count), shifted(after[middle:], -1, row_count)
     pieces = (piece, before, after, across, across_rest)
 
     def summed(products):
         return lax.psum_scatter(products, "row", scatter_dimension=0, tiled=True)
 
-    products_b = cross(turned, own, ELIMINATED, child_b, 0)
-    pieces, products_b = lax.optimization_barrier((pieces, products_b))
     inverse_high, inverse_low, leading, first = factor(turn, *pieces, summed(products_a))
     first = lax.all_to_all(
         first.reshape(2 * row_count, quarter, BLK), ("row", "col"), split_axis=0, concat_axis=0, tiled=True

time: 359 us -> 367 us (1.022)
  waiting for transfers between devices: 163 us -> 173 us
    ppermute x8, waiting for transfers between devices: 13.8 us -> 21.1 us  [shifted(): lax.ppermute(x, 'row', [(i, (i + shift) % count) for i in range(count)])]
  transfers between devices with their start and end apart: 15 -> 15, of which waited for: 9 -> 11; matrix products, arithmetic and copies ran while one was open for 3% -> 3% of each run, Pallas kernels for 26% -> 26%
where the time goes in v9:
time: 367 us; the launch traced here: 365 us
  waiting for transfers between devices  173 us (47%)
  Pallas kernels  108 us (29%)
  starting transfers between devices  39.6 us (11%)
  blocking collectives  15.8 us (4%)
  between operations  13.6 us (4%)
  local copies, waits for them, and re-layouts  8.74 us (2%)
  other arithmetic  6.9 us (2%)
    ppermute x1, waiting for transfers between devices, body(): passed_rest = lax.ppermute(own_a[split:], 'col', [(0, 1), (1, 0)])  116 us
    pallas_call x1, Pallas kernels, factor(): pl.pallas_call(factor_kernel, out_shape=(jax.ShapeDtypeStruct((ELIMINATED...  51.6 us
    all_to_all x1, waiting for transfers between devices, body(): lax.all_to_all(single.reshape(n_front * capacity, ELIMINATED), 'front', s...  27.6 us
    ppermute x8, waiting for transfers between devices, shifted(): lax.ppermute(x, 'row', [(i, (i + shift) % count) for i in range(count)])  21.1 us
    all_to_all x1, blocking collectives, body(): lax.all_to_all(second, 'row', split_axis=0, concat_axis=0, tiled=True)  15.8 us
    pallas_call x2, Pallas kernels, place(): pl.pallas_call(place_kernel, grid=(ELIMINATED // WIDE,), out_shape=jax.Sh...  14 us
    pallas_call x1, Pallas kernels, cross(): pl.pallas_call(cross_kernel, grid=(ELIMINATED // WIDE,), out_shape=jax.Sh...  14 us
    all_to_all x1, starting transfers between devices, body(): lax.all_to_all(single.reshape(n_front * capacity, ELIMINATED), 'front', s...  11.7 us
  transfers between devices with their start and end apart: 15, of which 11 were waited for; matrix products, arithmetic and copies ran while one was open for 3% of the time, Pallas kernels for 26%

profile of v9, /device:TPU:0, one launch (start us, length us, event | category | flops | bytes accessed | tf_op | source)
XLA Modules:
  0.0 365.0 jit_solution(29450373534277892)
XLA Ops:
  7.6 2.1 collective-permute-start
  9.6 1.5 copy.5.stair_ref
  11.2 7.4 %shard_map.46 = f32[16,2,64,1024]{3,2,1,0:T(8,128)} custom-call(s32[1,1]{1,0:T(1,128)} %bitcast.3.first_ref, s32[1,512]{1,0:T(1,128)} %bitcast.23, s32[512,1]{1,0:T(8,128)} %copy.5.stair_ref, f32[512,2048]{1,0:T(8,128)} %rows_ref.3), custom_call_target="tpu_custom_call" | custom-call | flops 1 | bytes 1 | tf_op jit(solution)/shard_map/pallas_call | solution.py:126
  18.8 8.6 %all-to-all-start = ((f32[32,64,1024]{2,1,0:T(8,128)}), f32[32,64,1024]{2,1,0:T(8,128)}, u32[]{:S(2)}, u32[]{:S(2)}) async-start(f32[32,64,1024]{2,1,0:T(8,128)} %bitcast.14), calls=%async_computation | async-start | bytes 16777216 | tf_op jit(solution)/shard_map/all_to_all | solution.py:459
  28.4 1.7 collective-permute-start.1
  30.1 6.6 %shard_map.47 = f32[16,1,64,1024]{3,2,1,0:T(8,128)} custom-call(s32[1,1]{1,0:T(1,128)} %bitcast.6.first_ref, s32[1,512]{1,0:T(1,128)} %bitcast.24, s32[512,1]{1,0:T(8,128)} %copy.5.stair_ref, f32[512,2048]{1,0:T(8,128)} %rows_ref.3), custom_call_target="tpu_custom_call" | custom-call | flops 1 | bytes 1 | tf_op jit(solution)/shard_map/pallas_call | solution.py:126
  36.8 116.1 %collective-permute-done.1 = f32[288,1024]{1,0:T(8,128)} collective-permute-done((f32[288,1024]{1,0:T(8,128)}, f32[288,1024]{1,0:T(8,128)}, u32[]{:S(2)}, u32[]{:S(2)}) %collective-permute-start.1) | collective-permute-done | bytes 1179680 | tf_op jit(solution)/shard_map/ppermute | solution.py:452
  152.9 1.3 constant_dynamic-update-slice_fusion
  154.3 1.2 copy-done.1
  155.5 1.4 slice_select_fusion.own_ref
  156.9 10.9 %shard_map.48 = (f32[128,1280]{1,0:T(8,128)}, f32[128,1280]{1,0:T(8,128)}, f32[128,1280]{1,0:T(8,128)}, f32[64,1280]{1,0:T(8,128)}, f32[64,1280]{1,0:T(8,128)}, /*index=5*/bf16[1024,2816]{1,0:T(8,128)(2,1)}) custom-call(s32[1,1]{1,0:T(1,128)} %bitcast.1.turn_ref, f32[384,1024]{1,0:T(8,128)} %slice_select_fusion.own_ref, f32[16,2,64,1024]{3,2,1,0:T(8,128)} %bitcast.8.child_ref), custom_call_target="tpu_custom_call" | custom-call | flops 1 | bytes 1 | tf_op jit(solution)/shard_map/pallas_call | solution.py:191
  167.8 1.5 collective-permute-start.2
  169.3 1.7 collective-permute-start.3
  171.1 11.7 %all-to-all-start.1 = ((f32[16,64,1024]{2,1,0:T(8,128)}), f32[16,64,1024]{2,1,0:T(8,128)}, u32[]{:S(2)}, u32[]{:S(2)}) async-start(f32[16,64,1024]{2,1,0:T(8,128)} %bitcast.15), calls=%async_computation.1 | async-start | bytes 8388608 | tf_op jit(solution)/shard_map/all_to_all | solution.py:473
  183.0 2.2 slice_select_fusion.1.own_ref
  185.9 9.0 %shard_map.50 = f32[4,1024,128]{2,1,0:T(8,128)} custom-call(s32[1]{0:T(128)} %bitcast.11._, bf16[1024,2816]{1,0:T(8,128)(2,1)} %get-tuple-element.47.turned_ref, f32[384,512]{1,0:T(8,128)} %slice_select_fusion.1.own_ref, f32[16,2,64,1024]{3,2,1,0:T(8,128)} %bitcast.8.child_ref), custom_call_target="tpu_custom_call" | custom-call | flops 1 | bytes 1 | tf_op jit(solution)/shard_map/pallas_call | solution.py:243
  196.9 3.0 collective-permute-start.5
  201.0 5.3 %collective-permute-done.5 = f32[64,1280]{1,0:T(8,128)S(1)} collective-permute-done((f32[64,1280]{1,0:T(8,128)S(1)}, f32[64,1280]{1,0:T(8,128)S(1)}, u32[]{:S(2)}, u32[]{:S(2)}) %collective-permute-start.5) | collective-permute-done | bytes 327712 | tf_op jit(solution)/shard_map/ppermute | solution.py:437
  206.3 3.9 %collective-permute-done.4 = f32[64,1280]{1,0:T(8,128)S(1)} collective-permute-done((f32[64,1280]{1,0:T(8,128)S(1)}, f32[64,1280]{1,0:T(8,128)S(1)}, u32[]{:S(2)}, u32[]{:S(2)}) %collective-permute-start.4) | collective-permute-done | bytes 327712 | tf_op jit(solution)/shard_map/ppermute | solution.py:437
  211.5 27.6 %all-to-all-done.1 = f32[16,64,1024]{2,1,0:T(8,128)} async-done(((f32[16,64,1024]{2,1,0:T(8,128)}), f32[16,64,1024]{2,1,0:T(8,128)}, u32[]{:S(2)}, u32[]{:S(2)}) %all-to-all-start.1) | async-done | bytes 4194336 | tf_op jit(solution)/shard_map/all_to_all | solution.py:473
  239.1 1.6 collective-permute-start.7
  241.2 14.0 %shard_map.49 = f32[4,1024,256]{2,1,0:T(8,128)} custom-call(bf16[1024,2816]{1,0:T(8,128)(2,1)} %get-tuple-element.47.turned_ref, f32[384,2048]{1,0:T(8,128)} %bitcast.17, f32[16,1,64,1024]{3,2,1,0:T(8,128)} %bitcast.10.child_ref), custom_call_target="tpu_custom_call" | custom-call | flops 1 | bytes 1 | tf_op jit(solution)/shard_map/pallas_call | solution.py:217
  255.7 2.5 collective-permute-done.6.before_ref
  259.6 1.6 collective-permute-start.8
  261.2 6.3 %collective-permute-done.9.across_rest_ref = f32[64,1280]{1,0:T(8,128)S(1)} collective-permute-done((f32[64,1280]{1,0:T(8,128)S(1)}, f32[64,1280]{1,0:T(8,128)S(1)}, u32[]{:S(2)}, u32[]{:S(2)}) %collective-permute-start.9) | collective-permute-done | bytes 327712 | tf_op jit(solution)/shard_map/ppermute | solution.py:437
  267.5 1.8 collective-permute-done.8.across_ref
  270.1 51.6 %shard_map.51 = (bf16[1024,1024]{1,0:T(8,128)(2,1)}, bf16[1024,1024]{1,0:T(8,128)(2,1)}, f32[256,1024]{1,0:T(8,128)}, f32[4,2,256,128]{3,2,1,0:T(8,128)}) custom-call(s32[1,1]{1,0:T(1,128)} %bitcast.1.turn_ref, f32[128,1280]{1,0:T(8,128)} %copy-done.3, f32[128,1280]{1,0:T(8,128)} %copy-done.5, f32[128,1280]{1,0:T(8,128)} %copy-done.4, ...), custom_call_target="tpu_custom_call" | custom-call | flops 1 | bytes 1 | tf_op jit(solution)/shard_map/pallas_call | solution.py:366
  321.7 4.8 %all-to-all-start.2 = ((f32[8,256,128]{2,1,0:T(8,128)}), f32[8,256,128]{2,1,0:T(8,128)S(1)}, u32[]{:S(2)}, u32[]{:S(2)}) async-start(f32[8,256,128]{2,1,0:T(8,128)} %bitcast.22), calls=%async_computation.3 | async-start | bytes 2097152 | tf_op jit(solution)/shard_map/all_to_all | solution.py:499
  326.5 4.7 %shard_map.52 = f32[4,256,256]{2,1,0:T(8,128)} custom-call(bf16[1024,1024]{1,0:T(8,128)(2,1)} %get-tuple-element.50.high_ref, bf16[1024,1024]{1,0:T(8,128)(2,1)} %get-tuple-element.51.low_ref, f32[1,1024,256]{2,1,0:T(8,128)} %reduce-scatter.5.cloned.1.call-done.sums_ref), custom_call_target="tpu_custom_call" | custom-call | flops 1 | bytes 1 | tf_op jit(solution)/shard_map/pallas_call | solution.py:401
  331.1 7.8 %all-to-all-done.2 = f32[8,256,128]{2,1,0:T(8,128)S(1)} async-done(((f32[8,256,128]{2,1,0:T(8,128)}), f32[8,256,128]{2,1,0:T(8,128)S(1)}, u32[]{:S(2)}, u32[]{:S(2)}) %all-to-all-start.2) | async-done | bytes 1048608 | tf_op jit(solution)/shard_map/all_to_all | solution.py:499
  338.9 15.8 %all_to_all.28.second_ref = f32[4,256,256]{2,1,0:T(8,128)} all-to-all(f32[4,256,256]{2,1,0:T(8,128)} %shard_map.52), channel_id=1, replica_groups=mesh['front'=16,'row'=4,'col'=2] {'row'}, dimensions={0} | all-to-all | bytes 2097152 | tf_op jit(solution)/shard_map/all_to_all | solution.py:503
  354.7 3.4 shard_map.53
  (44 shorter events, 10.7 us)
Async XLA Ops:
  7.6 11.2 %collective-permute-start = (f32[96,1024]{1,0:T(8,128)S(1)}, f32[96,1024]{1,0:T(8,128)S(1)}, u32[]{:S(2)}, u32[]{:S(2)}) collective-permute-start(f32[96,1024]{1,0:T(8,128)S(1)} %slice.48), channel_id=1, source_target_pairs={{0,1},{1,0},{2,3},{3,2},{4,5},{5,4},{6,7},{7,6},{8,9},{9,8},{10,11... | collective-permute-start | bytes 1179656 | tf_op jit(solution)/shard_map/ppermute | solution.py:451
  18.8 8.6 %copy-start = (f32[1,384,2048]{2,1,0:T(8,128)S(1)}, f32[1,384,2048]{2,1,0:T(8,128)}, u32[]{:S(2)}) copy-start(f32[1,384,2048]{2,1,0:T(8,128)} %param.4) | copy-start | bytes 9437188
  18.8 138.1 %all-to-all-start = ((f32[32,64,1024]{2,1,0:T(8,128)}), f32[32,64,1024]{2,1,0:T(8,128)}, u32[]{:S(2)}, u32[]{:S(2)}) async-start(f32[32,64,1024]{2,1,0:T(8,128)} %bitcast.14), calls=%async_computation | async-start | bytes 16777216 | tf_op jit(solution)/shard_map/all_to_all | solution.py:459
  28.4 124.5 %collective-permute-start.1 = (f32[288,1024]{1,0:T(8,128)}, f32[288,1024]{1,0:T(8,128)}, u32[]{:S(2)}, u32[]{:S(2)}) collective-permute-start(f32[288,1024]{1,0:T(8,128)} %slice.49), channel_id=1, source_target_pairs={{0,1},{1,0},{2,3},{3,2},{4,5},{5,4},{6,7},{7,6},{8,9},{9,8},{10,11... | collective-permute-start | bytes 3538952 | tf_op jit(solution)/shard_map/ppermute | solution.py:452
  154.3 1.2 copy-start.1
  167.8 18.0 %collective-permute-start.2 = (f32[128,1280]{1,0:T(8,128)}, f32[128,1280]{1,0:T(8,128)}, u32[]{:S(2)}, u32[]{:S(2)}) collective-permute-start(f32[128,1280]{1,0:T(8,128)} %get-tuple-element.34), channel_id=1, source_target_pairs={{0,2},{2,4},{4,6},{6,0},{1,3},{3,5},{5,7},{7,1},{8,10},{10,12},{12... | collective-permute-start | bytes 1966088 | tf_op jit(solution)/shard_map/ppermute | solution.py:437
  169.3 16.5 %collective-permute-start.3 = (f32[128,1280]{1,0:T(8,128)}, f32[128,1280]{1,0:T(8,128)}, u32[]{:S(2)}, u32[]{:S(2)}) collective-permute-start(f32[128,1280]{1,0:T(8,128)} %get-tuple-element.35), channel_id=1, source_target_pairs={{0,6},{2,0},{4,2},{6,4},{1,7},{3,1},{5,3},{7,5},{8,14},{10,8},{12,... | collective-permute-start | bytes 1966088 | tf_op jit(solution)/shard_map/ppermute | solution.py:437
  171.1 68.1 %all-to-all-start.1 = ((f32[16,64,1024]{2,1,0:T(8,128)}), f32[16,64,1024]{2,1,0:T(8,128)}, u32[]{:S(2)}, u32[]{:S(2)}) async-start(f32[16,64,1024]{2,1,0:T(8,128)} %bitcast.15), calls=%async_computation.1 | async-start | bytes 8388608 | tf_op jit(solution)/shard_map/all_to_all | solution.py:473
  182.8 86.6 %reduce-scatter.3.cloned.1.call-start = ((), (), s32[]{:S(2)}) async-start(), calls=%async_computation.6 | async-start | bytes 2621440 | tf_op jit(solution)/shard_map/reduce_scatter | solution.py:496
  194.9 1.0 copy-start.8
  194.9 5.0 %copy-start.7 = (f32[64,1280]{1,0:T(8,128)S(1)}, f32[64,1280]{1,0:T(8,128)}, u32[]{:S(2)}) copy-start(f32[64,1280]{1,0:T(8,128)} %get-tuple-element.33) | copy-start | bytes 983044
  194.9 16.5 %copy-start.6 = (f32[128,1280]{1,0:T(8,128)S(1)}, f32[128,1280]{1,0:T(8,128)}, u32[]{:S(2)}) copy-start(f32[128,1280]{1,0:T(8,128)} %get-tuple-element.32) | copy-start | bytes 1966084
  194.9 131.5 %reduce-scatter.5.cloned.1.call-start = ((), (), s32[]{:S(2)}) async-start(), calls=%async_computation.7 | async-start | bytes 5242880 | tf_op jit(solution)/shard_map/reduce_scatter | solution.py:496
  196.9 9.4 %collective-permute-start.5 = (f32[64,1280]{1,0:T(8,128)S(1)}, f32[64,1280]{1,0:T(8,128)S(1)}, u32[]{:S(2)}, u32[]{:S(2)}) collective-permute-start(f32[64,1280]{1,0:T(8,128)S(1)} %slice_add_fusion.2), channel_id=1, source_target_pairs={{0,6},{2,0},{4,2},{6,4},{1,7},{3,1},{5,3},{7,5},{8,14},{10,8},{12,... | collective-permute-start | bytes 983048 | tf_op jit(solution)/shard_map/ppermute | solution.py:437
  200.9 9.3 %collective-permute-start.4 = (f32[64,1280]{1,0:T(8,128)S(1)}, f32[64,1280]{1,0:T(8,128)S(1)}, u32[]{:S(2)}, u32[]{:S(2)}) collective-permute-start(f32[64,1280]{1,0:T(8,128)S(1)} %slice_add_fusion.3), channel_id=1, source_target_pairs={{0,2},{2,4},{4,6},{6,0},{1,3},{3,5},{5,7},{7,1},{8,10},{10,12},{12... | collective-permute-start | bytes 983048 | tf_op jit(solution)/shard_map/ppermute | solution.py:437
  211.5 43.6 %copy-start.3 = (f32[128,1280]{1,0:T(8,128)}, f32[128,1280]{1,0:T(8,128)S(1)}, u32[]{:S(2)}) copy-start(f32[128,1280]{1,0:T(8,128)S(1)} %maximum_add_fusion.piece_ref) | copy-start | bytes 1966084
  239.1 16.6 %collective-permute-start.7 = (f32[128,1280]{1,0:T(8,128)S(1)}, f32[128,1280]{1,0:T(8,128)S(1)}, u32[]{:S(2)}, u32[]{:S(2)}) collective-permute-start(f32[128,1280]{1,0:T(8,128)S(1)} %maximum_add_fusion.piece_ref), channel_id=1, source_target_pairs={{0,6},{2,0},{4,2},{6,4},{1,7},{3,1},{5,3},{7,5},{8,14},{10,8},{12,... | collective-permute-start | bytes 1966088 | tf_op jit(solution)/shard_map/ppermute | solution.py:437
  240.7 17.5 %collective-permute-start.6 = (f32[128,1280]{1,0:T(8,128)S(1)}, f32[128,1280]{1,0:T(8,128)S(1)}, u32[]{:S(2)}, u32[]{:S(2)}) collective-permute-start(f32[128,1280]{1,0:T(8,128)S(1)} %maximum_add_fusion.piece_ref), channel_id=1, source_target_pairs={{0,2},{2,4},{4,6},{6,0},{1,3},{3,5},{5,7},{7,1},{8,10},{10,12},{12... | collective-permute-start | bytes 1966088 | tf_op jit(solution)/shard_map/ppermute | solution.py:437
  255.7 3.4 copy-start.4
  258.2 0.8 copy-start.5
  259.1 8.4 %collective-permute-start.9 = (f32[64,1280]{1,0:T(8,128)S(1)}, f32[64,1280]{1,0:T(8,128)S(1)}, u32[]{:S(2)}, u32[]{:S(2)}) collective-permute-start(f32[64,1280]{1,0:T(8,128)S(1)} %slice.44), channel_id=1, source_target_pairs={{0,6},{2,0},{4,2},{6,4},{1,7},{3,1},{5,3},{7,5},{8,14},{10,8},{12,... | collective-permute-start | bytes 983048 | tf_op jit(solution)/shard_map/ppermute | solution.py:437
  259.6 9.7 %collective-permute-start.8 = (f32[64,1280]{1,0:T(8,128)S(1)}, f32[64,1280]{1,0:T(8,128)S(1)}, u32[]{:S(2)}, u32[]{:S(2)}) collective-permute-start(f32[64,1280]{1,0:T(8,128)S(1)} %slice.43), channel_id=1, source_target_pairs={{0,2},{2,4},{4,6},{6,0},{1,3},{3,5},{5,7},{7,1},{8,10},{10,12},{12... | collective-permute-start | bytes 983048 | tf_op jit(solution)/shard_map/ppermute | solution.py:437
  267.5 1.9 copy-start.9
  269.4 0.7 copy-start.10
  321.7 17.3 %all-to-all-start.2 = ((f32[8,256,128]{2,1,0:T(8,128)}), f32[8,256,128]{2,1,0:T(8,128)S(1)}, u32[]{:S(2)}, u32[]{:S(2)}) async-start(f32[8,256,128]{2,1,0:T(8,128)} %bitcast.22), calls=%async_computation.3 | async-start | bytes 2097152 | tf_op jit(solution)/shard_map/all_to_all | solution.py:499
  338.9 15.8 %copy-start.2 = (f32[8,256,128]{2,1,0:T(8,128)}, f32[8,256,128]{2,1,0:T(8,128)S(1)}, u32[]{:S(2)}) copy-start(f32[8,256,128]{2,1,0:T(8,128)S(1)} %all-to-all-done.2) | copy-start | bytes 3145732
Sparse Core Ops, SparseCore 0:
  195.0 36.3 reduce-scatter.2
  258.3 45.9 reduce-scatter.4

commit v10 on v9

--- a/solution.py
+++ b/solution.py
@@ -495,6 +495,7 @@
     def summed(products):
         return lax.psum_scatter(products, "row", scatter_dimension=0, tiled=True)
 
+    pieces, products_b = lax.optimization_barrier((pieces, products_b))
     inverse_high, inverse_low, leading, first = factor(turn, *pieces, summed(products_a))
     first = lax.all_to_all(
         first.reshape(2 * row_count, quarter, BLK), ("row", "col"), split_axis=0, concat_axis=0, tiled=True

time: 367 us -> 365 us (level)
    all_to_all x1, waiting for transfers between devices: 27.6 us -> 0.01 us  [body(): lax.all_to_all(single.reshape(n_front * capacity, ELIMINATED), 'front', s...]
    ppermute x8, waiting for transfers between devices: 21.1 us -> 45 us  [shifted(): lax.ppermute(x, 'row', [(i, (i + shift) % count) for i in range(count)])]
  transfers between devices with their start and end apart: 15 -> 15, of which waited for: 11 -> 10; matrix products, arithmetic and copies ran while one was open for 3% -> 3% of each run, Pallas kernels for 26% -> 29%
where the time goes in v10:
time: 365 us; the launch traced here: 364 us
  waiting for transfers between devices  171 us (47%)
  Pallas kernels  108 us (30%)
  starting transfers between devices  38.2 us (10%)
  blocking collectives  18.1 us (5%)
  between operations  13.6 us (4%)
  local copies, waits for them, and re-layouts  7.9 us (2%)
  other arithmetic  6.79 us (2%)
    ppermute x1, waiting for transfers between devices, body(): passed_rest = lax.ppermute(own_a[split:], 'col', [(0, 1), (1, 0)])  116 us
    pallas_call x1, Pallas kernels, factor(): pl.pallas_call(factor_kernel, out_shape=(jax.ShapeDtypeStruct((ELIMINATED...  51.5 us
    ppermute x8, waiting for transfers between devices, shifted(): lax.ppermute(x, 'row', [(i, (i + shift) % count) for i in range(count)])  45 us
    all_to_all x1, blocking collectives, body(): lax.all_to_all(second, 'row', split_axis=0, concat_axis=0, tiled=True)  18.1 us
    pallas_call x1, Pallas kernels, cross(): pl.pallas_call(cross_kernel, grid=(ELIMINATED // WIDE,), out_shape=jax.Sh...  14.1 us
    pallas_call x2, Pallas kernels, place(): pl.pallas_call(place_kernel, grid=(ELIMINATED // WIDE,), out_shape=jax.Sh...  14.1 us
    all_to_all x1, starting transfers between devices, body(): lax.all_to_all(single.reshape(n_front * capacity, ELIMINATED), 'front', s...  11.7 us
    pallas_call x1, Pallas kernels, packed_gram(): pl.pallas_call(gram_kernel, grid=(1,), out_shape=[jax.ShapeDtypeStruct((B...  11.1 us
  transfers between devices with their start and end apart: 15, of which 10 were waited for; matrix products, arithmetic and copies ran while one was open for 3% of the time, Pallas kernels for 29%

profile of v10, /device:TPU:0, one launch (start us, length us, event | category | flops | bytes accessed | tf_op | source)
XLA Modules:
  0.0 363.8 jit_solution(11669133134818842316)
XLA Ops:
  7.6 2.1 collective-permute-start
  9.6 1.5 copy.5.stair_ref
  11.2 7.4 %shard_map.46 = f32[16,2,64,1024]{3,2,1,0:T(8,128)} custom-call(s32[1,1]{1,0:T(1,128)} %bitcast.3.first_ref, s32[1,512]{1,0:T(1,128)} %bitcast.23, s32[512,1]{1,0:T(8,128)} %copy.5.stair_ref, f32[512,2048]{1,0:T(8,128)} %rows_ref.3), custom_call_target="tpu_custom_call" | custom-call | flops 1 | bytes 1 | tf_op jit(solution)/shard_map/pallas_call | solution.py:126
  18.8 8.6 %all-to-all-start = ((f32[32,64,1024]{2,1,0:T(8,128)}), f32[32,64,1024]{2,1,0:T(8,128)}, u32[]{:S(2)}, u32[]{:S(2)}) async-start(f32[32,64,1024]{2,1,0:T(8,128)} %bitcast.14), calls=%async_computation | async-start | bytes 16777216 | tf_op jit(solution)/shard_map/all_to_all | solution.py:459
  28.4 1.7 collective-permute-start.1
  30.1 6.6 %shard_map.47 = f32[16,1,64,1024]{3,2,1,0:T(8,128)} custom-call(s32[1,1]{1,0:T(1,128)} %bitcast.6.first_ref, s32[1,512]{1,0:T(1,128)} %bitcast.24, s32[512,1]{1,0:T(8,128)} %copy.5.stair_ref, f32[512,2048]{1,0:T(8,128)} %rows_ref.3), custom_call_target="tpu_custom_call" | custom-call | flops 1 | bytes 1 | tf_op jit(solution)/shard_map/pallas_call | solution.py:126
  36.8 116.1 %collective-permute-done.1 = f32[288,1024]{1,0:T(8,128)} collective-permute-done((f32[288,1024]{1,0:T(8,128)}, f32[288,1024]{1,0:T(8,128)}, u32[]{:S(2)}, u32[]{:S(2)}) %collective-permute-start.1) | collective-permute-done | bytes 1179680 | tf_op jit(solution)/shard_map/ppermute | solution.py:452
  152.9 1.3 constant_dynamic-update-slice_fusion
  155.5 1.4 slice_select_fusion.own_ref
  156.9 11.7 %all-to-all-start.1 = ((f32[16,64,1024]{2,1,0:T(8,128)}), f32[16,64,1024]{2,1,0:T(8,128)}, u32[]{:S(2)}, u32[]{:S(2)}) async-start(f32[16,64,1024]{2,1,0:T(8,128)} %bitcast.15), calls=%async_computation.1 | async-start | bytes 8388608 | tf_op jit(solution)/shard_map/all_to_all | solution.py:473
  168.6 11.1 %shard_map.48 = (f32[128,1280]{1,0:T(8,128)}, f32[128,1280]{1,0:T(8,128)}, f32[128,1280]{1,0:T(8,128)}, f32[64,1280]{1,0:T(8,128)}, f32[64,1280]{1,0:T(8,128)}, /*index=5*/bf16[1024,2816]{1,0:T(8,128)(2,1)}) custom-call(s32[1,1]{1,0:T(1,128)} %bitcast.1.turn_ref, f32[384,1024]{1,0:T(8,128)} %slice_select_fusion.own_ref, f32[16,2,64,1024]{3,2,1,0:T(8,128)} %bitcast.8.child_ref), custom_call_target="tpu_custom_call" | custom-call | flops 1 | bytes 1 | tf_op jit(solution)/shard_map/pallas_call | solution.py:191
  179.7 1.5 collective-permute-start.2
  181.2 1.8 collective-permute-start.3
  183.0 2.1 slice_select_fusion.1.own_ref
  185.1 13.1 %collective-permute-done.2 = f32[128,1280]{1,0:T(8,128)} collective-permute-done((f32[128,1280]{1,0:T(8,128)}, f32[128,1280]{1,0:T(8,128)}, u32[]{:S(2)}, u32[]{:S(2)}) %collective-permute-start.2) | collective-permute-done | bytes 655392 | tf_op jit(solution)/shard_map/ppermute | solution.py:437
  198.3 9.0 %shard_map.50 = f32[4,1024,128]{2,1,0:T(8,128)} custom-call(s32[1]{0:T(128)} %bitcast.11._, bf16[1024,2816]{1,0:T(8,128)(2,1)} %get-tuple-element.59.turned_ref, f32[384,512]{1,0:T(8,128)} %slice_select_fusion.1.own_ref, f32[16,2,64,1024]{3,2,1,0:T(8,128)} %bitcast.8.child_ref), custom_call_target="tpu_custom_call" | custom-call | flops 1 | bytes 1 | tf_op jit(solution)/shard_map/pallas_call | solution.py:243
  209.3 3.0 collective-permute-start.5
  213.4 6.3 %collective-permute-done.5 = f32[64,1280]{1,0:T(8,128)S(1)} collective-permute-done((f32[64,1280]{1,0:T(8,128)S(1)}, f32[64,1280]{1,0:T(8,128)S(1)}, u32[]{:S(2)}, u32[]{:S(2)}) %collective-permute-start.5) | collective-permute-done | bytes 327712 | tf_op jit(solution)/shard_map/ppermute | solution.py:437
  219.7 6.8 %collective-permute-done.4 = f32[64,1280]{1,0:T(8,128)S(1)} collective-permute-done((f32[64,1280]{1,0:T(8,128)S(1)}, f32[64,1280]{1,0:T(8,128)S(1)}, u32[]{:S(2)}, u32[]{:S(2)}) %collective-permute-start.4) | collective-permute-done | bytes 327712 | tf_op jit(solution)/shard_map/ppermute | solution.py:437
  227.8 2.0 collective-permute-start.6
  229.9 14.1 %shard_map.49 = f32[4,1024,256]{2,1,0:T(8,128)} custom-call(bf16[1024,2816]{1,0:T(8,128)(2,1)} %get-tuple-element.59.turned_ref, f32[384,2048]{1,0:T(8,128)} %bitcast.17, f32[16,1,64,1024]{3,2,1,0:T(8,128)} %bitcast.10.child_ref), custom_call_target="tpu_custom_call" | custom-call | flops 1 | bytes 1 | tf_op jit(solution)/shard_map/pallas_call | solution.py:217
  244.0 7.1 %collective-permute-done.7.after_ref = f32[128,1280]{1,0:T(8,128)S(1)} collective-permute-done((f32[128,1280]{1,0:T(8,128)S(1)}, f32[128,1280]{1,0:T(8,128)S(1)}, u32[]{:S(2)}, u32[]{:S(2)}) %collective-permute-start.7) | collective-permute-done | bytes 655392 | tf_op jit(solution)/shard_map/ppermute | solution.py:437
  251.1 3.0 collective-permute-done.6.before_ref
  254.2 2.0 collective-permute-start.8
  256.2 7.2 %collective-permute-done.9.across_rest_ref = f32[64,1280]{1,0:T(8,128)S(1)} collective-permute-done((f32[64,1280]{1,0:T(8,128)S(1)}, f32[64,1280]{1,0:T(8,128)S(1)}, u32[]{:S(2)}, u32[]{:S(2)}) %collective-permute-start.9) | collective-permute-done | bytes 327712 | tf_op jit(solution)/shard_map/ppermute | solution.py:437
  263.4 1.5 collective-permute-done.8.across_ref
  265.7 51.5 %shard_map.51 = (bf16[1024,1024]{1,0:T(8,128)(2,1)}, bf16[1024,1024]{1,0:T(8,128)(2,1)}, f32[256,1024]{1,0:T(8,128)}, f32[4,2,256,128]{3,2,1,0:T(8,128)}) custom-call(s32[1,1]{1,0:T(1,128)} %bitcast.1.turn_ref, f32[128,1280]{1,0:T(8,128)} %copy-done.3, f32[128,1280]{1,0:T(8,128)} %copy-done.5, f32[128,1280]{1,0:T(8,128)} %copy-done.4, ...), custom_call_target="tpu_custom_call" | custom-call | flops 1 | bytes 1 | tf_op jit(solution)/shard_map/pallas_call | solution.py:366
  317.2 3.6 all-to-all-start.2
  320.8 4.7 %shard_map.52 = f32[4,256,256]{2,1,0:T(8,128)} custom-call(bf16[1024,1024]{1,0:T(8,128)(2,1)} %get-tuple-element.62.high_ref, bf16[1024,1024]{1,0:T(8,128)(2,1)} %get-tuple-element.63.low_ref, f32[1,1024,256]{2,1,0:T(8,128)} %reduce-scatter.5.cloned.1.call-done.sums_ref), custom_call_target="tpu_custom_call" | custom-call | flops 1 | bytes 1 | tf_op jit(solution)/shard_map/pallas_call | solution.py:401
  325.5 9.9 %all-to-all-done.2 = f32[8,256,128]{2,1,0:T(8,128)S(1)} async-done(((f32[8,256,128]{2,1,0:T(8,128)}), f32[8,256,128]{2,1,0:T(8,128)S(1)}, u32[]{:S(2)}, u32[]{:S(2)}) %all-to-all-start.2) | async-done | bytes 1048608 | tf_op jit(solution)/shard_map/all_to_all | solution.py:500
  335.4 18.1 %all_to_all.28.second_ref = f32[4,256,256]{2,1,0:T(8,128)} all-to-all(f32[4,256,256]{2,1,0:T(8,128)} %shard_map.52), channel_id=1, replica_groups=mesh['front'=16,'row'=4,'col'=2] {'row'}, dimensions={0} | all-to-all | bytes 2097152 | tf_op jit(solution)/shard_map/all_to_all | solution.py:504
  353.5 3.4 shard_map.53
  (44 shorter events, 8.8 us)
Async XLA Ops:
  7.6 11.2 %collective-permute-start = (f32[96,1024]{1,0:T(8,128)S(1)}, f32[96,1024]{1,0:T(8,128)S(1)}, u32[]{:S(2)}, u32[]{:S(2)}) collective-permute-start(f32[96,1024]{1,0:T(8,128)S(1)} %slice.48), channel_id=1, source_target_pairs={{0,1},{1,0},{2,3},{3,2},{4,5},{5,4},{6,7},{7,6},{8,9},{9,8},{10,11... | collective-permute-start | bytes 1179656 | tf_op jit(solution)/shard_map/ppermute | solution.py:451
  18.8 8.6 %copy-start = (f32[1,384,2048]{2,1,0:T(8,128)S(1)}, f32[1,384,2048]{2,1,0:T(8,128)}, u32[]{:S(2)}) copy-start(f32[1,384,2048]{2,1,0:T(8,128)} %param.4) | copy-start | bytes 9437188
  18.8 138.1 %all-to-all-start = ((f32[32,64,1024]{2,1,0:T(8,128)}), f32[32,64,1024]{2,1,0:T(8,128)}, u32[]{:S(2)}, u32[]{:S(2)}) async-start(f32[32,64,1024]{2,1,0:T(8,128)} %bitcast.14), calls=%async_computation | async-start | bytes 16777216 | tf_op jit(solution)/shard_map/all_to_all | solution.py:459
  28.4 124.5 %collective-permute-start.1 = (f32[288,1024]{1,0:T(8,128)}, f32[288,1024]{1,0:T(8,128)}, u32[]{:S(2)}, u32[]{:S(2)}) collective-permute-start(f32[288,1024]{1,0:T(8,128)} %slice.49), channel_id=1, source_target_pairs={{0,1},{1,0},{2,3},{3,2},{4,5},{5,4},{6,7},{7,6},{8,9},{9,8},{10,11... | collective-permute-start | bytes 3538952 | tf_op jit(solution)/shard_map/ppermute | solution.py:452
  154.3 1.2 copy-start.1
  156.9 70.9 %all-to-all-start.1 = ((f32[16,64,1024]{2,1,0:T(8,128)}), f32[16,64,1024]{2,1,0:T(8,128)}, u32[]{:S(2)}, u32[]{:S(2)}) async-start(f32[16,64,1024]{2,1,0:T(8,128)} %bitcast.15), calls=%async_computation.1 | async-start | bytes 8388608 | tf_op jit(solution)/shard_map/all_to_all | solution.py:473
  168.6 97.1 %reduce-scatter.3.cloned.1.call-start = ((), (), s32[]{:S(2)}) async-start(), calls=%async_computation.6 | async-start | bytes 2621440 | tf_op jit(solution)/shard_map/reduce_scatter | solution.py:496
  179.7 18.5 %collective-permute-start.2 = (f32[128,1280]{1,0:T(8,128)}, f32[128,1280]{1,0:T(8,128)}, u32[]{:S(2)}, u32[]{:S(2)}) collective-permute-start(f32[128,1280]{1,0:T(8,128)} %get-tuple-element.40), channel_id=1, source_target_pairs={{0,2},{2,4},{4,6},{6,0},{1,3},{3,5},{5,7},{7,1},{8,10},{10,12},{12... | collective-permute-start | bytes 1966088 | tf_op jit(solution)/shard_map/ppermute | solution.py:437
  181.2 17.0 %collective-permute-start.3 = (f32[128,1280]{1,0:T(8,128)}, f32[128,1280]{1,0:T(8,128)}, u32[]{:S(2)}, u32[]{:S(2)}) collective-permute-start(f32[128,1280]{1,0:T(8,128)} %get-tuple-element.41), channel_id=1, source_target_pairs={{0,6},{2,0},{4,2},{6,4},{1,7},{3,1},{5,3},{7,5},{8,14},{10,8},{12,... | collective-permute-start | bytes 1966088 | tf_op jit(solution)/shard_map/ppermute | solution.py:437
  207.3 1.0 copy-start.8
  207.3 5.0 %copy-start.7 = (f32[64,1280]{1,0:T(8,128)S(1)}, f32[64,1280]{1,0:T(8,128)}, u32[]{:S(2)}) copy-start(f32[64,1280]{1,0:T(8,128)} %get-tuple-element.39) | copy-start | bytes 983044
  207.3 20.3 %copy-start.6 = (f32[128,1280]{1,0:T(8,128)S(1)}, f32[128,1280]{1,0:T(8,128)}, u32[]{:S(2)}) copy-start(f32[128,1280]{1,0:T(8,128)} %get-tuple-element.38) | copy-start | bytes 1966084
  207.3 113.5 %reduce-scatter.5.cloned.1.call-start = ((), (), s32[]{:S(2)}) async-start(), calls=%async_computation.7 | async-start | bytes 5242880 | tf_op jit(solution)/shard_map/reduce_scatter | solution.py:496
  209.3 10.4 %collective-permute-start.5 = (f32[64,1280]{1,0:T(8,128)S(1)}, f32[64,1280]{1,0:T(8,128)S(1)}, u32[]{:S(2)}, u32[]{:S(2)}) collective-permute-start(f32[64,1280]{1,0:T(8,128)S(1)} %slice_add_fusion.2), channel_id=1, source_target_pairs={{0,6},{2,0},{4,2},{6,4},{1,7},{3,1},{5,3},{7,5},{8,14},{10,8},{12,... | collective-permute-start | bytes 983048 | tf_op jit(solution)/shard_map/ppermute | solution.py:437
  213.3 13.2 %collective-permute-start.4 = (f32[64,1280]{1,0:T(8,128)S(1)}, f32[64,1280]{1,0:T(8,128)S(1)}, u32[]{:S(2)}, u32[]{:S(2)}) collective-permute-start(f32[64,1280]{1,0:T(8,128)S(1)} %slice_add_fusion.3), channel_id=1, source_target_pairs={{0,2},{2,4},{4,6},{6,0},{1,3},{3,5},{5,7},{7,1},{8,10},{10,12},{12... | collective-permute-start | bytes 983048 | tf_op jit(solution)/shard_map/ppermute | solution.py:437
  227.7 16.3 %copy-start.3 = (f32[128,1280]{1,0:T(8,128)}, f32[128,1280]{1,0:T(8,128)S(1)}, u32[]{:S(2)}) copy-start(f32[128,1280]{1,0:T(8,128)S(1)} %maximum_add_fusion.piece_ref) | copy-start | bytes 1966084
  227.8 23.3 %collective-permute-start.7 = (f32[128,1280]{1,0:T(8,128)S(1)}, f32[128,1280]{1,0:T(8,128)S(1)}, u32[]{:S(2)}, u32[]{:S(2)}) collective-permute-start(f32[128,1280]{1,0:T(8,128)S(1)} %maximum_add_fusion.piece_ref), channel_id=1, source_target_pairs={{0,6},{2,0},{4,2},{6,4},{1,7},{3,1},{5,3},{7,5},{8,14},{10,8},{12,... | collective-permute-start | bytes 1966088 | tf_op jit(solution)/shard_map/ppermute | solution.py:437
  227.8 26.2 %collective-permute-start.6 = (f32[128,1280]{1,0:T(8,128)S(1)}, f32[128,1280]{1,0:T(8,128)S(1)}, u32[]{:S(2)}, u32[]{:S(2)}) collective-permute-start(f32[128,1280]{1,0:T(8,128)S(1)} %maximum_add_fusion.piece_ref), channel_id=1, source_target_pairs={{0,2},{2,4},{4,6},{6,0},{1,3},{3,5},{5,7},{7,1},{8,10},{10,12},{12... | collective-permute-start | bytes 1966088 | tf_op jit(solution)/shard_map/ppermute | solution.py:437
  251.1 13.8 %copy-start.4 = (f32[128,1280]{1,0:T(8,128)}, f32[128,1280]{1,0:T(8,128)S(1)}, u32[]{:S(2)}) copy-start(f32[128,1280]{1,0:T(8,128)S(1)} %collective-permute-done.7.after_ref) | copy-start | bytes 1966084
  254.1 10.9 %copy-start.5 = (f32[128,1280]{1,0:T(8,128)}, f32[128,1280]{1,0:T(8,128)S(1)}, u32[]{:S(2)}) copy-start(f32[128,1280]{1,0:T(8,128)S(1)} %collective-permute-done.6.before_ref) | copy-start | bytes 1966084
  254.1 9.3 %collective-permute-start.9 = (f32[64,1280]{1,0:T(8,128)S(1)}, f32[64,1280]{1,0:T(8,128)S(1)}, u32[]{:S(2)}, u32[]{:S(2)}) collective-permute-start(f32[64,1280]{1,0:T(8,128)S(1)} %slice.44), channel_id=1, source_target_pairs={{0,6},{2,0},{4,2},{6,4},{1,7},{3,1},{5,3},{7,5},{8,14},{10,8},{12,... | collective-permute-start | bytes 983048 | tf_op jit(solution)/shard_map/ppermute | solution.py:437
  254.2 10.7 %collective-permute-start.8 = (f32[64,1280]{1,0:T(8,128)S(1)}, f32[64,1280]{1,0:T(8,128)S(1)}, u32[]{:S(2)}, u32[]{:S(2)}) collective-permute-start(f32[64,1280]{1,0:T(8,128)S(1)} %slice.43), channel_id=1, source_target_pairs={{0,2},{2,4},{4,6},{6,0},{1,3},{3,5},{5,7},{7,1},{8,10},{10,12},{12... | collective-permute-start | bytes 983048 | tf_op jit(solution)/shard_map/ppermute | solution.py:437
  263.4 1.6 copy-start.9
  264.9 0.8 copy-start.10
  317.2 18.2 %all-to-all-start.2 = ((f32[8,256,128]{2,1,0:T(8,128)}), f32[8,256,128]{2,1,0:T(8,128)S(1)}, u32[]{:S(2)}, u32[]{:S(2)}) async-start(f32[8,256,128]{2,1,0:T(8,128)} %bitcast.22), calls=%async_computation.3 | async-start | bytes 2097152 | tf_op jit(solution)/shard_map/all_to_all | solution.py:500
  335.4 18.1 %copy-start.2 = (f32[8,256,128]{2,1,0:T(8,128)}, f32[8,256,128]{2,1,0:T(8,128)S(1)}, u32[]{:S(2)}) copy-start(f32[8,256,128]{2,1,0:T(8,128)S(1)} %all-to-all-done.2) | copy-start | bytes 3145732
Sparse Core Ops, SparseCore 0:
  207.4 41.7 reduce-scatter.2
  265.0 45.7 reduce-scatter.4
